TPU v7x, 32 devices: a whole 2x2x4 slice. The times are simulated.
32 devices in a mesh: groups: 2 (over y), tensor: 4 (over z), dp: 4 (over x, core).
Axes of the slice: x: 2, y: 2, z: 4, core: 2. Of those that a mesh axis runs over, the one named last changes fastest.
Arguments:
- tokens: bfloat16 [512, 8192], P(('groups', 'tensor'), 'dp'), parts along dimension 0, may hold values from -6 to 6
- gate_code: bfloat16 [8192, 26624], P('dp', 'tensor'), may hold values from -8 to 7, as said below
- up_code: bfloat16 [8192, 26624], P('dp', 'tensor'), may hold values from -8 to 7, as said below
- down_code: bfloat16 [26624, 8192], P('tensor', 'dp'), may hold values from -8 to 7, as said below
- gate_scale: bfloat16 [64, 26624], P('dp', 'tensor'), may hold values from 0.0011825562 to 0.004760742
- up_scale: bfloat16 [64, 26624], P('dp', 'tensor'), may hold values from 0.0011825562 to 0.004760742
- down_scale: bfloat16 [208, 8192], P('tensor', 'dp'), may hold values from 0.0006599426 to 0.0026397705
- sign_bits: int32 [26624], P('tensor'), may hold values 0 or 1
Outputs:
- mixed: bfloat16 [512, 8192], P(('groups', 'tensor'), 'dp'), parts along dimension 0
There are 2 independent parts, one for each index of `groups`. A program takes and returns all parts, laid end to end along the dimension named above; an argument that names none is the same for every part. Nothing has to cross between parts.
Inputs may be any that keep to these rules, and one draw needn't show every extreme that they name: `gate_code`: integer codes. `up_code`: integer codes. `down_code`: integer codes.
All inputs are finite; a program needn't handle non-finite values. No bound on the sum of `sign_bits` on one device may be relied on, other than what follows from the above.
Results may differ from a plain program's by a relative error of at most 0.02.
Values may be sent and summed in bfloat16 or wider, within the bound.
No kernel may reach another device: no remote copies, remote signals or barrier semaphores. Data moves between devices by JAX's collectives and lax.ppermute only.
A program may use at most 320 MiB of HBM per device.

v0:
```python
import jax
import jax.numpy as jnp
from jax import lax
from jax.sharding import PartitionSpec as P

POW = 2048
FACTOR = 13


def swapped(shard, axis, distance):
    return lax.ppermute(shard, axis, [(i, i ^ 1 << distance) for i in range(lax.axis_size(axis))])


def sign_table(left, right, levels):
    common = jnp.bitwise_and(left, right)
    parity = jnp.zeros_like(common)
    for bit_index in range(levels):
        parity = parity + jnp.bitwise_and(jnp.right_shift(common, bit_index), 1)
    return (1 - 2 * (parity % 2)).astype(jnp.float32)


def dequant(codes, scales):
    row_count, col_count = codes.shape
    grouped = codes.reshape(scales.shape[0], row_count // scales.shape[0], col_count).astype(
        jnp.float32
    )
    product = grouped * scales.astype(jnp.float32)[:, None, :]
    return product.reshape(row_count, col_count).astype(jnp.bfloat16)


def local_rotation(hidden):
    row_count, units_here = hidden.shape
    order = units_here // FACTOR
    index = jnp.arange(order, dtype=jnp.int32)
    hadamard = sign_table(index[:, None], index[None, :], max(order.bit_length() - 1, 0))
    shaped = hidden.reshape(row_count, order, FACTOR)
    shaped = jnp.einsum("jk,rkc->rjc", hadamard, shaped, precision=lax.Precision.HIGHEST)
    return shaped.reshape(row_count, units_here)


def cross_tensor(hidden):
    peers = lax.axis_size("tensor")
    levels = peers.bit_length() - 1
    own_index = lax.axis_index("tensor")
    for bit_index in range(levels):
        partner = swapped(hidden.astype(jnp.bfloat16), "tensor", bit_index).astype(hidden.dtype)
        upper_half = jnp.bitwise_and(jnp.right_shift(own_index, bit_index), 1) == 1
        hidden = jnp.where(upper_half, partner - hidden, hidden + partner)
    return hidden


def on_device(tokens, gate_code, up_code, down_code, gate_scale, up_scale, down_scale, sign_bits):
    gate_up = jnp.concatenate([dequant(gate_code, gate_scale), dequant(up_code, up_scale)], axis=1)
    down_w = dequant(down_code, down_scale)
    unit_count = gate_code.shape[1]
    terms = jnp.dot(
        lax.all_gather(tokens, "tensor", axis=0, tiled=True),
        gate_up,
        preferred_element_type=jnp.float32,
    )
    terms = terms.reshape(terms.shape[0], 2, unit_count)
    sign_values = 2.0 * sign_bits.astype(jnp.float32) - 1.0
    norm_factor = POW ** (-0.5)
    shares = lax.psum_scatter(
        terms.astype(jnp.bfloat16), "dp", scatter_dimension=0, tiled=True
    ).astype(jnp.float32)
    hidden = jax.nn.silu(shares[:, 0]) * shares[:, 1] * sign_values[None, :]
    hidden = cross_tensor(local_rotation(hidden))
    rotated = (hidden * norm_factor).astype(jnp.bfloat16)
    partial_value = jnp.dot(
        lax.all_gather(rotated, "dp", axis=0, tiled=True),
        down_w,
        preferred_element_type=jnp.float32,
    )
    result = lax.psum_scatter(
        partial_value.astype(jnp.bfloat16), "tensor", scatter_dimension=0, tiled=True
    )
    return result


def solution(mesh):
    in_specs = (
        P(("groups", "tensor"), "dp"),
        P("dp", "tensor"),
        P("dp", "tensor"),
        P("tensor", "dp"),
        P("dp", "tensor"),
        P("dp", "tensor"),
        P("tensor", "dp"),
        P("tensor"),
    )
    out_specs = P(("groups", "tensor"), "dp")
    return jax.shard_map(
        on_device, mesh=mesh, in_specs=in_specs, out_specs=out_specs, check_vma=False
    )
```

profile of v0, /device:TPU:0, one launch (start us, length us, event | category | flops | bytes accessed | tf_op | source)
XLA Modules:
  0.0 416.0 jit_solution(12612640794163268487)
XLA Ops:
  6.5 0.0 all-gather.3.cloned.1.call-start
  6.5 0.7 all-gather.3.cloned.1.call-update
  7.3 0.0 all-reduce.3.cloned.1.call-start
  7.3 1.0 convert_element_type.67
  8.3 1.0 convert_element_type.70
  9.2 37.6 %fusion.5 = (bf16[2048,6656]{1,0:T(8,128)(2,1)}, bf16[2048,6656]{1,0:T(8,128)(2,1)}) fusion(bf16[2048,6656]{1,0:T(8,128)(2,1)} %param.10, f32[16,6656]{1,0:T(8,128)S(1)} %convert_element_type.70, f32[16,6656]{1,0:T(8,128)S(1)} %convert_element_type.67, bf16[2048,6656]{1,0:T(8,128)(2,1)} %param.9), kind=kLoop, calls=%fused_computation.7 | loop fusion | flops 81788928 | bytes 109903872 | tf_op jit(solution)/shard_map/convert_element_type | solution.py:28
  46.9 0.0 all-gather.3.cloned.1.call-done
  46.9 28.8 %fusion.7 = bf16[13312,256]{1,0:T(8,128)(2,1)} fusion(bf16[256,2048]{1,0:T(8,128)(2,1)} %all-gather.3.cloned.1.call-done, bf16[2048,6656]{1,0:T(8,128)(2,1)} %get-tuple-element.7, bf16[2048,6656]{1,0:T(8,128)(2,1)} %get-tuple-element.8), kind=kOutput, calls=%fused_computation.10 | convolution fusion | flops 14071103488 | bytes 62390272 | tf_op jit(solution)/shard_map/dot_general | solution.py:56
  75.6 17.5 %copy.21 = bf16[256,2,6656]{2,1,0:T(2,128)(2,1)} copy(bf16[256,2,6656]{0,2,1:T(8,128)(2,1)} %bitcast.30) | data formatting | bytes 13631488 | tf_op jit(solution)/shard_map/convert_element_type | solution.py:65
  93.2 0.0 copy-start.2
  93.2 0.0 copy-start.3
  93.2 0.0 all-reduce.3.cloned.1.call-update
  93.2 0.0 all-gather.5.cloned.1.call-start
  93.2 0.7 copy-done.2
  93.9 0.9 mul.78
  94.8 0.0 copy-done.3
  94.8 0.7 dynamic-slice
  96.2 128.2 %all-reduce.3.cloned.1.call-done = bf16[256,2,6656]{2,1,0:T(2,128)(2,1)} async-done(((bf16[256,2,6656]{2,1,0:T(2,128)(2,1)}), bf16[256,2,6656]{2,1,0:T(2,128)(2,1)}) %all-reduce.3.cloned.1.call-update) | async-done | bytes 6815760
  224.4 2.6 dynamic-slice_convert_fusion
  227.0 4.4 %fusion.48 = (f32[64,1,6656]{2,1,0:T(1,128)}, f32[64,1,6656]{2,1,0:T(1,128)}) fusion(f32[64,2,6656]{2,1,0:T(2,128)S(1)} %dynamic-slice_convert_fusion), kind=kLoop, calls=%fused_computation.57 | loop fusion | bytes 6815744 | tf_op jit(solution)/shard_map/slice | solution.py:67
  231.4 4.5 %copy.22 = f32[64,1,6656]{0,2,1:T(8,128)S(1)} copy(f32[64,1,6656]{2,1,0:T(1,128)} %get-tuple-element.5) | data formatting | bytes 3407872 | tf_op jit(solution)/shard_map/slice | solution.py:67
  235.9 2.1 squeeze.6
  238.1 4.5 %copy.23 = f32[64,1,6656]{0,2,1:T(8,128)S(1)} copy(f32[64,1,6656]{2,1,0:T(1,128)} %get-tuple-element.6) | data formatting | bytes 3407872 | tf_op jit(solution)/shard_map/slice | solution.py:67
  242.6 2.2 squeeze.7
  244.8 4.9 %multiply_multiply_fusion = f32[64,512,13]{0,2,1:T(8,128)S(1)} fusion(f32[64,512,13]{0,2,1:T(8,128)} %squeeze.7, f32[64,512,13]{0,2,1:T(8,128)} %squeeze.6, f32[512,13]{1,0:T(8,128)} %mul.78), kind=kLoop, calls=%fused_computation.11 | loop fusion | flops 2555904 | bytes 5138432 | tf_op jit(solution)/shard_map/mul | solution.py:67
  249.6 12.0 %fusion.16 = f32[64,512,13]{1,0,2:T(8,128)S(1)} fusion(f32[64,512,13]{0,2,1:T(8,128)S(1)} %multiply_multiply_fusion), kind=kOutput, calls=%fused_computation.27 | convolution fusion | flops 2627993600 | bytes 3407872 | tf_op jit(solution)/shard_map/jk,rkc->rjc/dot_general | solution.py:37
  261.7 4.0 copy.25
  265.6 2.9 reshape.26
  268.6 1.4 convert_element_type.78
  270.0 2.5 copy.26
  272.5 1.5 collective-permute-start
  274.0 2.1 copy.27
  276.1 0.0 copy-start
  276.1 17.1 %collective-permute-done = bf16[64,6656]{1,0:T(8,128)(2,1)} collective-permute-done((bf16[64,6656]{1,0:T(8,128)(2,1)}, bf16[64,6656]{1,0:T(8,128)(2,1)}, u32[]{:S(2)}, u32[]{:S(2)}) %collective-permute-start) | collective-permute-done | bytes 852000 | tf_op jit(solution)/shard_map/ppermute | solution.py:11
  293.2 1.9 fusion.28
  295.2 2.5 collective-permute-start.1
  297.6 36.3 %collective-permute-done.1 = bf16[64,6656]{1,0:T(8,128)(2,1)S(1)} collective-permute-done((bf16[64,6656]{1,0:T(8,128)(2,1)S(1)}, bf16[64,6656]{1,0:T(8,128)(2,1)S(1)}, u32[]{:S(2)}, u32[]{:S(2)}) %collective-permute-start.1) | collective-permute-done | bytes 852000 | tf_op jit(solution)/shard_map/ppermute | solution.py:11
  333.9 0.0 copy-done
  333.9 0.0 copy-start.1
  333.9 2.6 fusion.15
  336.6 0.0 all-gather.5.cloned.1.call-update
  336.6 0.0 reduce-scatter.2.cloned.1.call-start
  336.6 0.0 copy-done.1
  336.7 19.7 %fusion.4 = bf16[6656,2048]{1,0:T(8,128)(2,1)} fusion(bf16[6656,2048]{1,0:T(8,128)(2,1)} %param.11, f32[52,2048]{1,0:T(8,128)S(1)} %convert_element_type.84), kind=kLoop, calls=%fused_computation.5 | loop fusion | flops 40894464 | bytes 54951936 | tf_op jit(solution)/shard_map/convert_element_type | solution.py:28
  356.4 11.5 %all-gather.5.cloned.1.call-done = bf16[256,6656]{1,0:T(8,128)(2,1)} async-done(((bf16[64,6656]{1,0:T(8,128)(2,1)}), bf16[256,6656]{1,0:T(8,128)(2,1)}) %all-gather.5.cloned.1.call-update) | async-done | bytes 3407888 | tf_op jit(solution)/shard_map/all_gather | solution.py:71
  367.9 14.2 %convolution_convert_fusion = bf16[256,2048]{1,0:T(8,128)(2,1)} fusion(bf16[256,6656]{1,0:T(8,128)(2,1)} %all-gather.5.cloned.1.call-done, bf16[6656,2048]{1,0:T(8,128)(2,1)} %fusion.4), kind=kOutput, calls=%fused_computation.14 | convolution fusion | flops 6979846144 | bytes 31719424 | tf_op jit(solution)/shard_map/dot_general | solution.py:70
  382.1 0.0 reduce-scatter.2.cloned.1.call-update
  382.2 27.3 %reduce-scatter.2.cloned.1.call-done = bf16[64,2048]{1,0:T(8,128)(2,1)} async-done(((bf16[256,2048]{1,0:T(8,128)(2,1)}), bf16[64,2048]{1,0:T(8,128)(2,1)}) %reduce-scatter.2.cloned.1.call-update) | async-done | bytes 262160 | tf_op jit(solution)/shard_map/reduce_scatter | solution.py:75
  (2 shorter events, 0.0 us)
Async XLA Ops:
  6.5 40.3 %all-gather.3.cloned.1.call-start = ((), (), s32[]{:S(2)}) async-start(), calls=%async_computation.1 | async-start | bytes 1310720 | tf_op jit(solution)/shard_map/all_gather | solution.py:57
  7.3 217.1 %all-reduce.3.cloned.1.call-start = ((), (), s32[]{:S(2)}) async-start(), calls=%async_computation.4 | async-start | bytes 13631488
  93.2 0.7 copy-start.2
  93.2 1.7 copy-start.3
  93.2 274.7 %all-gather.5.cloned.1.call-start = ((), (), s32[]{:S(2)}) async-start(), calls=%async_computation.2 | async-start | bytes 4259840 | tf_op jit(solution)/shard_map/all_gather | solution.py:71
  272.5 20.8 %collective-permute-start = (bf16[64,6656]{1,0:T(8,128)(2,1)}, bf16[64,6656]{1,0:T(8,128)(2,1)}, u32[]{:S(2)}, u32[]{:S(2)}) collective-permute-start(bf16[64,6656]{1,0:T(8,128)(2,1)} %copy.26), channel_id=1, source_target_pairs={{0,4},{4,0},{8,12},{12,8},{1,5},{5,1},{9,13},{13,9},{2,6},{6,2},{1... | collective-permute-start | bytes 2555912 | tf_op jit(solution)/shard_map/ppermute | solution.py:11
  276.1 57.8 %copy-start = (f32[64,6656]{1,0:T(8,128)S(1)}, f32[64,6656]{1,0:T(8,128)}, u32[]{:S(2)}) copy-start(f32[64,6656]{1,0:T(8,128)} %copy.27) | copy-start | bytes 5111812
  295.2 38.8 %collective-permute-start.1 = (bf16[64,6656]{1,0:T(8,128)(2,1)S(1)}, bf16[64,6656]{1,0:T(8,128)(2,1)S(1)}, u32[]{:S(2)}, u32[]{:S(2)}) collective-permute-start(bf16[64,6656]{1,0:T(8,128)(2,1)S(1)} %fusion.28), channel_id=1, source_target_pairs={{0,8},{4,12},{8,0},{12,4},{1,9},{5,13},{9,1},{13,5},{2,10},{6,14},... | collective-permute-start | bytes 2555912 | tf_op jit(solution)/shard_map/ppermute | solution.py:11
  333.9 2.7 copy-start.1
  336.6 72.9 %reduce-scatter.2.cloned.1.call-start = ((), (), s32[]{:S(2)}) async-start(), calls=%async_computation.3 | async-start | bytes 1310720 | tf_op jit(solution)/shard_map/reduce_scatter | solution.py:75
Sparse Core Ops, SparseCore 0:
  8.9 30.6 all-gather.2
  93.3 131.0 all-reduce.2
  336.7 31.1 all-gather.4
  382.3 27.1 reduce-scatter.1
where the time goes:
time: 417 us; the launch traced here: 416 us
  waiting for transfers between devices  221 us (53%)
  other arithmetic  72.7 us (17%)
  matrix products  55 us (13%)
  local copies, waits for them, and re-layouts  49.1 us (12%)
  between operations  13.9 us (3%)
    unnamed x5, waiting for transfers between devices  129 us
    convert_element_type x2, other arithmetic, dequant(): return product.reshape(row_count, col_count).astype(jnp.bfloat16)  57.3 us
    ppermute x2, waiting for transfers between devices, swapped(): lax.ppermute(shard, axis, [(i, i ^ 1 << distance) for i in range(lax.axis...  53.4 us
    dot_general x1, matrix products, on_device(): jnp.dot(lax.all_gather(tokens, 'tensor', axis=0, tiled=True), gate_up, pr...  28.8 us
    reduce_scatter x1, waiting for transfers between devices, on_device(): lax.psum_scatter(partial_value.astype(jnp.bfloat16), 'tensor', scatter_di...  27.3 us
    convert_element_type x1, local copies, waits for them, and re-layouts, on_device(): terms.astype(jnp.bfloat16)  17.5 us
    dot_general x1, matrix products, on_device(): jnp.dot(lax.all_gather(rotated, 'dp', axis=0, tiled=True), down_w, prefer...  14.2 us
    slice x3, local copies, waits for them, and re-layouts, on_device(): hidden = jax.nn.silu(shares[:, 0]) * shares[:, 1] * sign_values[None, :]  13.5 us
  transfers between devices with their start and end apart: 6, of which 5 were waited for; matrix products, arithmetic and copies ran while one was open for 15% of the time, Pallas kernels for 0%

commit v1 on v0

v1 whole, which is shorter than its diff:
```python
import functools

import jax
import jax.numpy as jnp
import numpy as np
from jax import lax
from jax.experimental import pallas as pl
from jax.experimental.pallas import tpu as pltpu
from jax.sharding import PartitionSpec as P

POW = 2048
FACTOR = 13
LOW = 128
VMEM_LIMIT = 56 * 2**20


def bits_of(size):
    return size.bit_length() - 1


def swap(shard, axis, bit):
    return lax.ppermute(shard, axis, [(i, i ^ 1 << bit) for i in range(lax.axis_size(axis))])


def shift(shard, axis):
    size = lax.axis_size(axis)
    return lax.ppermute(shard, axis, [(i, (i + 1) % size) for i in range(size)])


def reversed_bits(value, bits):
    return sum((value >> i & 1) << (bits - 1 - i) for i in range(bits))


def params(**more):
    return pltpu.CompilerParams(vmem_limit_bytes=VMEM_LIMIT, **more)


def low_rotation():
    order = np.arange(LOW)
    common = order[:, None] & order[None, :]
    parity = np.zeros_like(common)
    for bit in range(bits_of(LOW)):
        parity ^= common >> bit & 1
    return np.kron(1 - 2 * parity, np.eye(FACTOR)).astype(jnp.bfloat16)


def scaled(codes, scales):
    depth, cols = codes.shape
    groups = scales.shape[0]
    product = codes.astype(jnp.float32).reshape(groups, depth // groups, cols) * scales[:, None, :]
    return product.astype(jnp.bfloat16).reshape(depth, cols)


def gate_up_kernel(peers, pieces, *refs):
    token_refs = refs[:peers]
    gate_ref, up_ref, gate_scale_ref, up_scale_ref, keep_ref, send_ref, rows_ref, scale_ref, total_ref = refs[peers:]
    step = pl.program_id(0)
    depth = gate_ref.shape[0]
    part = token_refs[0].shape[0]
    steps = rows_ref.shape[0]
    groups = scale_ref.shape[1] // steps

    @pl.when(step == 0)
    def _():
        place = lax.axis_index("tensor")
        for hop, token_ref in enumerate(token_refs):
            row = pl.multiple_of(lax.rem(place + peers - hop, peers) * part, part)
            for index in range(steps):
                rows_ref[index, pl.ds(row, part), :] = token_ref[:, index * depth : (index + 1) * depth]
        scale_ref[0] = gate_scale_ref[...].astype(jnp.float32)
        scale_ref[1] = up_scale_ref[...].astype(jnp.float32)
        total_ref[...] = jnp.zeros_like(total_ref)

    rows = rows_ref[step]
    first = pl.multiple_of(step * groups, groups)
    for side, code_ref in enumerate((gate_ref, up_ref)):
        weight = scaled(code_ref[...], scale_ref[side, pl.ds(first, groups), :])
        total_ref[side] += jnp.dot(rows, weight, preferred_element_type=jnp.float32)

    @pl.when(step == steps - 1)
    def _():
        own = lax.axis_index("dp")
        share = total_ref.shape[1] // pieces
        for piece in range(pieces):
            block = own ^ reversed_bits(piece, bits_of(pieces))
            row = pl.multiple_of(block * share, share)
            out_ref = keep_ref if piece < pieces // 2 else send_ref
            out_ref[piece % (pieces // 2)] = total_ref[:, pl.ds(row, share), :].astype(jnp.bfloat16)


def gate_up(token_parts, gate_code, up_code, gate_scale, up_scale, chunk, width):
    peers = len(token_parts)
    pieces = lax.axis_size("dp")
    part, features = token_parts[0].shape
    row_count = part * peers
    depth = min(features, 1024)
    steps = features // depth
    groups = gate_scale.shape[0]
    share = row_count // pieces
    code_spec = pl.BlockSpec((depth, width), lambda k: (k, chunk))
    scale_spec = pl.BlockSpec((groups, width), lambda k: (0, chunk))
    out = jax.ShapeDtypeStruct((pieces // 2, 2, share, width), jnp.bfloat16)
    out_spec = pl.BlockSpec(out.shape, lambda k: (0, 0, 0, 0))
    return pl.pallas_call(
        functools.partial(gate_up_kernel, peers, pieces),
        grid=(steps,),
        in_specs=[pl.BlockSpec((part, features), lambda k: (0, 0))] * peers
        + [code_spec, code_spec, scale_spec, scale_spec],
        out_specs=[out_spec, out_spec],
        out_shape=[out, out],
        scratch_shapes=[
            pltpu.VMEM((steps, row_count, depth), jnp.bfloat16),
            pltpu.VMEM((2, groups, width), jnp.float32),
            pltpu.VMEM((2, row_count, width), jnp.float32),
        ],
        compiler_params=params(),
        cost_estimate=pl.CostEstimate(
            flops=4 * row_count * features * width, bytes_accessed=4 * features * width, transcendentals=0
        ),
        name=f"gate_up_{chunk}",
    )(*token_parts, gate_code, up_code, gate_scale, up_scale)


def hidden_kernel(*refs):
    term_refs, (sign_ref, rotation_ref, out_ref) = refs[:-3], refs[-3:]
    total = sum(ref[0].astype(jnp.float32) for ref in term_refs)
    gate, up = total[0], total[1]
    hidden = gate / (1.0 + jnp.exp(-gate)) * up * sign_ref[0]
    out_ref[...] = jnp.dot(
        hidden.astype(jnp.bfloat16), rotation_ref[...], preferred_element_type=jnp.float32
    ).astype(jnp.bfloat16)


def hidden_of(terms, signs, rotation, chunk):
    _, _, share, width = terms[0].shape
    return pl.pallas_call(
        hidden_kernel,
        grid=(1,),
        in_specs=[pl.BlockSpec((1, 2, share, width), lambda k: (0, 0, 0, 0))] * len(terms)
        + [pl.BlockSpec((1, 1, width), lambda k: (chunk, 0, 0)), pl.BlockSpec((width, width), lambda k: (0, 0))],
        out_specs=pl.BlockSpec((share, width), lambda k: (0, 0)),
        out_shape=jax.ShapeDtypeStruct((share, width), jnp.bfloat16),
        compiler_params=params(),
        cost_estimate=pl.CostEstimate(
            flops=2 * share * width * width, bytes_accessed=2 * width * width, transcendentals=share * width
        ),
        name=f"hidden_{chunk}",
    )(*terms, signs, rotation)


def down_kernel(chunks, pieces, peers, *refs):
    part_refs = refs[: chunks * pieces]
    code_ref, scale_in_ref, out_ref, rows_ref, scale_ref, total_ref = refs[chunks * pieces :]
    step = pl.program_id(0)
    share, width = part_refs[0].shape
    row_count = share * pieces
    groups = scale_in_ref.shape[0] // chunks

    @pl.when(step == 0)
    def _():
        own = lax.axis_index("dp")
        place = lax.axis_index("tensor")
        part = row_count // peers
        for piece in range(pieces):
            block = own ^ reversed_bits(piece, bits_of(pieces))
            row = block * share
            turn = lax.rem(place + 2 * peers - 1 - row // part, peers)
            row = pl.multiple_of(turn * part + lax.rem(row, part), share)
            values = [part_refs[chunk * pieces + piece][...].astype(jnp.float32) for chunk in range(chunks)]
            gap = 1
            while gap < chunks:
                for low in range(chunks):
                    if not low & gap:
                        left, right = values[low], values[low | gap]
                        values[low], values[low | gap] = left + right, left - right
                gap *= 2
            for chunk in range(chunks):
                rows_ref[chunk, pl.ds(row, share), :] = (values[chunk] * POW**-0.5).astype(jnp.bfloat16)
        scales = scale_in_ref[...].astype(jnp.float32)
        for chunk in range(chunks):
            scale_ref[chunk, :groups, :] = scales[chunk * groups : (chunk + 1) * groups]
        total_ref[...] = jnp.zeros_like(total_ref)

    weight = scaled(code_ref[...], scale_ref[step, :groups, :])
    total_ref[...] += jnp.dot(rows_ref[step], weight, preferred_element_type=jnp.float32)

    @pl.when(step == chunks - 1)
    def _():
        out_ref[...] = total_ref[...].astype(jnp.bfloat16).reshape(out_ref.shape)


def down(parts, down_code, down_scale, column, columns):
    chunks, pieces = len(parts), len(parts[0])
    peers = lax.axis_size("tensor")
    share, width = parts[0][0].shape
    row_count = share * pieces
    groups = down_scale.shape[0]
    room = -(-groups // chunks // 8) * 8
    out = jax.ShapeDtypeStruct((peers, row_count // peers, columns), jnp.bfloat16)
    return pl.pallas_call(
        functools.partial(down_kernel, chunks, pieces, peers),
        grid=(chunks,),
        in_specs=[pl.BlockSpec((share, width), lambda k: (0, 0))] * (chunks * pieces)
        + [
            pl.BlockSpec((width, columns), lambda k: (k, column)),
            pl.BlockSpec((groups, columns), lambda k: (0, column)),
        ],
        out_specs=pl.BlockSpec(out.shape, lambda k: (0, 0, 0)),
        out_shape=out,
        scratch_shapes=[
            pltpu.VMEM((chunks, row_count, width), jnp.bfloat16),
            pltpu.VMEM((chunks, room, columns), jnp.float32),
            pltpu.VMEM((row_count, columns), jnp.float32),
        ],
        compiler_params=params(),
        cost_estimate=pl.CostEstimate(
            flops=2 * row_count * chunks * width * columns,
            bytes_accessed=2 * chunks * width * columns,
            transcendentals=0,
        ),
        name=f"down_{column}",
    )(*[part for row in parts for part in row], down_code, down_scale)


def add(*terms):
    return sum(term.astype(jnp.float32) for term in terms).astype(jnp.bfloat16)


def halved(keep, send):
    terms = [keep]
    for bit in range(bits_of(lax.axis_size("dp"))):
        if bit:
            half = terms[0].shape[0] // 2
            send = add(*[term[half : 2 * half] for term in terms])
            terms = [term[:half] for term in terms] if half > 1 else terms
        terms = terms + [swap(send, "dp", bit)]
    return terms


def rotated_over(hidden, axis):
    place = lax.axis_index(axis)
    for bit in range(bits_of(lax.axis_size(axis))):
        sign = (1 - 2 * (place >> bit & 1)).astype(jnp.float32)
        partner = swap(hidden, axis, bit)
        hidden = (partner.astype(jnp.float32) + sign * hidden.astype(jnp.float32)).astype(jnp.bfloat16)
    return hidden


def doubled(hidden, axis):
    parts = [hidden]
    for bit in reversed(range(bits_of(lax.axis_size(axis)))):
        parts = parts + [swap(part, axis, bit) for part in parts]
    return parts


def on_device(tokens, gate_code, up_code, down_code, gate_scale, up_scale, down_scale, sign_bits):
    peers = lax.axis_size("tensor")
    width = LOW * FACTOR
    chunks = gate_code.shape[1] // width
    rotation = jnp.asarray(low_rotation())
    signs = (2.0 * sign_bits.astype(jnp.float32) - 1.0).reshape(chunks, 1, width)

    token_parts = [tokens]
    for _ in range(peers - 1):
        token_parts.append(shift(token_parts[-1], "tensor"))

    parts = []
    for chunk in range(chunks):
        keep, send = gate_up(token_parts, gate_code, up_code, gate_scale, up_scale, chunk, width)
        hidden = hidden_of(halved(keep, send), signs, rotation, chunk)
        parts.append(doubled(rotated_over(hidden, "tensor"), "dp"))

    features = down_code.shape[1]
    halves = 2
    columns = features // halves
    results = []
    for column in range(halves):
        terms = down(parts, down_code, down_scale, column, columns)
        total = terms[0]
        for hop in range(1, peers):
            total = add(shift(total, "tensor"), terms[hop])
        results.append(total)
    return jnp.concatenate(results, axis=1)


def solution(mesh):
    in_specs = (
        P(("groups", "tensor"), "dp"),
        P("dp", "tensor"),
        P("dp", "tensor"),
        P("tensor", "dp"),
        P("dp", "tensor"),
        P("dp", "tensor"),
        P("tensor", "dp"),
        P("tensor"),
    )
    out_specs = P(("groups", "tensor"), "dp")
    return jax.shard_map(
        on_device, mesh=mesh, in_specs=in_specs, out_specs=out_specs, check_vma=False
    )
```

time: 417 us -> 218 us (0.52)
  waiting for transfers between devices: 221 us -> 105 us
  Pallas kernels: 0 us -> 78.3 us
  other arithmetic: 72.7 us -> 9.65 us
  matrix products: 55 us -> 0 us
  local copies, waits for them, and re-layouts: 49.1 us -> 4.04 us
  starting transfers between devices: 4.08 us -> 20.8 us
  between operations: 13.9 us -> 0.41 us
    unnamed x5 -> x0, waiting for transfers between devices: 129 us -> none
    pallas_call x0 -> x10, Pallas kernels: none -> 78.3 us  [the longest x4 37.3 us: gate_up(): pl.pallas_call(functools.partial(gate_up_kernel, peers, pieces), grid=(st...]
    convert_element_type x9 -> x18, other arithmetic: 67.8 us -> 8.92 us  [the longest x10 4.65 us: add(): sum((term.astype(jnp.float32) for term in terms)).astype(jnp.bfloat16)]
    dot_general x3 -> x0, matrix products: 55 us -> none  [the longest x1 28.8 us: on_device(): jnp.dot(lax.all_gather(tokens, 'tensor', axis=0, tiled=True), gate_up, pr...]
    ppermute x2 -> x37, waiting for transfers between devices: 53.4 us -> 105 us  [the longest x28 58.6 us: swap(): lax.ppermute(shard, axis, [(i, i ^ 1 << bit) for i in range(lax.axis_size...]
    reduce_scatter x1 -> x0, waiting for transfers between devices: 27.3 us -> none  [on_device(): lax.psum_scatter(partial_value.astype(jnp.bfloat16), 'tensor', scatter_di...]
    convert_element_type x2 -> x0, local copies, waits for them, and re-layouts: 20.1 us -> none  [the longest x1 17.5 us: on_device(): terms.astype(jnp.bfloat16)]
    ppermute x2 -> x37, starting transfers between devices: 3.96 us -> 20.8 us  [the longest x28 14.9 us: swap(): lax.ppermute(shard, axis, [(i, i ^ 1 << bit) for i in range(lax.axis_size...]
  transfers between devices with their start and end apart: 6 -> 37, of which waited for: 5 -> 21; matrix products, arithmetic and copies ran while one was open for 15% -> 4% of each run, Pallas kernels for 0% -> 27%
where the time goes in v1:
time: 218 us
  waiting for transfers between devices  105 us (48%)
  Pallas kernels  78.3 us (36%)
  starting transfers between devices  20.8 us (10%)
  other arithmetic  9.65 us (4%)
  local copies, waits for them, and re-layouts  4.04 us (2%)
    ppermute x28, waiting for transfers between devices, swap(): lax.ppermute(shard, axis, [(i, i ^ 1 << bit) for i in range(lax.axis_size...  58.6 us
    ppermute x9, waiting for transfers between devices, shift(): return lax.ppermute(shard, axis, [(i, (i + 1) % size) for i in range(size)])  45.9 us
    pallas_call x4, Pallas kernels, gate_up(): pl.pallas_call(functools.partial(gate_up_kernel, peers, pieces), grid=(st...  37.3 us
    pallas_call x2, Pallas kernels, down(): pl.pallas_call(functools.partial(down_kernel, chunks, pieces, peers), gri...  21.9 us
    pallas_call x4, Pallas kernels, hidden_of(): pl.pallas_call(hidden_kernel, grid=(1,), in_specs=[pl.BlockSpec((1, 2, sh...  19 us
    ppermute x28, starting transfers between devices, swap(): lax.ppermute(shard, axis, [(i, i ^ 1 << bit) for i in range(lax.axis_size...  14.9 us
    ppermute x9, starting transfers between devices, shift(): return lax.ppermute(shard, axis, [(i, (i + 1) % size) for i in range(size)])  5.91 us
    convert_element_type x10, other arithmetic, add(): sum((term.astype(jnp.float32) for term in terms)).astype(jnp.bfloat16)  4.65 us
  transfers between devices with their start and end apart: 37, of which 21 were waited for; matrix products, arithmetic and copies ran while one was open for 4% of the time, Pallas kernels for 27%

profile of v1, /device:TPU:0, one launch (start us, length us, event | category | flops | bytes accessed | tf_op | source)
XLA Modules:
  0.0 217.7 jit_solution(16086327431659549923)
XLA Ops:
  0.0 3.0 %collective-permute-start = (bf16[64,2048]{1,0:T(8,128)(2,1)}, bf16[64,2048]{1,0:T(8,128)(2,1)S(1)}, u32[]{:S(2)}, u32[]{:S(2)}) collective-permute-start(bf16[64,2048]{1,0:T(8,128)(2,1)} %refs_0_.7), channel_id=1, source_target_pairs={{0,4},{4,8},{8,12},{12,0},{1,5},{5,9},{9,13},{13,1},{2,6},{6,10},{... | collective-permute-start | bytes 786440 | tf_op jit(solution)/shard_map/ppermute | solution.py:27
  3.0 8.5 %collective-permute-done.refs_1_ = bf16[64,2048]{1,0:T(8,128)(2,1)S(1)} collective-permute-done((bf16[64,2048]{1,0:T(8,128)(2,1)}, bf16[64,2048]{1,0:T(8,128)(2,1)S(1)}, u32[]{:S(2)}, u32[]{:S(2)}) %collective-permute-start) | collective-permute-done | bytes 262176 | tf_op jit(solution)/shard_map/ppermute | solution.py:27
  11.6 9.3 %collective-permute-done.1.refs_2_ = bf16[64,2048]{1,0:T(8,128)(2,1)S(1)} collective-permute-done((bf16[64,2048]{1,0:T(8,128)(2,1)S(1)}, bf16[64,2048]{1,0:T(8,128)(2,1)S(1)}, u32[]{:S(2)}, u32[]{:S(2)}) %collective-permute-start.1) | collective-permute-done | bytes 262176 | tf_op jit(solution)/shard_map/ppermute | solution.py:27
  20.9 8.4 %collective-permute-done.2.refs_3_ = bf16[64,2048]{1,0:T(8,128)(2,1)S(1)} collective-permute-done((bf16[64,2048]{1,0:T(8,128)(2,1)S(1)}, bf16[64,2048]{1,0:T(8,128)(2,1)S(1)}, u32[]{:S(2)}, u32[]{:S(2)}) %collective-permute-start.2) | collective-permute-done | bytes 262176 | tf_op jit(solution)/shard_map/ppermute | solution.py:27
  29.2 0.7 copy-done.2
  30.0 9.4 %gate_up_3.1 = (bf16[2,2,64,1664]{3,2,1,0:T(8,128)(2,1)}, bf16[2,2,64,1664]{3,2,1,0:T(8,128)(2,1)}) custom-call(bf16[64,2048]{1,0:T(8,128)(2,1)} %refs_0_.7, bf16[64,2048]{1,0:T(8,128)(2,1)} %copy-done, bf16[64,2048]{1,0:T(8,128)(2,1)} %copy-done.1, bf16[64,2048]{1,0:T(8,128)(2,1)} %copy-done.2, bf16[2048,6656]{1,0:T(8,128)(2,1)} %refs_4_.11, ...), custom_call_target="tpu_custom_call" | custom-call | flops 3489660928 | bytes 13631488 | tf_op jit(solution)/shard_map/gate_up_3/pallas_call | solution.py:104
  39.4 9.2 %gate_up_2.1 = (bf16[2,2,64,1664]{3,2,1,0:T(8,128)(2,1)}, bf16[2,2,64,1664]{3,2,1,0:T(8,128)(2,1)}) custom-call(bf16[64,2048]{1,0:T(8,128)(2,1)} %refs_0_.7, bf16[64,2048]{1,0:T(8,128)(2,1)} %copy-done, bf16[64,2048]{1,0:T(8,128)(2,1)} %copy-done.1, bf16[64,2048]{1,0:T(8,128)(2,1)} %copy-done.2, bf16[2048,6656]{1,0:T(8,128)(2,1)} %refs_4_.11, ...), custom_call_target="tpu_custom_call" | custom-call | flops 3489660928 | bytes 13631488 | tf_op jit(solution)/shard_map/gate_up_2/pallas_call | solution.py:104
  48.7 0.5 collective-permute-start.17
  49.2 9.2 %gate_up_1.1 = (bf16[2,2,64,1664]{3,2,1,0:T(8,128)(2,1)}, bf16[2,2,64,1664]{3,2,1,0:T(8,128)(2,1)}) custom-call(bf16[64,2048]{1,0:T(8,128)(2,1)} %refs_0_.7, bf16[64,2048]{1,0:T(8,128)(2,1)} %copy-done, bf16[64,2048]{1,0:T(8,128)(2,1)} %copy-done.1, bf16[64,2048]{1,0:T(8,128)(2,1)} %copy-done.2, bf16[2048,6656]{1,0:T(8,128)(2,1)} %refs_4_.11, ...), custom_call_target="tpu_custom_call" | custom-call | flops 3489660928 | bytes 13631488 | tf_op jit(solution)/shard_map/gate_up_1/pallas_call | solution.py:104
  58.5 9.4 %gate_up_0.1 = (bf16[2,2,64,1664]{3,2,1,0:T(8,128)(2,1)}, bf16[2,2,64,1664]{3,2,1,0:T(8,128)(2,1)}) custom-call(bf16[64,2048]{1,0:T(8,128)(2,1)} %refs_0_.7, bf16[64,2048]{1,0:T(8,128)(2,1)} %copy-done, bf16[64,2048]{1,0:T(8,128)(2,1)} %copy-done.1, bf16[64,2048]{1,0:T(8,128)(2,1)} %copy-done.2, bf16[2048,6656]{1,0:T(8,128)(2,1)} %refs_4_.11, ...), custom_call_target="tpu_custom_call" | custom-call | flops 3489660928 | bytes 13631488 | tf_op jit(solution)/shard_map/gate_up_0/pallas_call | solution.py:104
  67.9 0.5 collective-permute-start.3
  68.6 1.1 collective-permute-start.25
  69.8 1.0 collective-permute-start.18
  70.9 1.1 collective-permute-start.11
  72.1 1.4 add_convert_fusion.3
  73.5 1.0 collective-permute-start.4
  74.5 0.6 reshape.15.refs_3_
  75.2 6.2 %collective-permute-done.25.refs_2_ = bf16[1,2,64,1664]{3,2,1,0:T(8,128)(2,1)} collective-permute-done((bf16[1,2,64,1664]{3,2,1,0:T(8,128)(2,1)S(1)}, bf16[1,2,64,1664]{3,2,1,0:T(8,128)(2,1)}, u32[]{:S(2)}, u32[]{:S(2)}) %collective-permute-start.25) | collective-permute-done | bytes 426016 | tf_op jit(solution)/shard_map/ppermute | solution.py:22
  81.4 4.7 %hidden_3.1 = bf16[64,1664]{1,0:T(8,128)(2,1)} custom-call(bf16[2,2,64,1664]{3,2,1,0:T(8,128)(2,1)} %get-tuple-element.19.refs_0_, bf16[2,2,64,1664]{3,2,1,0:T(8,128)(2,1)} %copy-done.14, bf16[1,2,64,1664]{3,2,1,0:T(8,128)(2,1)} %collective-permute-done.25.refs_2_, f32[4,1,1664]{2,1,0:T(1,128)} %reshape.15.refs_3_, bf16[1664,1664]{1,0:T(8,128)(2,1)} %constant.18.clone.refs_4_), custom_call_target="tpu_custom_call" | custom-call | flops 354418688 | bytes 5537792 | tf_op jit(solution)/shard_map/hidden_3/pallas_call | solution.py:136
  86.2 4.4 %collective-permute-done.18.refs_2_ = bf16[1,2,64,1664]{3,2,1,0:T(8,128)(2,1)} collective-permute-done((bf16[1,2,64,1664]{3,2,1,0:T(8,128)(2,1)S(1)}, bf16[1,2,64,1664]{3,2,1,0:T(8,128)(2,1)}, u32[]{:S(2)}, u32[]{:S(2)}) %collective-permute-start.18) | collective-permute-done | bytes 426016 | tf_op jit(solution)/shard_map/ppermute | solution.py:22
  90.5 4.8 %hidden_2.1 = bf16[64,1664]{1,0:T(8,128)(2,1)} custom-call(bf16[2,2,64,1664]{3,2,1,0:T(8,128)(2,1)} %get-tuple-element.17.refs_0_, bf16[2,2,64,1664]{3,2,1,0:T(8,128)(2,1)} %copy-done.12, bf16[1,2,64,1664]{3,2,1,0:T(8,128)(2,1)} %collective-permute-done.18.refs_2_, f32[4,1,1664]{2,1,0:T(1,128)} %reshape.15.refs_3_, bf16[1664,1664]{1,0:T(8,128)(2,1)} %constant.18.clone.refs_4_), custom_call_target="tpu_custom_call" | custom-call | flops 354418688 | bytes 5537792 | tf_op jit(solution)/shard_map/hidden_2/pallas_call | solution.py:136
  95.3 4.4 %collective-permute-done.11.refs_2_ = bf16[1,2,64,1664]{3,2,1,0:T(8,128)(2,1)} collective-permute-done((bf16[1,2,64,1664]{3,2,1,0:T(8,128)(2,1)S(1)}, bf16[1,2,64,1664]{3,2,1,0:T(8,128)(2,1)}, u32[]{:S(2)}, u32[]{:S(2)}) %collective-permute-start.11) | collective-permute-done | bytes 426016 | tf_op jit(solution)/shard_map/ppermute | solution.py:22
  99.7 4.8 %hidden_1.1 = bf16[64,1664]{1,0:T(8,128)(2,1)} custom-call(bf16[2,2,64,1664]{3,2,1,0:T(8,128)(2,1)} %get-tuple-element.15.refs_0_, bf16[2,2,64,1664]{3,2,1,0:T(8,128)(2,1)} %copy-done.10, bf16[1,2,64,1664]{3,2,1,0:T(8,128)(2,1)} %collective-permute-done.11.refs_2_, f32[4,1,1664]{2,1,0:T(1,128)} %reshape.15.refs_3_, bf16[1664,1664]{1,0:T(8,128)(2,1)} %constant.18.clone.refs_4_), custom_call_target="tpu_custom_call" | custom-call | flops 354418688 | bytes 5537792 | tf_op jit(solution)/shard_map/hidden_1/pallas_call | solution.py:136
  104.4 3.4 %collective-permute-done.4.refs_2_ = bf16[1,2,64,1664]{3,2,1,0:T(8,128)(2,1)} collective-permute-done((bf16[1,2,64,1664]{3,2,1,0:T(8,128)(2,1)S(1)}, bf16[1,2,64,1664]{3,2,1,0:T(8,128)(2,1)}, u32[]{:S(2)}, u32[]{:S(2)}) %collective-permute-start.4) | collective-permute-done | bytes 426016 | tf_op jit(solution)/shard_map/ppermute | solution.py:22
  107.9 4.7 %hidden_0.1 = bf16[64,1664]{1,0:T(8,128)(2,1)} custom-call(bf16[2,2,64,1664]{3,2,1,0:T(8,128)(2,1)} %get-tuple-element.13.refs_0_, bf16[2,2,64,1664]{3,2,1,0:T(8,128)(2,1)} %copy-done.9, bf16[1,2,64,1664]{3,2,1,0:T(8,128)(2,1)} %collective-permute-done.4.refs_2_, f32[4,1,1664]{2,1,0:T(1,128)} %reshape.15.refs_3_, bf16[1664,1664]{1,0:T(8,128)(2,1)} %constant.18.clone.refs_4_), custom_call_target="tpu_custom_call" | custom-call | flops 354418688 | bytes 5537792 | tf_op jit(solution)/shard_map/hidden_0/pallas_call | solution.py:136
  112.6 1.0 add_convert_fusion.5
  113.6 0.2 collective-permute-start.27
  113.8 1.0 add_convert_fusion.7
  114.8 2.9 %collective-permute-start.20 = (bf16[64,1664]{1,0:T(8,128)(2,1)S(1)}, bf16[64,1664]{1,0:T(8,128)(2,1)S(1)}, u32[]{:S(2)}, u32[]{:S(2)}) collective-permute-start(bf16[64,1664]{1,0:T(8,128)(2,1)S(1)} %add_convert_fusion.7), channel_id=1, source_target_pairs={{0,8},{4,12},{8,0},{12,4},{1,9},{5,13},{9,1},{13,5},{2,10},{6,14},... | collective-permute-start | bytes 638984 | tf_op jit(solution)/shard_map/ppermute | solution.py:22
  117.7 1.0 add_convert_fusion.9
  118.7 0.2 collective-permute-start.13
  118.9 1.5 collective-permute-done.5
  120.4 1.0 add_convert_fusion.11
  121.4 1.3 collective-permute-start.6
  122.8 17.8 %collective-permute-done.27 = bf16[64,1664]{1,0:T(8,128)(2,1)S(1)} collective-permute-done((bf16[64,1664]{1,0:T(8,128)(2,1)S(1)}, bf16[64,1664]{1,0:T(8,128)(2,1)S(1)}, u32[]{:S(2)}, u32[]{:S(2)}) %collective-permute-start.27) | collective-permute-done | bytes 213024 | tf_op jit(solution)/shard_map/ppermute | solution.py:22
  140.7 1.1 collective-permute-start.28
  141.8 3.3 %collective-permute-done.20 = bf16[64,1664]{1,0:T(8,128)(2,1)S(1)} collective-permute-done((bf16[64,1664]{1,0:T(8,128)(2,1)S(1)}, bf16[64,1664]{1,0:T(8,128)(2,1)S(1)}, u32[]{:S(2)}, u32[]{:S(2)}) %collective-permute-start.20) | collective-permute-done | bytes 213024 | tf_op jit(solution)/shard_map/ppermute | solution.py:22
  145.3 4.4 %collective-permute-done.13 = bf16[64,1664]{1,0:T(8,128)(2,1)S(1)} collective-permute-done((bf16[64,1664]{1,0:T(8,128)(2,1)S(1)}, bf16[64,1664]{1,0:T(8,128)(2,1)S(1)}, u32[]{:S(2)}, u32[]{:S(2)}) %collective-permute-start.13) | collective-permute-done | bytes 213024 | tf_op jit(solution)/shard_map/ppermute | solution.py:22
  149.7 1.0 collective-permute-start.21
  150.8 2.1 collective-permute-done.6
  153.0 1.1 collective-permute-start.14
  154.2 1.0 collective-permute-start.7
  155.1 0.4 collective-permute-done.21.refs_9_
  155.5 0.1 collective-permute-start.30
  155.7 0.4 collective-permute-start.23
  156.0 5.1 %collective-permute-done.14.refs_5_ = bf16[64,1664]{1,0:T(8,128)(2,1)S(1)} collective-permute-done((bf16[64,1664]{1,0:T(8,128)(2,1)S(1)}, bf16[64,1664]{1,0:T(8,128)(2,1)S(1)}, u32[]{:S(2)}, u32[]{:S(2)}) %collective-permute-start.14) | collective-permute-done | bytes 213024 | tf_op jit(solution)/shard_map/ppermute | solution.py:22
  161.2 4.2 %collective-permute-done.7.refs_1_ = bf16[64,1664]{1,0:T(8,128)(2,1)S(1)} collective-permute-done((bf16[64,1664]{1,0:T(8,128)(2,1)S(1)}, bf16[64,1664]{1,0:T(8,128)(2,1)S(1)}, u32[]{:S(2)}, u32[]{:S(2)}) %collective-permute-start.7) | collective-permute-done | bytes 213024 | tf_op jit(solution)/shard_map/ppermute | solution.py:22
  165.4 1.4 collective-permute-done.9.refs_3_
  166.9 0.7 copy-done.26
  167.6 10.9 %down_1.1 = bf16[4,64,1024]{2,1,0:T(8,128)(2,1)} custom-call(bf16[64,1664]{1,0:T(8,128)(2,1)} %copy-done.7, bf16[64,1664]{1,0:T(8,128)(2,1)} %copy-done.21, bf16[64,1664]{1,0:T(8,128)(2,1)} %copy-done.22, bf16[64,1664]{1,0:T(8,128)(2,1)} %copy-done.26, bf16[64,1664]{1,0:T(8,128)(2,1)} %copy-done.6, bf16[64,1664]{1,0:T(8,128)(2,1)} %copy-done.20, ...), custom_call_target="tpu_custom_call" | custom-call | flops 3489660928 | bytes 13631488 | tf_op jit(solution)/shard_map/down_1/pallas_call | solution.py:200
  178.6 1.0 slice_bitcast_fusion.3
  179.6 11.0 %down_0.1 = bf16[4,64,1024]{2,1,0:T(8,128)(2,1)} custom-call(bf16[64,1664]{1,0:T(8,128)(2,1)} %copy-done.7, bf16[64,1664]{1,0:T(8,128)(2,1)} %copy-done.21, bf16[64,1664]{1,0:T(8,128)(2,1)} %copy-done.22, bf16[64,1664]{1,0:T(8,128)(2,1)} %copy-done.26, bf16[64,1664]{1,0:T(8,128)(2,1)} %copy-done.6, bf16[64,1664]{1,0:T(8,128)(2,1)} %copy-done.20, ...), custom_call_target="tpu_custom_call" | custom-call | flops 3489660928 | bytes 13631488 | tf_op jit(solution)/shard_map/down_0/pallas_call | solution.py:200
  190.6 0.9 slice_bitcast_fusion.7
  191.5 0.1 collective-permute-start.31
  191.6 2.5 %collective-permute-start.35 = (bf16[64,1024]{1,0:T(8,128)(2,1)S(1)}, bf16[64,1024]{1,0:T(8,128)(2,1)S(1)}, u32[]{:S(2)}, u32[]{:S(2)}) collective-permute-start(bf16[64,1024]{1,0:T(8,128)(2,1)S(1)} %fusion.2), channel_id=1, source_target_pairs={{0,4},{4,8},{8,12},{12,0},{1,5},{5,9},{9,13},{13,1},{2,6},{6,10},{... | collective-permute-start | bytes 393224 | tf_op jit(solution)/shard_map/ppermute | solution.py:27
  194.2 5.5 %collective-permute-done.31 = bf16[64,1024]{1,0:T(8,128)(2,1)S(1)} collective-permute-done((bf16[64,1024]{1,0:T(8,128)(2,1)S(1)}, bf16[64,1024]{1,0:T(8,128)(2,1)S(1)}, u32[]{:S(2)}, u32[]{:S(2)}) %collective-permute-start.31) | collective-permute-done | bytes 131104 | tf_op jit(solution)/shard_map/ppermute | solution.py:27
  199.7 0.9 fusion.5
  200.7 1.0 collective-permute-done.35
  201.8 6.5 %collective-permute-done.32 = bf16[64,1024]{1,0:T(8,128)(2,1)S(1)} collective-permute-done((bf16[64,1024]{1,0:T(8,128)(2,1)S(1)}, bf16[64,1024]{1,0:T(8,128)(2,1)S(1)}, u32[]{:S(2)}, u32[]{:S(2)}) %collective-permute-start.32) | collective-permute-done | bytes 131104 | tf_op jit(solution)/shard_map/ppermute | solution.py:27
  208.3 0.9 fusion.4
  209.3 0.4 collective-permute-done.36
  209.7 6.3 %collective-permute-done.33 = bf16[64,1024]{1,0:T(8,128)(2,1)S(1)} collective-permute-done((bf16[64,1024]{1,0:T(8,128)(2,1)S(1)}, bf16[64,1024]{1,0:T(8,128)(2,1)S(1)}, u32[]{:S(2)}, u32[]{:S(2)}) %collective-permute-start.33) | collective-permute-done | bytes 131104 | tf_op jit(solution)/shard_map/ppermute | solution.py:27
  216.1 0.9 fusion.3
  217.0 0.7 pad_maximum_fusion
  (99 shorter events, 1.3 us)
Async XLA Ops:
  0.0 11.6 %collective-permute-start = (bf16[64,2048]{1,0:T(8,128)(2,1)}, bf16[64,2048]{1,0:T(8,128)(2,1)S(1)}, u32[]{:S(2)}, u32[]{:S(2)}) collective-permute-start(bf16[64,2048]{1,0:T(8,128)(2,1)} %refs_0_.7), channel_id=1, source_target_pairs={{0,4},{4,8},{8,12},{12,0},{1,5},{5,9},{9,13},{13,1},{2,6},{6,10},{... | collective-permute-start | bytes 786440 | tf_op jit(solution)/shard_map/ppermute | solution.py:27
  11.6 17.7 %copy-start = (bf16[64,2048]{1,0:T(8,128)(2,1)}, bf16[64,2048]{1,0:T(8,128)(2,1)S(1)}, u32[]{:S(2)}) copy-start(bf16[64,2048]{1,0:T(8,128)(2,1)S(1)} %collective-permute-done.refs_1_) | copy-start | bytes 786436
  11.6 9.3 %collective-permute-start.1 = (bf16[64,2048]{1,0:T(8,128)(2,1)S(1)}, bf16[64,2048]{1,0:T(8,128)(2,1)S(1)}, u32[]{:S(2)}, u32[]{:S(2)}) collective-permute-start(bf16[64,2048]{1,0:T(8,128)(2,1)S(1)} %collective-permute-done.refs_1_), channel_id=1, source_target_pairs={{0,4},{4,8},{8,12},{12,0},{1,5},{5,9},{9,13},{13,1},{2,6},{6,10},{... | collective-permute-start | bytes 786440 | tf_op jit(solution)/shard_map/ppermute | solution.py:27
  20.9 8.4 %copy-start.1 = (bf16[64,2048]{1,0:T(8,128)(2,1)}, bf16[64,2048]{1,0:T(8,128)(2,1)S(1)}, u32[]{:S(2)}) copy-start(bf16[64,2048]{1,0:T(8,128)(2,1)S(1)} %collective-permute-done.1.refs_2_) | copy-start | bytes 786436
  20.9 8.4 %collective-permute-start.2 = (bf16[64,2048]{1,0:T(8,128)(2,1)S(1)}, bf16[64,2048]{1,0:T(8,128)(2,1)S(1)}, u32[]{:S(2)}, u32[]{:S(2)}) collective-permute-start(bf16[64,2048]{1,0:T(8,128)(2,1)S(1)} %collective-permute-done.1.refs_2_), channel_id=1, source_target_pairs={{0,4},{4,8},{8,12},{12,0},{1,5},{5,9},{9,13},{13,1},{2,6},{6,10},{... | collective-permute-start | bytes 786440 | tf_op jit(solution)/shard_map/ppermute | solution.py:27
  29.2 0.7 copy-start.2
  39.4 29.0 %collective-permute-start.24 = (bf16[2,2,64,1664]{3,2,1,0:T(8,128)(2,1)}, bf16[2,2,64,1664]{3,2,1,0:T(8,128)(2,1)S(1)}, u32[]{:S(2)}, u32[]{:S(2)}) collective-permute-start(bf16[2,2,64,1664]{3,2,1,0:T(8,128)(2,1)} %get-tuple-element.20), channel_id=1, source_target_pairs={{0,1},{1,0},{2,3},{3,2},{4,5},{5,4},{6,7},{7,6},{8,9},{9,8},{10,11... | collective-permute-start | bytes 2555912 | tf_op jit(solution)/shard_map/ppermute | solution.py:22
  48.7 21.0 %collective-permute-start.17 = (bf16[2,2,64,1664]{3,2,1,0:T(8,128)(2,1)}, bf16[2,2,64,1664]{3,2,1,0:T(8,128)(2,1)S(1)}, u32[]{:S(2)}, u32[]{:S(2)}) collective-permute-start(bf16[2,2,64,1664]{3,2,1,0:T(8,128)(2,1)} %get-tuple-element.18), channel_id=1, source_target_pairs={{0,1},{1,0},{2,3},{3,2},{4,5},{5,4},{6,7},{7,6},{8,9},{9,8},{10,11... | collective-permute-start | bytes 2555912 | tf_op jit(solution)/shard_map/ppermute | solution.py:22
  58.4 10.1 %copy-start.13 = (bf16[2,2,64,1664]{3,2,1,0:T(8,128)(2,1)S(1)}, bf16[2,2,64,1664]{3,2,1,0:T(8,128)(2,1)}, u32[]{:S(2)}) copy-start(bf16[2,2,64,1664]{3,2,1,0:T(8,128)(2,1)} %get-tuple-element.19.refs_0_) | copy-start | bytes 2555908
  58.4 11.3 %copy-start.11 = (bf16[2,2,64,1664]{3,2,1,0:T(8,128)(2,1)S(1)}, bf16[2,2,64,1664]{3,2,1,0:T(8,128)(2,1)}, u32[]{:S(2)}) copy-start(bf16[2,2,64,1664]{3,2,1,0:T(8,128)(2,1)} %get-tuple-element.17.refs_0_) | copy-start | bytes 2555908
  58.4 12.5 %copy-start.8 = (bf16[2,2,64,1664]{3,2,1,0:T(8,128)(2,1)S(1)}, bf16[2,2,64,1664]{3,2,1,0:T(8,128)(2,1)}, u32[]{:S(2)}) copy-start(bf16[2,2,64,1664]{3,2,1,0:T(8,128)(2,1)} %get-tuple-element.15.refs_0_) | copy-start | bytes 2555908
  58.4 16.1 %copy-start.27 = (s32[6656]{0:T(1024)S(1)}, s32[6656]{0:T(1024)}, u32[]{:S(2)}) copy-start(s32[6656]{0:T(1024)} %param.16) | copy-start | bytes 79876
  58.4 12.4 %collective-permute-start.10 = (bf16[2,2,64,1664]{3,2,1,0:T(8,128)(2,1)}, bf16[2,2,64,1664]{3,2,1,0:T(8,128)(2,1)S(1)}, u32[]{:S(2)}, u32[]{:S(2)}) collective-permute-start(bf16[2,2,64,1664]{3,2,1,0:T(8,128)(2,1)} %get-tuple-element.16), channel_id=1, source_target_pairs={{0,1},{1,0},{2,3},{3,2},{4,5},{5,4},{6,7},{7,6},{8,9},{9,8},{10,11... | collective-permute-start | bytes 2555912 | tf_op jit(solution)/shard_map/ppermute | solution.py:22
  67.9 4.1 %collective-permute-start.3 = (bf16[2,2,64,1664]{3,2,1,0:T(8,128)(2,1)}, bf16[2,2,64,1664]{3,2,1,0:T(8,128)(2,1)S(1)}, u32[]{:S(2)}, u32[]{:S(2)}) collective-permute-start(bf16[2,2,64,1664]{3,2,1,0:T(8,128)(2,1)} %get-tuple-element.14), channel_id=1, source_target_pairs={{0,1},{1,0},{2,3},{3,2},{4,5},{5,4},{6,7},{7,6},{8,9},{9,8},{10,11... | collective-permute-start | bytes 2555912 | tf_op jit(solution)/shard_map/ppermute | solution.py:22
  68.5 3.6 %copy-start.14 = (bf16[2,2,64,1664]{3,2,1,0:T(8,128)(2,1)}, bf16[2,2,64,1664]{3,2,1,0:T(8,128)(2,1)S(1)}, u32[]{:S(2)}) copy-start(bf16[2,2,64,1664]{3,2,1,0:T(8,128)(2,1)S(1)} %collective-permute-done.24.refs_1_) | copy-start | bytes 2555908
  68.6 12.8 %collective-permute-start.25 = (bf16[1,2,64,1664]{3,2,1,0:T(8,128)(2,1)S(1)}, bf16[1,2,64,1664]{3,2,1,0:T(8,128)(2,1)}, u32[]{:S(2)}, u32[]{:S(2)}) collective-permute-start(bf16[1,2,64,1664]{3,2,1,0:T(8,128)(2,1)S(1)} %add_convert_fusion), channel_id=1, source_target_pairs={{0,2},{1,3},{2,0},{3,1},{4,6},{5,7},{6,4},{7,5},{8,10},{9,11},{10,... | collective-permute-start | bytes 1277960 | tf_op jit(solution)/shard_map/ppermute | solution.py:22
  69.7 2.4 %copy-start.12 = (bf16[2,2,64,1664]{3,2,1,0:T(8,128)(2,1)}, bf16[2,2,64,1664]{3,2,1,0:T(8,128)(2,1)S(1)}, u32[]{:S(2)}) copy-start(bf16[2,2,64,1664]{3,2,1,0:T(8,128)(2,1)S(1)} %collective-permute-done.17.refs_1_) | copy-start | bytes 2555908
  69.8 20.8 %collective-permute-start.18 = (bf16[1,2,64,1664]{3,2,1,0:T(8,128)(2,1)S(1)}, bf16[1,2,64,1664]{3,2,1,0:T(8,128)(2,1)}, u32[]{:S(2)}, u32[]{:S(2)}) collective-permute-start(bf16[1,2,64,1664]{3,2,1,0:T(8,128)(2,1)S(1)} %add_convert_fusion.1), channel_id=1, source_target_pairs={{0,2},{1,3},{2,0},{3,1},{4,6},{5,7},{6,4},{7,5},{8,10},{9,11},{10,... | collective-permute-start | bytes 1277960 | tf_op jit(solution)/shard_map/ppermute | solution.py:22
  70.8 28.8 %copy-start.10 = (bf16[2,2,64,1664]{3,2,1,0:T(8,128)(2,1)}, bf16[2,2,64,1664]{3,2,1,0:T(8,128)(2,1)S(1)}, u32[]{:S(2)}) copy-start(bf16[2,2,64,1664]{3,2,1,0:T(8,128)(2,1)S(1)} %collective-permute-done.10.refs_1_) | copy-start | bytes 2555908
  70.9 28.7 %collective-permute-start.11 = (bf16[1,2,64,1664]{3,2,1,0:T(8,128)(2,1)S(1)}, bf16[1,2,64,1664]{3,2,1,0:T(8,128)(2,1)}, u32[]{:S(2)}, u32[]{:S(2)}) collective-permute-start(bf16[1,2,64,1664]{3,2,1,0:T(8,128)(2,1)S(1)} %add_convert_fusion.2), channel_id=1, source_target_pairs={{0,2},{1,3},{2,0},{3,1},{4,6},{5,7},{6,4},{7,5},{8,10},{9,11},{10,... | collective-permute-start | bytes 1277960 | tf_op jit(solution)/shard_map/ppermute | solution.py:22
  72.1 35.8 %copy-start.9 = (bf16[2,2,64,1664]{3,2,1,0:T(8,128)(2,1)}, bf16[2,2,64,1664]{3,2,1,0:T(8,128)(2,1)S(1)}, u32[]{:S(2)}) copy-start(bf16[2,2,64,1664]{3,2,1,0:T(8,128)(2,1)S(1)} %collective-permute-done.3.refs_1_) | copy-start | bytes 2555908
  73.5 34.4 %collective-permute-start.4 = (bf16[1,2,64,1664]{3,2,1,0:T(8,128)(2,1)S(1)}, bf16[1,2,64,1664]{3,2,1,0:T(8,128)(2,1)}, u32[]{:S(2)}, u32[]{:S(2)}) collective-permute-start(bf16[1,2,64,1664]{3,2,1,0:T(8,128)(2,1)S(1)} %add_convert_fusion.3), channel_id=1, source_target_pairs={{0,2},{1,3},{2,0},{3,1},{4,6},{5,7},{6,4},{7,5},{8,10},{9,11},{10,... | collective-permute-start | bytes 1277960 | tf_op jit(solution)/shard_map/ppermute | solution.py:22
  86.2 26.5 %collective-permute-start.26 = (bf16[64,1664]{1,0:T(8,128)(2,1)}, bf16[64,1664]{1,0:T(8,128)(2,1)S(1)}, u32[]{:S(2)}, u32[]{:S(2)}) collective-permute-start(bf16[64,1664]{1,0:T(8,128)(2,1)} %hidden_3.1), channel_id=1, source_target_pairs={{0,4},{4,0},{8,12},{12,8},{1,5},{5,1},{9,13},{13,9},{2,6},{6,2},{1... | collective-permute-start | bytes 638984 | tf_op jit(solution)/shard_map/ppermute | solution.py:22
  95.3 18.5 %collective-permute-start.19 = (bf16[64,1664]{1,0:T(8,128)(2,1)}, bf16[64,1664]{1,0:T(8,128)(2,1)S(1)}, u32[]{:S(2)}, u32[]{:S(2)}) collective-permute-start(bf16[64,1664]{1,0:T(8,128)(2,1)} %hidden_2.1), channel_id=1, source_target_pairs={{0,4},{4,0},{8,12},{12,8},{1,5},{5,1},{9,13},{13,9},{2,6},{6,2},{1... | collective-permute-start | bytes 638984 | tf_op jit(solution)/shard_map/ppermute | solution.py:22
  104.4 13.3 %collective-permute-start.12 = (bf16[64,1664]{1,0:T(8,128)(2,1)}, bf16[64,1664]{1,0:T(8,128)(2,1)S(1)}, u32[]{:S(2)}, u32[]{:S(2)}) collective-permute-start(bf16[64,1664]{1,0:T(8,128)(2,1)} %hidden_1.1), channel_id=1, source_target_pairs={{0,4},{4,0},{8,12},{12,8},{1,5},{5,1},{9,13},{13,9},{2,6},{6,2},{1... | collective-permute-start | bytes 638984 | tf_op jit(solution)/shard_map/ppermute | solution.py:22
  112.6 7.8 %collective-permute-start.5 = (bf16[64,1664]{1,0:T(8,128)(2,1)}, bf16[64,1664]{1,0:T(8,128)(2,1)S(1)}, u32[]{:S(2)}, u32[]{:S(2)}) collective-permute-start(bf16[64,1664]{1,0:T(8,128)(2,1)} %hidden_0.1), channel_id=1, source_target_pairs={{0,4},{4,0},{8,12},{12,8},{1,5},{5,1},{9,13},{13,9},{2,6},{6,2},{1... | collective-permute-start | bytes 638984 | tf_op jit(solution)/shard_map/ppermute | solution.py:22
  113.6 26.9 %collective-permute-start.27 = (bf16[64,1664]{1,0:T(8,128)(2,1)S(1)}, bf16[64,1664]{1,0:T(8,128)(2,1)S(1)}, u32[]{:S(2)}, u32[]{:S(2)}) collective-permute-start(bf16[64,1664]{1,0:T(8,128)(2,1)S(1)} %add_convert_fusion.5), channel_id=1, source_target_pairs={{0,8},{4,12},{8,0},{12,4},{1,9},{5,13},{9,1},{13,5},{2,10},{6,14},... | collective-permute-start | bytes 638984 | tf_op jit(solution)/shard_map/ppermute | solution.py:22
  114.8 30.3 %collective-permute-start.20 = (bf16[64,1664]{1,0:T(8,128)(2,1)S(1)}, bf16[64,1664]{1,0:T(8,128)(2,1)S(1)}, u32[]{:S(2)}, u32[]{:S(2)}) collective-permute-start(bf16[64,1664]{1,0:T(8,128)(2,1)S(1)} %add_convert_fusion.7), channel_id=1, source_target_pairs={{0,8},{4,12},{8,0},{12,4},{1,9},{5,13},{9,1},{13,5},{2,10},{6,14},... | collective-permute-start | bytes 638984 | tf_op jit(solution)/shard_map/ppermute | solution.py:22
  118.7 31.0 %collective-permute-start.13 = (bf16[64,1664]{1,0:T(8,128)(2,1)S(1)}, bf16[64,1664]{1,0:T(8,128)(2,1)S(1)}, u32[]{:S(2)}, u32[]{:S(2)}) collective-permute-start(bf16[64,1664]{1,0:T(8,128)(2,1)S(1)} %add_convert_fusion.9), channel_id=1, source_target_pairs={{0,8},{4,12},{8,0},{12,4},{1,9},{5,13},{9,1},{13,5},{2,10},{6,14},... | collective-permute-start | bytes 638984 | tf_op jit(solution)/shard_map/ppermute | solution.py:22
  121.4 31.5 %collective-permute-start.6 = (bf16[64,1664]{1,0:T(8,128)(2,1)S(1)}, bf16[64,1664]{1,0:T(8,128)(2,1)S(1)}, u32[]{:S(2)}, u32[]{:S(2)}) collective-permute-start(bf16[64,1664]{1,0:T(8,128)(2,1)S(1)} %add_convert_fusion.11), channel_id=1, source_target_pairs={{0,8},{4,12},{8,0},{12,4},{1,9},{5,13},{9,1},{13,5},{2,10},{6,14},... | collective-permute-start | bytes 638984 | tf_op jit(solution)/shard_map/ppermute | solution.py:22
  140.6 26.2 %copy-start.4 = (bf16[64,1664]{1,0:T(8,128)(2,1)}, bf16[64,1664]{1,0:T(8,128)(2,1)S(1)}, u32[]{:S(2)}) copy-start(bf16[64,1664]{1,0:T(8,128)(2,1)S(1)} %add_convert_fusion.4.refs_12_) | copy-start | bytes 638980
  140.6 12.4 %collective-permute-start.29 = (bf16[64,1664]{1,0:T(8,128)(2,1)S(1)}, bf16[64,1664]{1,0:T(8,128)(2,1)S(1)}, u32[]{:S(2)}, u32[]{:S(2)}) collective-permute-start(bf16[64,1664]{1,0:T(8,128)(2,1)S(1)} %add_convert_fusion.4.refs_12_), channel_id=1, source_target_pairs={{0,1},{1,0},{2,3},{3,2},{4,5},{5,4},{6,7},{7,6},{8,9},{9,8},{10,11... | collective-permute-start | bytes 638984 | tf_op jit(solution)/shard_map/ppermute | solution.py:22
  140.7 13.5 %collective-permute-start.28 = (bf16[64,1664]{1,0:T(8,128)(2,1)S(1)}, bf16[64,1664]{1,0:T(8,128)(2,1)S(1)}, u32[]{:S(2)}, u32[]{:S(2)}) collective-permute-start(bf16[64,1664]{1,0:T(8,128)(2,1)S(1)} %add_convert_fusion.4.refs_12_), channel_id=1, source_target_pairs={{0,2},{1,3},{2,0},{3,1},{4,6},{5,7},{6,4},{7,5},{8,10},{9,11},{10,... | collective-permute-start | bytes 638984 | tf_op jit(solution)/shard_map/ppermute | solution.py:22
  145.2 21.6 %copy-start.5 = (bf16[64,1664]{1,0:T(8,128)(2,1)}, bf16[64,1664]{1,0:T(8,128)(2,1)S(1)}, u32[]{:S(2)}) copy-start(bf16[64,1664]{1,0:T(8,128)(2,1)S(1)} %add_convert_fusion.6.refs_8_) | copy-start | bytes 638980
  145.2 10.0 %collective-permute-start.22 = (bf16[64,1664]{1,0:T(8,128)(2,1)S(1)}, bf16[64,1664]{1,0:T(8,128)(2,1)S(1)}, u32[]{:S(2)}, u32[]{:S(2)}) collective-permute-start(bf16[64,1664]{1,0:T(8,128)(2,1)S(1)} %add_convert_fusion.6.refs_8_), channel_id=1, source_target_pairs={{0,1},{1,0},{2,3},{3,2},{4,5},{5,4},{6,7},{7,6},{8,9},{9,8},{10,11... | collective-permute-start | bytes 638984 | tf_op jit(solution)/shard_map/ppermute | solution.py:22
  149.7 5.8 %collective-permute-start.21 = (bf16[64,1664]{1,0:T(8,128)(2,1)S(1)}, bf16[64,1664]{1,0:T(8,128)(2,1)S(1)}, u32[]{:S(2)}, u32[]{:S(2)}) collective-permute-start(bf16[64,1664]{1,0:T(8,128)(2,1)S(1)} %add_convert_fusion.6.refs_8_), channel_id=1, source_target_pairs={{0,2},{1,3},{2,0},{3,1},{4,6},{5,7},{6,4},{7,5},{8,10},{9,11},{10,... | collective-permute-start | bytes 638984 | tf_op jit(solution)/shard_map/ppermute | solution.py:22
  150.8 16.0 %copy-start.6 = (bf16[64,1664]{1,0:T(8,128)(2,1)}, bf16[64,1664]{1,0:T(8,128)(2,1)S(1)}, u32[]{:S(2)}) copy-start(bf16[64,1664]{1,0:T(8,128)(2,1)S(1)} %add_convert_fusion.8.refs_4_) | copy-start | bytes 638980
  152.9 2.7 %collective-permute-start.15 = (bf16[64,1664]{1,0:T(8,128)(2,1)S(1)}, bf16[64,1664]{1,0:T(8,128)(2,1)S(1)}, u32[]{:S(2)}, u32[]{:S(2)}) collective-permute-start(bf16[64,1664]{1,0:T(8,128)(2,1)S(1)} %add_convert_fusion.8.refs_4_), channel_id=1, source_target_pairs={{0,1},{1,0},{2,3},{3,2},{4,5},{5,4},{6,7},{7,6},{8,9},{9,8},{10,11... | collective-permute-start | bytes 638984 | tf_op jit(solution)/shard_map/ppermute | solution.py:22
  153.0 13.8 %copy-start.7 = (bf16[64,1664]{1,0:T(8,128)(2,1)}, bf16[64,1664]{1,0:T(8,128)(2,1)S(1)}, u32[]{:S(2)}) copy-start(bf16[64,1664]{1,0:T(8,128)(2,1)S(1)} %add_convert_fusion.10.refs_0_) | copy-start | bytes 638980
  153.0 13.8 %copy-start.15 = (bf16[64,1664]{1,0:T(8,128)(2,1)}, bf16[64,1664]{1,0:T(8,128)(2,1)S(1)}, u32[]{:S(2)}) copy-start(bf16[64,1664]{1,0:T(8,128)(2,1)S(1)} %collective-permute-done.29.refs_14_) | copy-start | bytes 638980
  153.0 8.1 %collective-permute-start.14 = (bf16[64,1664]{1,0:T(8,128)(2,1)S(1)}, bf16[64,1664]{1,0:T(8,128)(2,1)S(1)}, u32[]{:S(2)}, u32[]{:S(2)}) collective-permute-start(bf16[64,1664]{1,0:T(8,128)(2,1)S(1)} %add_convert_fusion.8.refs_4_), channel_id=1, source_target_pairs={{0,2},{1,3},{2,0},{3,1},{4,6},{5,7},{6,4},{7,5},{8,10},{9,11},{10,... | collective-permute-start | bytes 638984 | tf_op jit(solution)/shard_map/ppermute | solution.py:22
  154.2 12.7 %copy-start.16 = (bf16[64,1664]{1,0:T(8,128)(2,1)}, bf16[64,1664]{1,0:T(8,128)(2,1)S(1)}, u32[]{:S(2)}) copy-start(bf16[64,1664]{1,0:T(8,128)(2,1)S(1)} %collective-permute-done.28.refs_13_) | copy-start | bytes 638980
  154.2 11.2 %collective-permute-start.7 = (bf16[64,1664]{1,0:T(8,128)(2,1)S(1)}, bf16[64,1664]{1,0:T(8,128)(2,1)S(1)}, u32[]{:S(2)}, u32[]{:S(2)}) collective-permute-start(bf16[64,1664]{1,0:T(8,128)(2,1)S(1)} %add_convert_fusion.10.refs_0_), channel_id=1, source_target_pairs={{0,2},{1,3},{2,0},{3,1},{4,6},{5,7},{6,4},{7,5},{8,10},{9,11},{10,... | collective-permute-start | bytes 638984 | tf_op jit(solution)/shard_map/ppermute | solution.py:22
  155.1 11.7 %copy-start.17 = (bf16[64,1664]{1,0:T(8,128)(2,1)}, bf16[64,1664]{1,0:T(8,128)(2,1)S(1)}, u32[]{:S(2)}) copy-start(bf16[64,1664]{1,0:T(8,128)(2,1)S(1)} %collective-permute-done.22.refs_10_) | copy-start | bytes 638980
  155.1 10.2 %collective-permute-start.8 = (bf16[64,1664]{1,0:T(8,128)(2,1)S(1)}, bf16[64,1664]{1,0:T(8,128)(2,1)S(1)}, u32[]{:S(2)}, u32[]{:S(2)}) collective-permute-start(bf16[64,1664]{1,0:T(8,128)(2,1)S(1)} %add_convert_fusion.10.refs_0_), channel_id=1, source_target_pairs={{0,1},{1,0},{2,3},{3,2},{4,5},{5,4},{6,7},{7,6},{8,9},{9,8},{10,11... | collective-permute-start | bytes 638984 | tf_op jit(solution)/shard_map/ppermute | solution.py:22
  155.5 11.3 %copy-start.18 = (bf16[64,1664]{1,0:T(8,128)(2,1)}, bf16[64,1664]{1,0:T(8,128)(2,1)S(1)}, u32[]{:S(2)}) copy-start(bf16[64,1664]{1,0:T(8,128)(2,1)S(1)} %collective-permute-done.21.refs_9_) | copy-start | bytes 638980
  155.5 9.8 %collective-permute-start.30 = (bf16[64,1664]{1,0:T(8,128)(2,1)S(1)}, bf16[64,1664]{1,0:T(8,128)(2,1)S(1)}, u32[]{:S(2)}, u32[]{:S(2)}) collective-permute-start(bf16[64,1664]{1,0:T(8,128)(2,1)S(1)} %collective-permute-done.28.refs_13_), channel_id=1, source_target_pairs={{0,1},{1,0},{2,3},{3,2},{4,5},{5,4},{6,7},{7,6},{8,9},{9,8},{10,11... | collective-permute-start | bytes 638984 | tf_op jit(solution)/shard_map/ppermute | solution.py:22
  155.7 11.2 %copy-start.19 = (bf16[64,1664]{1,0:T(8,128)(2,1)}, bf16[64,1664]{1,0:T(8,128)(2,1)S(1)}, u32[]{:S(2)}) copy-start(bf16[64,1664]{1,0:T(8,128)(2,1)S(1)} %collective-permute-done.15.refs_6_) | copy-start | bytes 638980
  155.7 9.7 %collective-permute-start.23 = (bf16[64,1664]{1,0:T(8,128)(2,1)S(1)}, bf16[64,1664]{1,0:T(8,128)(2,1)S(1)}, u32[]{:S(2)}, u32[]{:S(2)}) collective-permute-start(bf16[64,1664]{1,0:T(8,128)(2,1)S(1)} %collective-permute-done.21.refs_9_), channel_id=1, source_target_pairs={{0,1},{1,0},{2,3},{3,2},{4,5},{5,4},{6,7},{7,6},{8,9},{9,8},{10,11... | collective-permute-start | bytes 638984 | tf_op jit(solution)/shard_map/ppermute | solution.py:22
  161.2 5.7 %copy-start.20 = (bf16[64,1664]{1,0:T(8,128)(2,1)}, bf16[64,1664]{1,0:T(8,128)(2,1)S(1)}, u32[]{:S(2)}) copy-start(bf16[64,1664]{1,0:T(8,128)(2,1)S(1)} %collective-permute-done.14.refs_5_) | copy-start | bytes 638980
  161.2 4.2 %collective-permute-start.16 = (bf16[64,1664]{1,0:T(8,128)(2,1)S(1)}, bf16[64,1664]{1,0:T(8,128)(2,1)S(1)}, u32[]{:S(2)}, u32[]{:S(2)}) collective-permute-start(bf16[64,1664]{1,0:T(8,128)(2,1)S(1)} %collective-permute-done.14.refs_5_), channel_id=1, source_target_pairs={{0,1},{1,0},{2,3},{3,2},{4,5},{5,4},{6,7},{7,6},{8,9},{9,8},{10,11... | collective-permute-start | bytes 638984 | tf_op jit(solution)/shard_map/ppermute | solution.py:22
  165.3 1.6 copy-start.21
  165.3 1.5 collective-permute-start.9
  165.3 1.5 copy-start.22
  165.4 1.5 copy-start.23
  165.4 1.5 copy-start.24
  165.4 1.5 copy-start.25
  178.6 13.0 %copy-start.3 = (bf16[4,64,1024]{2,1,0:T(8,128)(2,1)S(1)}, bf16[4,64,1024]{2,1,0:T(8,128)(2,1)}, u32[]{:S(2)}) copy-start(bf16[4,64,1024]{2,1,0:T(8,128)(2,1)} %down_1.1) | copy-start | bytes 1572868
  179.5 12.0 %collective-permute-start.34 = (bf16[64,1024]{1,0:T(8,128)(2,1)S(1)}, bf16[64,1024]{1,0:T(8,128)(2,1)S(1)}, u32[]{:S(2)}, u32[]{:S(2)}) collective-permute-start(bf16[64,1024]{1,0:T(8,128)(2,1)S(1)} %slice_bitcast_fusion.3), channel_id=1, source_target_pairs={{0,4},{4,8},{8,12},{12,0},{1,5},{5,9},{9,13},{13,1},{2,6},{6,10},{... | collective-permute-start | bytes 393224 | tf_op jit(solution)/shard_map/ppermute | solution.py:27
  191.5 8.2 %collective-permute-start.31 = (bf16[64,1024]{1,0:T(8,128)(2,1)S(1)}, bf16[64,1024]{1,0:T(8,128)(2,1)S(1)}, u32[]{:S(2)}, u32[]{:S(2)}) collective-permute-start(bf16[64,1024]{1,0:T(8,128)(2,1)S(1)} %slice_bitcast_fusion.7), channel_id=1, source_target_pairs={{0,4},{4,8},{8,12},{12,0},{1,5},{5,9},{9,13},{13,1},{2,6},{6,10},{... | collective-permute-start | bytes 393224 | tf_op jit(solution)/shard_map/ppermute | solution.py:27
  191.6 10.1 %collective-permute-start.35 = (bf16[64,1024]{1,0:T(8,128)(2,1)S(1)}, bf16[64,1024]{1,0:T(8,128)(2,1)S(1)}, u32[]{:S(2)}, u32[]{:S(2)}) collective-permute-start(bf16[64,1024]{1,0:T(8,128)(2,1)S(1)} %fusion.2), channel_id=1, source_target_pairs={{0,4},{4,8},{8,12},{12,0},{1,5},{5,9},{9,13},{13,1},{2,6},{6,10},{... | collective-permute-start | bytes 393224 | tf_op jit(solution)/shard_map/ppermute | solution.py:27
  200.6 7.7 %collective-permute-start.32 = (bf16[64,1024]{1,0:T(8,128)(2,1)S(1)}, bf16[64,1024]{1,0:T(8,128)(2,1)S(1)}, u32[]{:S(2)}, u32[]{:S(2)}) collective-permute-start(bf16[64,1024]{1,0:T(8,128)(2,1)S(1)} %fusion.5), channel_id=1, source_target_pairs={{0,4},{4,8},{8,12},{12,0},{1,5},{5,9},{9,13},{13,1},{2,6},{6,10},{... | collective-permute-start | bytes 393224 | tf_op jit(solution)/shard_map/ppermute | solution.py:27
  201.7 8.0 %collective-permute-start.36 = (bf16[64,1024]{1,0:T(8,128)(2,1)S(1)}, bf16[64,1024]{1,0:T(8,128)(2,1)S(1)}, u32[]{:S(2)}, u32[]{:S(2)}) collective-permute-start(bf16[64,1024]{1,0:T(8,128)(2,1)S(1)} %fusion.1), channel_id=1, source_target_pairs={{0,4},{4,8},{8,12},{12,0},{1,5},{5,9},{9,13},{13,1},{2,6},{6,10},{... | collective-permute-start | bytes 393224 | tf_op jit(solution)/shard_map/ppermute | solution.py:27
  209.2 6.8 %collective-permute-start.33 = (bf16[64,1024]{1,0:T(8,128)(2,1)S(1)}, bf16[64,1024]{1,0:T(8,128)(2,1)S(1)}, u32[]{:S(2)}, u32[]{:S(2)}) collective-permute-start(bf16[64,1024]{1,0:T(8,128)(2,1)S(1)} %fusion.4), channel_id=1, source_target_pairs={{0,4},{4,8},{8,12},{12,0},{1,5},{5,9},{9,13},{13,1},{2,6},{6,10},{... | collective-permute-start | bytes 393224 | tf_op jit(solution)/shard_map/ppermute | solution.py:27
  (1 other events, 0.7 us)

commit v2 on v1

v2 whole, which is shorter than its diff:
```python
import functools

import jax
import jax.numpy as jnp
import numpy as np
from jax import lax
from jax.experimental import pallas as pl
from jax.experimental.pallas import tpu as pltpu
from jax.sharding import PartitionSpec as P

POW = 2048
FACTOR = 13
LOW = 128
SMALL = 16
TILE = 512
AHEAD = 3
VMEM_LIMIT = 56 * 2**20


def bits_of(size):
    return size.bit_length() - 1


def swap(shard, axis, bit):
    return lax.ppermute(shard, axis, [(i, i ^ 1 << bit) for i in range(lax.axis_size(axis))])


def shift(shard, axis, step=1):
    size = lax.axis_size(axis)
    return lax.ppermute(shard, axis, [(i, (i + step) % size) for i in range(size)])


def reversed_bits(value, bits):
    return sum((value >> i & 1) << (bits - 1 - i) for i in range(bits))


def params(**more):
    return pltpu.CompilerParams(vmem_limit_bytes=VMEM_LIMIT, **more)


def matrix_part():
    order = np.arange(SMALL)
    common = order[:, None] & order[None, :]
    parity = np.zeros_like(common)
    for bit in range(bits_of(SMALL)):
        parity ^= common >> bit & 1
    return np.kron(1 - 2 * parity, np.eye(FACTOR)).astype(jnp.bfloat16)


def butterflies(values):
    values = list(values)
    gap = 1
    while gap < len(values):
        for low in range(len(values)):
            if not low & gap:
                left, right = values[low], values[low | gap]
                values[low], values[low | gap] = left + right, left - right
        gap *= 2
    return values


def scaled(codes, scales):
    depth, cols = codes.shape
    groups = scales.shape[0]
    product = codes.astype(jnp.float32).reshape(groups, depth // groups, cols) * scales[:, None, :]
    return product.astype(jnp.bfloat16).reshape(depth, cols)


def fold_kernel(chunks, blocks, first, *refs):
    code_refs, (scale_in_ref, out_ref, scale_ref) = refs[:chunks], refs[chunks:]
    step = pl.program_id(0)

    @pl.when(step == 0)
    def _():
        scale_ref[...] = scale_in_ref[...].astype(jnp.float32)

    values = [
        code_refs[chunk][...].astype(jnp.float32) * scale_ref[pl.ds(chunk * blocks + first + step, 1), :]
        for chunk in range(chunks)
    ]
    for chunk, value in enumerate(butterflies(values)):
        out_ref[chunk] = value.astype(jnp.bfloat16)


def folded(down_code, down_scale, chunks, first, count):
    units, features = down_code.shape
    groups = down_scale.shape[0]
    blocks = groups // chunks
    depth = units // groups

    def code_spec(chunk):
        return pl.BlockSpec((depth, features), lambda k: (chunk * blocks + first + k, 0))

    return pl.pallas_call(
        functools.partial(fold_kernel, chunks, blocks, first),
        grid=(count,),
        in_specs=[code_spec(chunk) for chunk in range(chunks)]
        + [pl.BlockSpec((groups, features), lambda k: (0, 0))],
        out_specs=pl.BlockSpec((chunks, depth, features), lambda k: (0, k, 0)),
        out_shape=jax.ShapeDtypeStruct((chunks, count * depth, features), jnp.bfloat16),
        scratch_shapes=[pltpu.VMEM((groups, features), jnp.float32)],
        compiler_params=params(),
        cost_estimate=pl.CostEstimate(
            flops=0, bytes_accessed=4 * chunks * count * depth * features, transcendentals=0
        ),
        name=f"fold_down_{first}",
    )(*[down_code] * chunks, down_scale)


def tiles_of(width):
    return [(low, min(TILE, width - low)) for low in range(0, width, TILE)]


def gate_up_kernel(parts, peers, pieces, chunk, *refs):
    token_refs = refs[:parts]
    code_refs = refs[parts : parts + 2]
    scale_refs = refs[parts + 2 : parts + 4]
    keep_ref, send_ref, rows_ref, codes_ref, terms_ref, arrived, done, left = refs[parts + 4 :]
    part = token_refs[0].shape[0]
    half, _, share, width = keep_ref.shape
    tiles = [(side, low, size) for side in range(2) for low, size in tiles_of(width)]

    def fetch(index):
        side, low, size = tiles[index]
        return pltpu.make_async_copy(
            code_refs[side].at[:, pl.ds(chunk * width + low, size)],
            codes_ref.at[side, :, pl.ds(low, size)],
            done.at[index],
        )

    def leave(index, which):
        side, low, size = tiles[index]
        return pltpu.make_async_copy(
            terms_ref.at[pl.ds(which * half, half), side, :, pl.ds(low, size)],
            (keep_ref, send_ref)[which].at[:, side, :, pl.ds(low, size)],
            left.at[index, which],
        )

    place = lax.axis_index("tensor")
    own = lax.axis_index("dp")
    piece_bits = bits_of(pieces)
    unit = min(part, share)
    fetch(0).start()
    placed = []
    for hop in range(peers):
        base = lax.rem(place + peers - hop, peers) * part
        for low in range(0, part, unit):
            row = base + low
            mixed = (row // share) ^ own
            piece = sum((mixed >> bit & 1) << (piece_bits - 1 - bit) for bit in range(piece_bits))
            slot = pl.multiple_of(piece * share + lax.rem(row, share), unit)

            def put(index, low=low, slot=slot, number=len(placed)):
                return pltpu.make_async_copy(
                    token_refs[index].at[pl.ds(low, unit), :],
                    rows_ref.at[pl.ds(slot, unit), :],
                    arrived.at[number],
                )

            placed.append(put(hop))
            if parts > peers and hop == peers // 2:
                pl.when(place < peers // 2)(put(hop).start)
                pl.when(place >= peers // 2)(put(parts - 1).start)
            else:
                put(hop).start()
    for index in range(1, min(AHEAD, len(tiles))):
        fetch(index).start()
    for copy in placed:
        copy.wait()

    for index, (side, low, size) in enumerate(tiles):
        if index + AHEAD < len(tiles):
            fetch(index + AHEAD).start()
        fetch(index).wait()
        cols = slice(low, low + size)
        weight = scaled(codes_ref[side, :, cols], scale_refs[side][:, cols].astype(jnp.float32))
        terms = jnp.dot(rows_ref[...], weight, preferred_element_type=jnp.float32).astype(jnp.bfloat16)
        for piece in range(pieces):
            terms_ref[piece, side, :, cols] = terms[piece * share : (piece + 1) * share]
        for which in range(2):
            leave(index, which).start()
    for index in range(len(tiles)):
        for which in range(2):
            leave(index, which).wait()


def gate_up(token_parts, gate_code, up_code, gate_scale, up_scale, chunk, width):
    peers = lax.axis_size("tensor")
    pieces = lax.axis_size("dp")
    part, features = token_parts[0].shape
    row_count = part * peers
    share = row_count // pieces
    groups = gate_scale.shape[0]
    count = 2 * len(tiles_of(width))
    out = jax.ShapeDtypeStruct((pieces // 2, 2, share, width), jnp.bfloat16)
    anywhere = pl.BlockSpec(memory_space=pl.ANY)
    return pl.pallas_call(
        functools.partial(gate_up_kernel, len(token_parts), peers, pieces, chunk),
        grid=(1,),
        in_specs=[anywhere] * (len(token_parts) + 2) + [pl.BlockSpec((groups, width), lambda k: (0, chunk))] * 2,
        out_specs=[anywhere, anywhere],
        out_shape=[out, out],
        scratch_shapes=[
            pltpu.VMEM((row_count, features), jnp.bfloat16),
            pltpu.VMEM((2, features, width), jnp.bfloat16),
            pltpu.VMEM((pieces, 2, share, width), jnp.bfloat16),
            pltpu.SemaphoreType.DMA((row_count // min(part, share),)),
            pltpu.SemaphoreType.DMA((count,)),
            pltpu.SemaphoreType.DMA((count, 2)),
        ],
        compiler_params=params(),
        cost_estimate=pl.CostEstimate(
            flops=4 * row_count * features * width, bytes_accessed=4 * features * width, transcendentals=0
        ),
        name=f"gate_up_{chunk}",
    )(*token_parts, gate_code, up_code, gate_scale, up_scale)


def hidden_kernel(count, *refs):
    sign_ref, rotation_ref, out_ref = refs[count:]
    total = sum(ref[0].astype(jnp.float32) for ref in refs[:count])
    gate, up = total[0], total[1]
    hidden = gate / (1.0 + jnp.exp(-gate)) * up * sign_ref[0]
    share, width = out_ref.shape
    small = rotation_ref.shape[0]
    slices = butterflies(hidden[:, low : low + small] for low in range(0, width, small))
    stacked = jnp.concatenate(slices, axis=0).astype(jnp.bfloat16)
    turned = jnp.dot(stacked, rotation_ref[...], preferred_element_type=jnp.float32) * POW**-0.5
    turned = [turned[index * share : (index + 1) * share] for index in range(len(slices))]
    out_ref[...] = jnp.concatenate(turned, axis=1).astype(jnp.bfloat16)


def hidden_of(terms, signs, rotation, chunk):
    _, _, share, width = terms[0].shape
    small = rotation.shape[0]
    return pl.pallas_call(
        functools.partial(hidden_kernel, len(terms)),
        grid=(1,),
        in_specs=[pl.BlockSpec((1, 2, share, width), lambda k: (0, 0, 0, 0))] * len(terms)
        + [pl.BlockSpec((1, 1, width), lambda k: (chunk, 0, 0)), pl.BlockSpec((small, small), lambda k: (0, 0))],
        out_specs=pl.BlockSpec((share, width), lambda k: (0, 0)),
        out_shape=jax.ShapeDtypeStruct((share, width), jnp.bfloat16),
        compiler_params=params(),
        cost_estimate=pl.CostEstimate(
            flops=2 * share * width * small, bytes_accessed=2 * share * width * 7, transcendentals=share * width
        ),
        name=f"hidden_{chunk}",
    )(*terms, signs, rotation)


def down_kernel(chunks, pieces, peers, sums, weights, *refs):
    part_refs = refs[: chunks * pieces]
    weight_refs = refs[chunks * pieces : chunks * (pieces + weights)]
    sum_refs = refs[chunks * (pieces + weights) : chunks * (pieces + weights) + sums]
    out_ref, rows_ref = refs[chunks * (pieces + weights) + sums :]
    share = part_refs[0].shape[0]
    row_count = share * pieces

    @pl.when(pl.program_id(0) == 0)
    def _():
        own = lax.axis_index("dp")
        place = lax.axis_index("tensor")
        part = row_count // peers
        for piece in range(pieces):
            block = own ^ reversed_bits(piece, bits_of(pieces))
            row = block * share
            turn = lax.rem(place + 2 * peers - 1 - row // part, peers)
            row = pl.multiple_of(turn * part + lax.rem(row, part), share)
            for chunk in range(chunks):
                rows_ref[chunk, pl.ds(row, share), :] = part_refs[chunk * pieces + piece][...]

    total = None
    for chunk in range(chunks):
        low = 0
        for weight_ref in weight_refs[chunk * weights : (chunk + 1) * weights]:
            high = low + weight_ref.shape[1]
            term = jnp.dot(rows_ref[chunk, :, low:high], weight_ref[0], preferred_element_type=jnp.float32)
            total = term if total is None else total + term
            low = high
    total = total.reshape(out_ref.shape)
    for sum_ref in sum_refs:
        total = total + sum_ref[...]
    out_ref[...] = total.astype(out_ref.dtype)


def down(parts, weights, sums, chunk, column, columns, tile, kind):
    peers = lax.axis_size("tensor")
    chunks, pieces = len(parts), len(parts[0])
    share, width = parts[0][0].shape
    row_count = share * pieces
    part = row_count // peers
    start = column * columns // tile

    def weight_spec(weight, index):
        return pl.BlockSpec((1, weight.shape[1], tile), lambda k: (index, 0, start + k))

    return pl.pallas_call(
        functools.partial(down_kernel, chunks, pieces, peers, len(sums), len(weights)),
        grid=(columns // tile,),
        in_specs=[pl.BlockSpec((share, width), lambda k: (0, 0))] * (chunks * pieces)
        + [weight_spec(weight, chunk + index) for index in range(chunks) for weight in weights]
        + [pl.BlockSpec((peers, part, tile), lambda k: (0, 0, start + k))] * len(sums),
        out_specs=pl.BlockSpec((peers, part, tile), lambda k: (0, 0, k)),
        out_shape=jax.ShapeDtypeStruct((peers, part, columns), kind),
        scratch_shapes=[pltpu.VMEM((chunks, row_count, width), jnp.bfloat16)],
        compiler_params=params(),
        cost_estimate=pl.CostEstimate(
            flops=2 * row_count * chunks * width * columns,
            bytes_accessed=2 * chunks * width * columns,
            transcendentals=0,
        ),
        name=f"down_{chunk}_{column}",
    )(*[piece for row in parts for piece in row], *weights * chunks, *sums)


def add(*terms):
    return sum(term.astype(jnp.float32) for term in terms).astype(jnp.bfloat16)


class Order:
    def __init__(self):
        self.last = None

    def __call__(self, step, operands):
        if self.last is not None:
            operands, _ = lax.optimization_barrier((operands, self.last))
        result = step(operands)
        self.last = jax.tree.leaves(result)[0]
        return result

    def land(self, value):
        value, self.last = lax.optimization_barrier((value, self.last))
        return value


def upper(terms):
    half = terms[0].shape[0] // 2
    return add(*[term[half : 2 * half] for term in terms])


def lower(terms):
    half = terms[0].shape[0] // 2
    return [term[:half] for term in terms] if half > 1 else terms


def doubled(hidden, axis):
    parts = [hidden]
    for bit in reversed(range(bits_of(lax.axis_size(axis)))):
        parts = parts + [swap(part, axis, bit) for part in parts]
    return parts


def on_device(tokens, gate_code, up_code, down_code, gate_scale, up_scale, down_scale, sign_bits):
    peers = lax.axis_size("tensor")
    dp_bits = bits_of(lax.axis_size("dp"))
    turns = bits_of(peers)
    width = LOW * FACTOR
    chunks = gate_code.shape[1] // width
    rotation = jnp.asarray(matrix_part())
    signs = (2.0 * sign_bits.astype(jnp.float32) - 1.0).reshape(chunks, 1, width)
    place = lax.axis_index("tensor")
    features = down_code.shape[1]
    blocks = down_scale.shape[0] // chunks
    order = Order()
    weights = []
    all_terms = {}
    hiddens = {}
    parts = {}

    def fold(count):
        first = sum(weight.shape[1] for weight in weights) * chunks * down_scale.shape[0] // down_code.shape[0]
        first //= chunks
        weights.append(order(lambda codes: folded(codes, down_scale, chunks, first, count), down_code))

    def start_terms(chunk):
        keep, send = order(
            lambda ts: gate_up(ts, gate_code, up_code, gate_scale, up_scale, chunk, width), token_parts
        )
        all_terms[chunk] = [keep, swap(send, "dp", 0)]

    def pass_terms(chunk, bit=1):
        terms = all_terms[chunk]
        send = order(upper, terms)
        all_terms[chunk] = lower(terms) + [swap(send, "dp", bit)]

    def finish_terms(chunk):
        hidden = order(lambda ts: hidden_of(ts, signs, rotation, chunk), all_terms[chunk])
        hiddens[chunk] = hidden, swap(hidden, "tensor", 0)

    def turn(chunk, bit):
        sign = (1 - 2 * (place >> bit & 1)).astype(jnp.float32)
        hidden = order(lambda pair: add(pair[1], sign * pair[0].astype(jnp.float32)), hiddens[chunk])
        if bit + 1 < turns:
            hiddens[chunk] = hidden, swap(hidden, "tensor", bit + 1)
        else:
            parts[chunk] = doubled(hidden, "dp")

    def product(first, count, sums, column, columns, kind):
        given = [parts[chunk] for chunk in range(first, first + count)]
        tile = min(columns, 512)
        return order(lambda ps: down(ps, weights, sums, first, column, columns, tile, kind), given)

    def finish(first, count, sums, halves=2):
        columns = features // halves
        terms, totals = [], []
        for column in range(halves):
            terms.append(product(first, count, sums, column, columns, jnp.bfloat16))
            totals.append(shift(terms[-1][0], "tensor"))
        for hop in range(1, peers):
            for column in range(halves):
                totals[column] = order(lambda pair: add(*pair), (totals[column], terms[column][hop]))
                if hop < peers - 1:
                    totals[column] = shift(totals[column], "tensor")
        return jnp.concatenate(totals, axis=1)

    if peers == 4:
        before = shift(tokens, "tensor")
        behind = shift(tokens, "tensor", -1)
        fold(blocks // 3)
        before, behind, weights[0] = lax.optimization_barrier((before, behind, weights[0]))
        far_low = lax.ppermute(behind, "tensor", [(1, 0), (2, 1)])
        far_high = lax.ppermute(before, "tensor", [(1, 2), (2, 3)])
        token_parts = [tokens, before, far_low, behind, far_high]
        fold(blocks // 3)
    else:
        token_parts = [tokens]
        for _ in range(peers - 1):
            token_parts.append(shift(token_parts[-1], "tensor"))
    rest = blocks - sum(weight.shape[1] for weight in weights) * down_scale.shape[0] // down_code.shape[0]

    def land_terms(chunk):
        all_terms[chunk][-1] = order.land(all_terms[chunk][-1])

    def land_turn(chunk):
        hidden, partner = hiddens[chunk]
        hiddens[chunk] = hidden, order.land(partner)

    def land_parts(chunk):
        parts[chunk][1:] = order.land(parts[chunk][1:])

    if chunks == 4 and dp_bits == 2 and turns == 2:
        start_terms(0)
        start_terms(1)
        land_terms(0)
        pass_terms(0)
        start_terms(2)
        land_terms(0)
        land_terms(1)
        pass_terms(1)
        finish_terms(0)
        start_terms(3)
        land_turn(0)
        land_terms(1)
        land_terms(2)
        pass_terms(2)
        turn(0, 0)
        finish_terms(1)
        land_terms(3)
        pass_terms(3)
        fold(rest // 2)
        land_turn(1)
        turn(1, 0)
        land_terms(2)
        finish_terms(2)
        land_turn(0)
        turn(0, 1)
        fold(rest - rest // 2)
        land_turn(2)
        land_terms(3)
        finish_terms(3)
        turn(2, 0)
        land_turn(1)
        turn(1, 1)
        land_turn(3)
        turn(3, 0)
        land_parts(0)
        land_parts(1)
        sums = [product(0, 2, [], 0, features, jnp.float32)]
        land_turn(2)
        turn(2, 1)
        land_turn(3)
        turn(3, 1)
        land_parts(2)
        sums = [product(2, 1, sums, 0, features, jnp.float32)]
        return finish(3, 1, sums)
    fold(rest)
    for chunk in range(chunks):
        start_terms(chunk)
        for bit in range(1, dp_bits):
            pass_terms(chunk, bit)
        finish_terms(chunk)
        for bit in range(turns):
            turn(chunk, bit)
    return finish(0, chunks, [])


def solution(mesh):
    in_specs = (
        P(("groups", "tensor"), "dp"),
        P("dp", "tensor"),
        P("dp", "tensor"),
        P("tensor", "dp"),
        P("dp", "tensor"),
        P("dp", "tensor"),
        P("tensor", "dp"),
        P("tensor"),
    )
    out_specs = P(("groups", "tensor"), "dp")
    return jax.shard_map(
        on_device, mesh=mesh, in_specs=in_specs, out_specs=out_specs, check_vma=False
    )
```

time: 218 us -> 196 us (0.90)
  waiting for transfers between devices: 105 us -> 42.2 us
  Pallas kernels: 78.3 us -> 107 us
  starting transfers between devices: 20.8 us -> 30.4 us
  local copies, waits for them, and re-layouts: 4.04 us -> 10.7 us
  other arithmetic: 9.65 us -> 4.19 us
    ppermute x28, waiting for transfers between devices: 58.6 us -> 19.6 us  [swap(): lax.ppermute(shard, axis, [(i, i ^ 1 << bit) for i in range(lax.axis_size...]
    pallas_call x10 -> x16, Pallas kernels: 78.3 us -> 107 us  [the longest x4 40.9 us: gate_up(): pl.pallas_call(functools.partial(gate_up_kernel, len(token_parts), peers,...]
    ppermute x9 -> x10, waiting for transfers between devices: 45.9 us -> 22.6 us  [the longest x8 22.6 us: shift(): lax.ppermute(shard, axis, [(i, (i + step) % size) for i in range(size)])]
    unnamed x56 -> x70, local copies, waits for them, and re-layouts: 1.52 us -> 7.87 us
    ppermute x28, starting transfers between devices: 14.9 us -> 20.7 us  [swap(): lax.ppermute(shard, axis, [(i, i ^ 1 << bit) for i in range(lax.axis_size...]
    convert_element_type x8 -> x0, other arithmetic: 4.27 us -> none  [rotated_over(): (partner.astype(jnp.float32) + sign * hidden.astype(jnp.float32)).astype(...]
    ppermute x9 -> x10, starting transfers between devices: 5.91 us -> 9.66 us  [the longest x8 7.7 us: shift(): lax.ppermute(shard, axis, [(i, (i + step) % size) for i in range(size)])]
    convert_element_type x10 -> x18, other arithmetic: 4.65 us -> 3.46 us  [add(): sum((term.astype(jnp.float32) for term in terms)).astype(jnp.bfloat16)]
  transfers between devices with their start and end apart: 37 -> 38, of which waited for: 21 -> 14; matrix products, arithmetic and copies ran while one was open for 4% -> 3% of each run, Pallas kernels for 27% -> 48%
where the time goes in v2:
time: 196 us; the launch traced here: 195 us
  Pallas kernels  107 us (55%)
  waiting for transfers between devices  42.2 us (22%)
  starting transfers between devices  30.4 us (16%)
  local copies, waits for them, and re-layouts  10.7 us (5%)
  other arithmetic  4.19 us (2%)
    pallas_call x4, Pallas kernels, gate_up(): pl.pallas_call(functools.partial(gate_up_kernel, len(token_parts), peers,...  40.9 us
    pallas_call x4, Pallas kernels, folded(): pl.pallas_call(functools.partial(fold_kernel, chunks, blocks, first), gri...  30.3 us
    pallas_call x4, Pallas kernels, down(): pl.pallas_call(functools.partial(down_kernel, chunks, pieces, peers, len(...  25.2 us
    ppermute x8, waiting for transfers between devices, shift(): lax.ppermute(shard, axis, [(i, (i + step) % size) for i in range(size)])  22.6 us
    ppermute x28, starting transfers between devices, swap(): lax.ppermute(shard, axis, [(i, i ^ 1 << bit) for i in range(lax.axis_size...  20.7 us
    ppermute x28, waiting for transfers between devices, swap(): lax.ppermute(shard, axis, [(i, i ^ 1 << bit) for i in range(lax.axis_size...  19.6 us
    pallas_call x4, Pallas kernels, hidden_of(): pl.pallas_call(functools.partial(hidden_kernel, len(terms)), grid=(1,), i...  10.9 us
    unnamed x70, local copies, waits for them, and re-layouts  7.87 us
  transfers between devices with their start and end apart: 38, of which 14 were waited for; matrix products, arithmetic and copies ran while one was open for 3% of the time, Pallas kernels for 48%

profile of v2, /device:TPU:0, one launch (start us, length us, event | category | flops | bytes accessed | tf_op | source)
XLA Modules:
  0.0 195.4 jit_solution(440620943394879704)
XLA Ops:
  0.0 3.0 %collective-permute-start = (bf16[64,2048]{1,0:T(8,128)(2,1)}, bf16[64,2048]{1,0:T(8,128)(2,1)S(1)}, u32[]{:S(2)}, u32[]{:S(2)}) collective-permute-start(bf16[64,2048]{1,0:T(8,128)(2,1)} %refs_0_.6), channel_id=1, source_target_pairs={{0,4},{4,8},{8,12},{12,0},{1,5},{5,9},{9,13},{13,1},{2,6},{6,10},{... | collective-permute-start | bytes 786440 | tf_op jit(solution)/shard_map/ppermute | solution.py:30
  3.0 2.0 %collective-permute-start.1 = (bf16[64,2048]{1,0:T(8,128)(2,1)}, bf16[64,2048]{1,0:T(8,128)(2,1)S(1)}, u32[]{:S(2)}, u32[]{:S(2)}) collective-permute-start(bf16[64,2048]{1,0:T(8,128)(2,1)} %refs_0_.6), channel_id=1, source_target_pairs={{0,12},{4,0},{8,4},{12,8},{1,13},{5,1},{9,5},{13,9},{2,14},{6,2},{... | collective-permute-start | bytes 786440 | tf_op jit(solution)/shard_map/ppermute | solution.py:30
  5.1 8.8 %fold_down_0.1.refs_8_.refs_12_.refs_4_ = bf16[4,512,2048]{2,1,0:T(8,128)(2,1)} custom-call(bf16[6656,2048]{1,0:T(8,128)(2,1)} %refs_3_.4, bf16[6656,2048]{1,0:T(8,128)(2,1)} %refs_3_.4, bf16[6656,2048]{1,0:T(8,128)(2,1)} %refs_3_.4, bf16[6656,2048]{1,0:T(8,128)(2,1)} %refs_3_.4, bf16[52,2048]{1,0:T(8,128)(2,1)} %refs_4_.11), custom_call_target="tpu_custom_call" | custom-call | bytes 16777216 | tf_op jit(solution)/shard_map/fold_down_0/pallas_call | solution.py:94
  13.8 2.8 %collective-permute-done.1.refs_3_ = bf16[64,2048]{1,0:T(8,128)(2,1)S(1)} collective-permute-done((bf16[64,2048]{1,0:T(8,128)(2,1)}, bf16[64,2048]{1,0:T(8,128)(2,1)S(1)}, u32[]{:S(2)}, u32[]{:S(2)}) %collective-permute-start.1) | collective-permute-done | bytes 262176 | tf_op jit(solution)/shard_map/ppermute | solution.py:30
  16.6 1.3 collective-permute-start.2
  17.9 0.7 collective-permute-start.3
  18.6 8.8 %fold_down_4.1.refs_9_.refs_13_.refs_5_ = bf16[4,512,2048]{2,1,0:T(8,128)(2,1)} custom-call(bf16[6656,2048]{1,0:T(8,128)(2,1)} %refs_3_.4, bf16[6656,2048]{1,0:T(8,128)(2,1)} %refs_3_.4, bf16[6656,2048]{1,0:T(8,128)(2,1)} %refs_3_.4, bf16[6656,2048]{1,0:T(8,128)(2,1)} %refs_3_.4, bf16[52,2048]{1,0:T(8,128)(2,1)} %refs_4_.11), custom_call_target="tpu_custom_call" | custom-call | bytes 16777216 | tf_op jit(solution)/shard_map/fold_down_4/pallas_call | solution.py:94
  27.4 0.7 copy-done.2
  28.1 0.7 copy-done.3
  28.8 10.2 %gate_up_0.1 = (bf16[2,2,64,1664]{3,2,1,0:T(8,128)(2,1)}, bf16[2,2,64,1664]{3,2,1,0:T(8,128)(2,1)}) custom-call(bf16[64,2048]{1,0:T(8,128)(2,1)} %refs_0_.6, bf16[64,2048]{1,0:T(8,128)(2,1)} %copy-done, bf16[64,2048]{1,0:T(8,128)(2,1)} %copy-done.2, bf16[64,2048]{1,0:T(8,128)(2,1)} %copy-done.1, bf16[64,2048]{1,0:T(8,128)(2,1)} %copy-done.3, ...), custom_call_target="tpu_custom_call" | custom-call | flops 3489660928 | bytes 13631488 | tf_op jit(solution)/shard_map/gate_up_0/pallas_call | solution.py:197
  39.1 10.2 %gate_up_1.1 = (bf16[2,2,64,1664]{3,2,1,0:T(8,128)(2,1)}, bf16[2,2,64,1664]{3,2,1,0:T(8,128)(2,1)}) custom-call(bf16[64,2048]{1,0:T(8,128)(2,1)} %refs_0_.6, bf16[64,2048]{1,0:T(8,128)(2,1)} %copy-done, bf16[64,2048]{1,0:T(8,128)(2,1)} %copy-done.2, bf16[64,2048]{1,0:T(8,128)(2,1)} %copy-done.1, bf16[64,2048]{1,0:T(8,128)(2,1)} %copy-done.3, ...), custom_call_target="tpu_custom_call" | custom-call | flops 3489660928 | bytes 13631488 | tf_op jit(solution)/shard_map/gate_up_1/pallas_call | solution.py:197
  49.3 0.6 collective-permute-start.6
  50.0 1.5 collective-permute-start.5
  51.6 10.3 %gate_up_2.1 = (bf16[2,2,64,1664]{3,2,1,0:T(8,128)(2,1)}, bf16[2,2,64,1664]{3,2,1,0:T(8,128)(2,1)}) custom-call(bf16[64,2048]{1,0:T(8,128)(2,1)} %refs_0_.6, bf16[64,2048]{1,0:T(8,128)(2,1)} %copy-done, bf16[64,2048]{1,0:T(8,128)(2,1)} %copy-done.2, bf16[64,2048]{1,0:T(8,128)(2,1)} %copy-done.1, bf16[64,2048]{1,0:T(8,128)(2,1)} %copy-done.3, ...), custom_call_target="tpu_custom_call" | custom-call | flops 3489660928 | bytes 13631488 | tf_op jit(solution)/shard_map/gate_up_2/pallas_call | solution.py:197
  62.1 0.6 collective-permute-start.8
  62.8 0.6 reshape.3.refs_3_
  63.4 0.7 copy-done.22
  64.1 2.7 %hidden_0.1 = bf16[64,1664]{1,0:T(8,128)(2,1)} custom-call(bf16[2,2,64,1664]{3,2,1,0:T(8,128)(2,1)} %get-tuple-element.157.refs_0_, bf16[2,2,64,1664]{3,2,1,0:T(8,128)(2,1)} %copy-done.11, bf16[1,2,64,1664]{3,2,1,0:T(8,128)(2,1)} %copy-done.22, f32[4,1,1664]{2,1,0:T(1,128)} %reshape.3.refs_3_, bf16[208,208]{1,0:T(8,128)(2,1)} %constant.18.clone.refs_4_), custom_call_target="tpu_custom_call" | custom-call | flops 44302336 | bytes 1490944 | tf_op jit(solution)/shard_map/hidden_0/pallas_call | solution.py:236
  66.9 5.0 %collective-permute-start.9 = (bf16[64,1664]{1,0:T(8,128)(2,1)}, bf16[64,1664]{1,0:T(8,128)(2,1)S(1)}, u32[]{:S(2)}, u32[]{:S(2)}) collective-permute-start(bf16[64,1664]{1,0:T(8,128)(2,1)} %hidden_0.1), channel_id=1, source_target_pairs={{0,4},{4,0},{8,12},{12,8},{1,5},{5,1},{9,13},{13,9},{2,6},{6,2},{1... | collective-permute-start | bytes 638984 | tf_op jit(solution)/shard_map/ppermute | solution.py:25
  71.9 10.1 %gate_up_3.1 = (bf16[2,2,64,1664]{3,2,1,0:T(8,128)(2,1)}, bf16[2,2,64,1664]{3,2,1,0:T(8,128)(2,1)}) custom-call(bf16[64,2048]{1,0:T(8,128)(2,1)} %refs_0_.6, bf16[64,2048]{1,0:T(8,128)(2,1)} %copy-done, bf16[64,2048]{1,0:T(8,128)(2,1)} %copy-done.2, bf16[64,2048]{1,0:T(8,128)(2,1)} %copy-done.1, bf16[64,2048]{1,0:T(8,128)(2,1)} %copy-done.3, ...), custom_call_target="tpu_custom_call" | custom-call | flops 3489660928 | bytes 13631488 | tf_op jit(solution)/shard_map/gate_up_3/pallas_call | solution.py:197
  82.3 1.5 collective-permute-start.15
  84.0 2.7 %hidden_1.1 = bf16[64,1664]{1,0:T(8,128)(2,1)} custom-call(bf16[2,2,64,1664]{3,2,1,0:T(8,128)(2,1)} %get-tuple-element.173.refs_0_, bf16[2,2,64,1664]{3,2,1,0:T(8,128)(2,1)} %copy-done.8, bf16[1,2,64,1664]{3,2,1,0:T(8,128)(2,1)} %copy-done.21, f32[4,1,1664]{2,1,0:T(1,128)} %reshape.3.refs_3_, bf16[208,208]{1,0:T(8,128)(2,1)} %constant.18.clone.refs_4_), custom_call_target="tpu_custom_call" | custom-call | flops 44302336 | bytes 1490944 | tf_op jit(solution)/shard_map/hidden_1/pallas_call | solution.py:236
  86.7 1.4 collective-permute-start.13
  88.1 1.4 add_convert_fusion
  89.5 0.6 collective-permute-start.11
  90.1 4.9 %fold_down_8.1.refs_10_.refs_14_.refs_6_ = bf16[4,256,2048]{2,1,0:T(8,128)(2,1)} custom-call(bf16[6656,2048]{1,0:T(8,128)(2,1)} %refs_3_.4, bf16[6656,2048]{1,0:T(8,128)(2,1)} %refs_3_.4, bf16[6656,2048]{1,0:T(8,128)(2,1)} %refs_3_.4, bf16[6656,2048]{1,0:T(8,128)(2,1)} %refs_3_.4, bf16[52,2048]{1,0:T(8,128)(2,1)} %refs_4_.11), custom_call_target="tpu_custom_call" | custom-call | bytes 8388608 | tf_op jit(solution)/shard_map/fold_down_8/pallas_call | solution.py:94
  95.1 3.7 %collective-permute-done.13 = bf16[64,1664]{1,0:T(8,128)(2,1)S(1)} collective-permute-done((bf16[64,1664]{1,0:T(8,128)(2,1)}, bf16[64,1664]{1,0:T(8,128)(2,1)S(1)}, u32[]{:S(2)}, u32[]{:S(2)}) %collective-permute-start.13) | collective-permute-done | bytes 213024 | tf_op jit(solution)/shard_map/ppermute | solution.py:25
  99.1 0.8 copy-done.24
  99.8 2.7 %hidden_2.1 = bf16[64,1664]{1,0:T(8,128)(2,1)} custom-call(bf16[2,2,64,1664]{3,2,1,0:T(8,128)(2,1)} %get-tuple-element.187.refs_0_, bf16[2,2,64,1664]{3,2,1,0:T(8,128)(2,1)} %copy-done.6, bf16[1,2,64,1664]{3,2,1,0:T(8,128)(2,1)} %copy-done.24, f32[4,1,1664]{2,1,0:T(1,128)} %reshape.3.refs_3_, bf16[208,208]{1,0:T(8,128)(2,1)} %constant.18.clone.refs_4_), custom_call_target="tpu_custom_call" | custom-call | flops 44302336 | bytes 1490944 | tf_op jit(solution)/shard_map/hidden_2/pallas_call | solution.py:236
  102.6 2.4 %collective-permute-start.16 = (bf16[64,1664]{1,0:T(8,128)(2,1)}, bf16[64,1664]{1,0:T(8,128)(2,1)S(1)}, u32[]{:S(2)}, u32[]{:S(2)}) collective-permute-start(bf16[64,1664]{1,0:T(8,128)(2,1)} %hidden_2.1), channel_id=1, source_target_pairs={{0,4},{4,0},{8,12},{12,8},{1,5},{5,1},{9,13},{13,9},{2,6},{6,2},{1... | collective-permute-start | bytes 638984 | tf_op jit(solution)/shard_map/ppermute | solution.py:25
  105.0 0.6 collective-permute-start.20
  105.6 7.8 %fold_down_10.1.refs_11_.refs_15_.refs_7_ = bf16[4,384,2048]{2,1,0:T(8,128)(2,1)} custom-call(bf16[6656,2048]{1,0:T(8,128)(2,1)} %refs_3_.4, bf16[6656,2048]{1,0:T(8,128)(2,1)} %refs_3_.4, bf16[6656,2048]{1,0:T(8,128)(2,1)} %refs_3_.4, bf16[6656,2048]{1,0:T(8,128)(2,1)} %refs_3_.4, bf16[52,2048]{1,0:T(8,128)(2,1)} %refs_4_.11), custom_call_target="tpu_custom_call" | custom-call | bytes 12582912 | tf_op jit(solution)/shard_map/fold_down_10/pallas_call | solution.py:94
  113.9 0.8 copy-done.23
  114.6 2.7 %hidden_3.1 = bf16[64,1664]{1,0:T(8,128)(2,1)} custom-call(bf16[2,2,64,1664]{3,2,1,0:T(8,128)(2,1)} %get-tuple-element.179.refs_0_, bf16[2,2,64,1664]{3,2,1,0:T(8,128)(2,1)} %copy-done.9, bf16[1,2,64,1664]{3,2,1,0:T(8,128)(2,1)} %copy-done.23, f32[4,1,1664]{2,1,0:T(1,128)} %reshape.3.refs_3_, bf16[208,208]{1,0:T(8,128)(2,1)} %constant.18.clone.refs_4_), custom_call_target="tpu_custom_call" | custom-call | flops 44302336 | bytes 1490944 | tf_op jit(solution)/shard_map/hidden_3/pallas_call | solution.py:236
  117.5 1.2 collective-permute-start.23
  119.3 4.7 %collective-permute-done.12 = bf16[64,1664]{1,0:T(8,128)(2,1)S(1)} collective-permute-done((bf16[64,1664]{1,0:T(8,128)(2,1)}, bf16[64,1664]{1,0:T(8,128)(2,1)S(1)}, u32[]{:S(2)}, u32[]{:S(2)}) %collective-permute-start.12) | collective-permute-done | bytes 213024 | tf_op jit(solution)/shard_map/ppermute | solution.py:25
  124.0 0.9 collective-permute-start.19
  124.9 1.1 add_convert_fusion.6
  126.0 2.1 %collective-permute-start.18 = (bf16[64,1664]{1,0:T(8,128)(2,1)S(1)}, bf16[64,1664]{1,0:T(8,128)(2,1)S(1)}, u32[]{:S(2)}, u32[]{:S(2)}) collective-permute-start(bf16[64,1664]{1,0:T(8,128)(2,1)S(1)} %add_convert_fusion.6), channel_id=1, source_target_pairs={{0,8},{4,12},{8,0},{12,4},{1,9},{5,13},{9,1},{13,5},{2,10},{6,14},... | collective-permute-start | bytes 638984 | tf_op jit(solution)/shard_map/ppermute | solution.py:25
  128.1 0.6 copy-done.28
  128.9 0.7 copy-done.30
  129.5 9.6 %down_0_0.1.refs_8_ = f32[4,64,2048]{2,1,0:T(8,128)} custom-call(bf16[64,1664]{1,0:T(8,128)(2,1)} %copy-done.12, bf16[64,1664]{1,0:T(8,128)(2,1)} %copy-done.25, bf16[64,1664]{1,0:T(8,128)(2,1)} %copy-done.27, bf16[64,1664]{1,0:T(8,128)(2,1)} %copy-done.28, bf16[64,1664]{1,0:T(8,128)(2,1)} %copy-done.13, bf16[64,1664]{1,0:T(8,128)(2,1)} %copy-done.26, ...), custom_call_target="tpu_custom_call" | custom-call | flops 3489660928 | bytes 13631488 | tf_op jit(solution)/shard_map/down_0_0/pallas_call | solution.py:297
  140.2 3.9 %collective-permute-done.18 = bf16[64,1664]{1,0:T(8,128)(2,1)S(1)} collective-permute-done((bf16[64,1664]{1,0:T(8,128)(2,1)S(1)}, bf16[64,1664]{1,0:T(8,128)(2,1)S(1)}, u32[]{:S(2)}, u32[]{:S(2)}) %collective-permute-start.18) | collective-permute-done | bytes 213024 | tf_op jit(solution)/shard_map/ppermute | solution.py:25
  144.3 2.5 %collective-permute-done.29.refs_1_ = bf16[64,1664]{1,0:T(8,128)(2,1)S(1)} collective-permute-done((bf16[64,1664]{1,0:T(8,128)(2,1)S(1)}, bf16[64,1664]{1,0:T(8,128)(2,1)S(1)}, u32[]{:S(2)}, u32[]{:S(2)}) %collective-permute-start.29) | collective-permute-done | bytes 213024 | tf_op jit(solution)/shard_map/ppermute | solution.py:25
  146.8 0.5 collective-permute-start.27
  147.3 4.1 %collective-permute-done.26.refs_1_ = bf16[64,1664]{1,0:T(8,128)(2,1)S(1)} collective-permute-done((bf16[64,1664]{1,0:T(8,128)(2,1)S(1)}, bf16[64,1664]{1,0:T(8,128)(2,1)S(1)}, u32[]{:S(2)}, u32[]{:S(2)}) %collective-permute-start.26) | collective-permute-done | bytes 213024 | tf_op jit(solution)/shard_map/ppermute | solution.py:25
  151.4 0.7 copy-done.32
  152.1 0.7 copy-done.33
  152.8 7.1 %down_2_0.1.refs_8_ = f32[4,64,2048]{2,1,0:T(8,128)} custom-call(bf16[64,1664]{1,0:T(8,128)(2,1)} %copy-done.17, bf16[64,1664]{1,0:T(8,128)(2,1)} %copy-done.31, bf16[64,1664]{1,0:T(8,128)(2,1)} %copy-done.32, bf16[64,1664]{1,0:T(8,128)(2,1)} %copy-done.33, bf16[4,512,2048]{2,1,0:T(8,128)(2,1)} %fold_down_0.1.refs_8_.refs_12_.refs_4_, ...), custom_call_target="tpu_custom_call" | custom-call | flops 1744830464 | bytes 6815744 | tf_op jit(solution)/shard_map/down_2_0/pallas_call | solution.py:297
  159.9 0.7 copy-done.15
  160.5 0.7 copy-done.16
  161.2 4.2 %down_3_0.1 = bf16[4,64,1024]{2,1,0:T(8,128)(2,1)} custom-call(bf16[64,1664]{1,0:T(8,128)(2,1)} %copy-done.4, bf16[64,1664]{1,0:T(8,128)(2,1)} %copy-done.14, bf16[64,1664]{1,0:T(8,128)(2,1)} %copy-done.15, bf16[64,1664]{1,0:T(8,128)(2,1)} %copy-done.16, bf16[4,512,2048]{2,1,0:T(8,128)(2,1)} %fold_down_0.1.refs_8_.refs_12_.refs_4_, ...), custom_call_target="tpu_custom_call" | custom-call | flops 872415232 | bytes 3407872 | tf_op jit(solution)/shard_map/down_3_0/pallas_call | solution.py:297
  165.4 1.1 slice_bitcast_fusion.2
  166.8 4.2 %down_3_1.1 = bf16[4,64,1024]{2,1,0:T(8,128)(2,1)} custom-call(bf16[64,1664]{1,0:T(8,128)(2,1)} %copy-done.4, bf16[64,1664]{1,0:T(8,128)(2,1)} %copy-done.14, bf16[64,1664]{1,0:T(8,128)(2,1)} %copy-done.15, bf16[64,1664]{1,0:T(8,128)(2,1)} %copy-done.16, bf16[4,512,2048]{2,1,0:T(8,128)(2,1)} %fold_down_0.1.refs_8_.refs_12_.refs_4_, ...), custom_call_target="tpu_custom_call" | custom-call | flops 872415232 | bytes 3407872 | tf_op jit(solution)/shard_map/down_3_1/pallas_call | solution.py:297
  171.0 1.1 slice_bitcast_fusion
  172.1 1.3 collective-permute-start.34
  173.4 0.9 collective-permute-done.32
  174.3 1.0 collective-permute-start.33
  175.4 4.9 %collective-permute-done.34 = bf16[64,1024]{1,0:T(8,128)(2,1)S(1)} collective-permute-done((bf16[64,1024]{1,0:T(8,128)(2,1)S(1)}, bf16[64,1024]{1,0:T(8,128)(2,1)S(1)}, u32[]{:S(2)}, u32[]{:S(2)}) %collective-permute-start.34) | collective-permute-done | bytes 131104 | tf_op jit(solution)/shard_map/ppermute | solution.py:30
  180.4 2.2 %collective-permute-done.33 = bf16[64,1024]{1,0:T(8,128)(2,1)S(1)} collective-permute-done((bf16[64,1024]{1,0:T(8,128)(2,1)S(1)}, bf16[64,1024]{1,0:T(8,128)(2,1)S(1)}, u32[]{:S(2)}, u32[]{:S(2)}) %collective-permute-start.33) | collective-permute-done | bytes 131104 | tf_op jit(solution)/shard_map/ppermute | solution.py:30
  182.7 5.1 %collective-permute-done.36 = bf16[64,1024]{1,0:T(8,128)(2,1)S(1)} collective-permute-done((bf16[64,1024]{1,0:T(8,128)(2,1)S(1)}, bf16[64,1024]{1,0:T(8,128)(2,1)S(1)}, u32[]{:S(2)}, u32[]{:S(2)}) %collective-permute-start.36) | collective-permute-done | bytes 131104 | tf_op jit(solution)/shard_map/ppermute | solution.py:30
  187.8 2.5 %collective-permute-done.35 = bf16[64,1024]{1,0:T(8,128)(2,1)S(1)} collective-permute-done((bf16[64,1024]{1,0:T(8,128)(2,1)S(1)}, bf16[64,1024]{1,0:T(8,128)(2,1)S(1)}, u32[]{:S(2)}, u32[]{:S(2)}) %collective-permute-start.35) | collective-permute-done | bytes 131104 | tf_op jit(solution)/shard_map/ppermute | solution.py:30
  190.4 4.2 %collective-permute-done.37 = bf16[64,1024]{1,0:T(8,128)(2,1)S(1)} collective-permute-done((bf16[64,1024]{1,0:T(8,128)(2,1)S(1)}, bf16[64,1024]{1,0:T(8,128)(2,1)S(1)}, u32[]{:S(2)}, u32[]{:S(2)}) %collective-permute-start.37) | collective-permute-done | bytes 131104 | tf_op jit(solution)/shard_map/ppermute | solution.py:30
  194.6 0.7 pad_maximum_fusion
  (121 shorter events, 4.2 us)
Async XLA Ops:
  0.0 13.8 %collective-permute-start = (bf16[64,2048]{1,0:T(8,128)(2,1)}, bf16[64,2048]{1,0:T(8,128)(2,1)S(1)}, u32[]{:S(2)}, u32[]{:S(2)}) collective-permute-start(bf16[64,2048]{1,0:T(8,128)(2,1)} %refs_0_.6), channel_id=1, source_target_pairs={{0,4},{4,8},{8,12},{12,0},{1,5},{5,9},{9,13},{13,1},{2,6},{6,10},{... | collective-permute-start | bytes 786440 | tf_op jit(solution)/shard_map/ppermute | solution.py:30
  3.0 13.6 %collective-permute-start.1 = (bf16[64,2048]{1,0:T(8,128)(2,1)}, bf16[64,2048]{1,0:T(8,128)(2,1)S(1)}, u32[]{:S(2)}, u32[]{:S(2)}) collective-permute-start(bf16[64,2048]{1,0:T(8,128)(2,1)} %refs_0_.6), channel_id=1, source_target_pairs={{0,12},{4,0},{8,4},{12,8},{1,13},{5,1},{9,5},{13,9},{2,14},{6,2},{... | collective-permute-start | bytes 786440 | tf_op jit(solution)/shard_map/ppermute | solution.py:30
  13.8 13.6 %copy-start = (bf16[64,2048]{1,0:T(8,128)(2,1)}, bf16[64,2048]{1,0:T(8,128)(2,1)S(1)}, u32[]{:S(2)}) copy-start(bf16[64,2048]{1,0:T(8,128)(2,1)S(1)} %collective-permute-done.refs_1_) | copy-start | bytes 786436
  16.6 10.8 %copy-start.1 = (bf16[64,2048]{1,0:T(8,128)(2,1)}, bf16[64,2048]{1,0:T(8,128)(2,1)S(1)}, u32[]{:S(2)}) copy-start(bf16[64,2048]{1,0:T(8,128)(2,1)S(1)} %collective-permute-done.1.refs_3_) | copy-start | bytes 786436
  16.6 10.8 %collective-permute-start.2 = (bf16[64,2048]{1,0:T(8,128)(2,1)S(1)}, bf16[64,2048]{1,0:T(8,128)(2,1)S(1)}, u32[]{:S(2)}, u32[]{:S(2)}) collective-permute-start(bf16[64,2048]{1,0:T(8,128)(2,1)S(1)} %collective-permute-done.1.refs_3_), channel_id=1, source_target_pairs={{4,0},{8,4},{5,1},{9,5},{6,2},{10,6},{7,3},{11,7},{20,16},{24,20},... | collective-permute-start | bytes 786440 | tf_op jit(solution)/shard_map/ppermute | solution.py:421
  17.9 9.5 %collective-permute-start.3 = (bf16[64,2048]{1,0:T(8,128)(2,1)S(1)}, bf16[64,2048]{1,0:T(8,128)(2,1)S(1)}, u32[]{:S(2)}, u32[]{:S(2)}) collective-permute-start(bf16[64,2048]{1,0:T(8,128)(2,1)S(1)} %collective-permute-done.refs_1_), channel_id=1, source_target_pairs={{4,8},{8,12},{5,9},{9,13},{6,10},{10,14},{7,11},{11,15},{20,24},{2... | collective-permute-start | bytes 786440 | tf_op jit(solution)/shard_map/ppermute | solution.py:422
  39.0 10.9 %collective-permute-start.4 = (bf16[2,2,64,1664]{3,2,1,0:T(8,128)(2,1)}, bf16[2,2,64,1664]{3,2,1,0:T(8,128)(2,1)S(1)}, u32[]{:S(2)}, u32[]{:S(2)}) collective-permute-start(bf16[2,2,64,1664]{3,2,1,0:T(8,128)(2,1)} %get-tuple-element.137), channel_id=1, source_target_pairs={{0,1},{1,0},{2,3},{3,2},{4,5},{5,4},{6,7},{7,6},{8,9},{9,8},{10,11... | collective-permute-start | bytes 2555912 | tf_op jit(solution)/shard_map/ppermute | solution.py:25
  39.1 10.8 %copy-start.10 = (bf16[2,2,64,1664]{3,2,1,0:T(8,128)(2,1)S(1)}, bf16[2,2,64,1664]{3,2,1,0:T(8,128)(2,1)}, u32[]{:S(2)}) copy-start(bf16[2,2,64,1664]{3,2,1,0:T(8,128)(2,1)} %get-tuple-element.157.refs_0_) | copy-start | bytes 2555908
  49.3 12.7 %collective-permute-start.6 = (bf16[2,2,64,1664]{3,2,1,0:T(8,128)(2,1)}, bf16[2,2,64,1664]{3,2,1,0:T(8,128)(2,1)S(1)}, u32[]{:S(2)}, u32[]{:S(2)}) collective-permute-start(bf16[2,2,64,1664]{3,2,1,0:T(8,128)(2,1)} %get-tuple-element.154), channel_id=1, source_target_pairs={{0,1},{1,0},{2,3},{3,2},{4,5},{5,4},{6,7},{7,6},{8,9},{9,8},{10,11... | collective-permute-start | bytes 2555912 | tf_op jit(solution)/shard_map/ppermute | solution.py:25
  49.9 12.0 %copy-start.11 = (bf16[2,2,64,1664]{3,2,1,0:T(8,128)(2,1)}, bf16[2,2,64,1664]{3,2,1,0:T(8,128)(2,1)S(1)}, u32[]{:S(2)}) copy-start(bf16[2,2,64,1664]{3,2,1,0:T(8,128)(2,1)S(1)} %collective-permute-done.4.refs_1_) | copy-start | bytes 2555908
  50.0 12.0 %copy-start.7 = (bf16[2,2,64,1664]{3,2,1,0:T(8,128)(2,1)S(1)}, bf16[2,2,64,1664]{3,2,1,0:T(8,128)(2,1)}, u32[]{:S(2)}) copy-start(bf16[2,2,64,1664]{3,2,1,0:T(8,128)(2,1)} %get-tuple-element.173.refs_0_) | copy-start | bytes 2555908
  50.0 12.7 %copy-start.34 = (s32[6656]{0:T(1024)S(1)}, s32[6656]{0:T(1024)}, u32[]{:S(2)}) copy-start(s32[6656]{0:T(1024)} %param.16) | copy-start | bytes 79876
  50.0 13.4 %collective-permute-start.5 = (bf16[1,2,64,1664]{3,2,1,0:T(8,128)(2,1)S(1)}, bf16[1,2,64,1664]{3,2,1,0:T(8,128)(2,1)S(1)}, u32[]{:S(2)}, u32[]{:S(2)}) collective-permute-start(bf16[1,2,64,1664]{3,2,1,0:T(8,128)(2,1)S(1)} %add_convert_fusion.3), channel_id=1, source_target_pairs={{0,2},{1,3},{2,0},{3,1},{4,6},{5,7},{6,4},{7,5},{8,10},{9,11},{10,... | collective-permute-start | bytes 1277960 | tf_op jit(solution)/shard_map/ppermute | solution.py:25
  61.9 20.2 %collective-permute-start.10 = (bf16[2,2,64,1664]{3,2,1,0:T(8,128)(2,1)}, bf16[2,2,64,1664]{3,2,1,0:T(8,128)(2,1)S(1)}, u32[]{:S(2)}, u32[]{:S(2)}) collective-permute-start(bf16[2,2,64,1664]{3,2,1,0:T(8,128)(2,1)} %get-tuple-element.168), channel_id=1, source_target_pairs={{0,1},{1,0},{2,3},{3,2},{4,5},{5,4},{6,7},{7,6},{8,9},{9,8},{10,11... | collective-permute-start | bytes 2555912 | tf_op jit(solution)/shard_map/ppermute | solution.py:25
  62.0 20.0 %copy-start.8 = (bf16[2,2,64,1664]{3,2,1,0:T(8,128)(2,1)}, bf16[2,2,64,1664]{3,2,1,0:T(8,128)(2,1)S(1)}, u32[]{:S(2)}) copy-start(bf16[2,2,64,1664]{3,2,1,0:T(8,128)(2,1)S(1)} %collective-permute-done.6.refs_1_) | copy-start | bytes 2555908
  62.1 20.0 %collective-permute-start.8 = (bf16[1,2,64,1664]{3,2,1,0:T(8,128)(2,1)S(1)}, bf16[1,2,64,1664]{3,2,1,0:T(8,128)(2,1)S(1)}, u32[]{:S(2)}, u32[]{:S(2)}) collective-permute-start(bf16[1,2,64,1664]{3,2,1,0:T(8,128)(2,1)S(1)} %add_convert_fusion.2), channel_id=1, source_target_pairs={{0,2},{1,3},{2,0},{3,1},{4,6},{5,7},{6,4},{7,5},{8,10},{9,11},{10,... | collective-permute-start | bytes 1277960 | tf_op jit(solution)/shard_map/ppermute | solution.py:25
  66.9 15.3 %copy-start.5 = (bf16[2,2,64,1664]{3,2,1,0:T(8,128)(2,1)S(1)}, bf16[2,2,64,1664]{3,2,1,0:T(8,128)(2,1)}, u32[]{:S(2)}) copy-start(bf16[2,2,64,1664]{3,2,1,0:T(8,128)(2,1)} %get-tuple-element.187.refs_0_) | copy-start | bytes 2555908
  66.9 17.0 %copy-start.18 = (bf16[64,1664]{1,0:T(8,128)(2,1)S(1)}, bf16[64,1664]{1,0:T(8,128)(2,1)}, u32[]{:S(2)}) copy-start(bf16[64,1664]{1,0:T(8,128)(2,1)} %hidden_0.1) | copy-start | bytes 638980
  66.9 15.3 %collective-permute-start.9 = (bf16[64,1664]{1,0:T(8,128)(2,1)}, bf16[64,1664]{1,0:T(8,128)(2,1)S(1)}, u32[]{:S(2)}, u32[]{:S(2)}) collective-permute-start(bf16[64,1664]{1,0:T(8,128)(2,1)} %hidden_0.1), channel_id=1, source_target_pairs={{0,4},{4,0},{8,12},{12,8},{1,5},{5,1},{9,13},{13,9},{2,6},{6,2},{1... | collective-permute-start | bytes 638984 | tf_op jit(solution)/shard_map/ppermute | solution.py:25
  82.0 6.1 %collective-permute-start.7 = (bf16[2,2,64,1664]{3,2,1,0:T(8,128)(2,1)}, bf16[2,2,64,1664]{3,2,1,0:T(8,128)(2,1)S(1)}, u32[]{:S(2)}, u32[]{:S(2)}) collective-permute-start(bf16[2,2,64,1664]{3,2,1,0:T(8,128)(2,1)} %get-tuple-element.166), channel_id=1, source_target_pairs={{0,1},{1,0},{2,3},{3,2},{4,5},{5,4},{6,7},{7,6},{8,9},{9,8},{10,11... | collective-permute-start | bytes 2555912 | tf_op jit(solution)/shard_map/ppermute | solution.py:25
  82.1 1.9 copy-start.21
  82.2 12.9 %copy-start.6 = (bf16[2,2,64,1664]{3,2,1,0:T(8,128)(2,1)}, bf16[2,2,64,1664]{3,2,1,0:T(8,128)(2,1)S(1)}, u32[]{:S(2)}) copy-start(bf16[2,2,64,1664]{3,2,1,0:T(8,128)(2,1)S(1)} %collective-permute-done.10.refs_1_) | copy-start | bytes 2555908
  82.3 16.8 %collective-permute-start.15 = (bf16[1,2,64,1664]{3,2,1,0:T(8,128)(2,1)S(1)}, bf16[1,2,64,1664]{3,2,1,0:T(8,128)(2,1)S(1)}, u32[]{:S(2)}, u32[]{:S(2)}) collective-permute-start(bf16[1,2,64,1664]{3,2,1,0:T(8,128)(2,1)S(1)} %add_convert_fusion.1), channel_id=1, source_target_pairs={{0,2},{1,3},{2,0},{3,1},{4,6},{5,7},{6,4},{7,5},{8,10},{9,11},{10,... | collective-permute-start | bytes 1277960 | tf_op jit(solution)/shard_map/ppermute | solution.py:25
  83.9 21.0 %collective-permute-start.17 = (bf16[64,1664]{1,0:T(8,128)(2,1)S(1)}, bf16[64,1664]{1,0:T(8,128)(2,1)S(1)}, u32[]{:S(2)}, u32[]{:S(2)}) collective-permute-start(bf16[64,1664]{1,0:T(8,128)(2,1)S(1)} %add_convert_fusion.11), channel_id=1, source_target_pairs={{0,8},{4,12},{8,0},{12,4},{1,9},{5,13},{9,1},{13,5},{2,10},{6,14},... | collective-permute-start | bytes 638984 | tf_op jit(solution)/shard_map/ppermute | solution.py:25
  86.7 12.0 %collective-permute-start.13 = (bf16[64,1664]{1,0:T(8,128)(2,1)}, bf16[64,1664]{1,0:T(8,128)(2,1)S(1)}, u32[]{:S(2)}, u32[]{:S(2)}) collective-permute-start(bf16[64,1664]{1,0:T(8,128)(2,1)} %hidden_1.1), channel_id=1, source_target_pairs={{0,4},{4,0},{8,12},{12,8},{1,5},{5,1},{9,13},{13,9},{2,6},{6,2},{1... | collective-permute-start | bytes 638984 | tf_op jit(solution)/shard_map/ppermute | solution.py:25
  88.1 6.9 %copy-start.9 = (bf16[2,2,64,1664]{3,2,1,0:T(8,128)(2,1)}, bf16[2,2,64,1664]{3,2,1,0:T(8,128)(2,1)S(1)}, u32[]{:S(2)}) copy-start(bf16[2,2,64,1664]{3,2,1,0:T(8,128)(2,1)S(1)} %collective-permute-done.7.refs_1_) | copy-start | bytes 2555908
  89.5 9.2 %copy-start.20 = (bf16[64,1664]{1,0:T(8,128)(2,1)S(1)}, bf16[64,1664]{1,0:T(8,128)(2,1)}, u32[]{:S(2)}) copy-start(bf16[64,1664]{1,0:T(8,128)(2,1)} %hidden_1.1) | copy-start | bytes 638980
  89.5 24.3 %collective-permute-start.11 = (bf16[1,2,64,1664]{3,2,1,0:T(8,128)(2,1)S(1)}, bf16[1,2,64,1664]{3,2,1,0:T(8,128)(2,1)S(1)}, u32[]{:S(2)}, u32[]{:S(2)}) collective-permute-start(bf16[1,2,64,1664]{3,2,1,0:T(8,128)(2,1)S(1)} %add_convert_fusion), channel_id=1, source_target_pairs={{0,2},{1,3},{2,0},{3,1},{4,6},{5,7},{6,4},{7,5},{8,10},{9,11},{10,... | collective-permute-start | bytes 1277960 | tf_op jit(solution)/shard_map/ppermute | solution.py:25
  98.8 18.6 %collective-permute-start.14 = (bf16[64,1664]{1,0:T(8,128)(2,1)S(1)}, bf16[64,1664]{1,0:T(8,128)(2,1)S(1)}, u32[]{:S(2)}, u32[]{:S(2)}) collective-permute-start(bf16[64,1664]{1,0:T(8,128)(2,1)S(1)} %add_convert_fusion.10), channel_id=1, source_target_pairs={{0,8},{4,12},{8,0},{12,4},{1,9},{5,13},{9,1},{13,5},{2,10},{6,14},... | collective-permute-start | bytes 638984 | tf_op jit(solution)/shard_map/ppermute | solution.py:25
  99.1 0.8 copy-start.24
  102.6 11.3 %collective-permute-start.16 = (bf16[64,1664]{1,0:T(8,128)(2,1)}, bf16[64,1664]{1,0:T(8,128)(2,1)S(1)}, u32[]{:S(2)}, u32[]{:S(2)}) collective-permute-start(bf16[64,1664]{1,0:T(8,128)(2,1)} %hidden_2.1), channel_id=1, source_target_pairs={{0,4},{4,0},{8,12},{12,8},{1,5},{5,1},{9,13},{13,9},{2,6},{6,2},{1... | collective-permute-start | bytes 638984 | tf_op jit(solution)/shard_map/ppermute | solution.py:25
  105.0 13.7 %copy-start.12 = (bf16[64,1664]{1,0:T(8,128)(2,1)}, bf16[64,1664]{1,0:T(8,128)(2,1)S(1)}, u32[]{:S(2)}) copy-start(bf16[64,1664]{1,0:T(8,128)(2,1)S(1)} %add_convert_fusion.9.refs_0_) | copy-start | bytes 638980
  105.0 12.3 %copy-start.19 = (bf16[64,1664]{1,0:T(8,128)(2,1)S(1)}, bf16[64,1664]{1,0:T(8,128)(2,1)}, u32[]{:S(2)}) copy-start(bf16[64,1664]{1,0:T(8,128)(2,1)} %hidden_2.1) | copy-start | bytes 638980
  105.0 13.7 %collective-permute-start.20 = (bf16[64,1664]{1,0:T(8,128)(2,1)S(1)}, bf16[64,1664]{1,0:T(8,128)(2,1)S(1)}, u32[]{:S(2)}, u32[]{:S(2)}) collective-permute-start(bf16[64,1664]{1,0:T(8,128)(2,1)S(1)} %add_convert_fusion.9.refs_0_), channel_id=1, source_target_pairs={{0,2},{1,3},{2,0},{3,1},{4,6},{5,7},{6,4},{7,5},{8,10},{9,11},{10,... | collective-permute-start | bytes 638984 | tf_op jit(solution)/shard_map/ppermute | solution.py:25
  113.9 0.8 copy-start.23
  117.4 6.6 %collective-permute-start.12 = (bf16[64,1664]{1,0:T(8,128)(2,1)}, bf16[64,1664]{1,0:T(8,128)(2,1)S(1)}, u32[]{:S(2)}, u32[]{:S(2)}) collective-permute-start(bf16[64,1664]{1,0:T(8,128)(2,1)} %hidden_3.1), channel_id=1, source_target_pairs={{0,4},{4,0},{8,12},{12,8},{1,5},{5,1},{9,13},{13,9},{2,6},{6,2},{1... | collective-permute-start | bytes 638984 | tf_op jit(solution)/shard_map/ppermute | solution.py:25
  117.5 10.6 %copy-start.13 = (bf16[64,1664]{1,0:T(8,128)(2,1)}, bf16[64,1664]{1,0:T(8,128)(2,1)S(1)}, u32[]{:S(2)}) copy-start(bf16[64,1664]{1,0:T(8,128)(2,1)S(1)} %add_convert_fusion.7.refs_4_) | copy-start | bytes 638980
  117.5 7.4 %collective-permute-start.23 = (bf16[64,1664]{1,0:T(8,128)(2,1)S(1)}, bf16[64,1664]{1,0:T(8,128)(2,1)S(1)}, u32[]{:S(2)}, u32[]{:S(2)}) collective-permute-start(bf16[64,1664]{1,0:T(8,128)(2,1)S(1)} %add_convert_fusion.7.refs_4_), channel_id=1, source_target_pairs={{0,2},{1,3},{2,0},{3,1},{4,6},{5,7},{6,4},{7,5},{8,10},{9,11},{10,... | collective-permute-start | bytes 638984 | tf_op jit(solution)/shard_map/ppermute | solution.py:25
  118.7 7.3 %collective-permute-start.21 = (bf16[64,1664]{1,0:T(8,128)(2,1)S(1)}, bf16[64,1664]{1,0:T(8,128)(2,1)S(1)}, u32[]{:S(2)}, u32[]{:S(2)}) collective-permute-start(bf16[64,1664]{1,0:T(8,128)(2,1)S(1)} %add_convert_fusion.9.refs_0_), channel_id=1, source_target_pairs={{0,1},{1,0},{2,3},{3,2},{4,5},{5,4},{6,7},{7,6},{8,9},{9,8},{10,11... | collective-permute-start | bytes 638984 | tf_op jit(solution)/shard_map/ppermute | solution.py:25
  118.7 9.4 %copy-start.25 = (bf16[64,1664]{1,0:T(8,128)(2,1)}, bf16[64,1664]{1,0:T(8,128)(2,1)S(1)}, u32[]{:S(2)}) copy-start(bf16[64,1664]{1,0:T(8,128)(2,1)S(1)} %collective-permute-done.20.refs_1_) | copy-start | bytes 638980
  118.7 9.4 %collective-permute-start.22 = (bf16[64,1664]{1,0:T(8,128)(2,1)S(1)}, bf16[64,1664]{1,0:T(8,128)(2,1)S(1)}, u32[]{:S(2)}, u32[]{:S(2)}) collective-permute-start(bf16[64,1664]{1,0:T(8,128)(2,1)S(1)} %collective-permute-done.20.refs_1_), channel_id=1, source_target_pairs={{0,1},{1,0},{2,3},{3,2},{4,5},{5,4},{6,7},{7,6},{8,9},{9,8},{10,11... | collective-permute-start | bytes 638984 | tf_op jit(solution)/shard_map/ppermute | solution.py:25
  119.2 8.9 %collective-permute-start.24 = (bf16[64,1664]{1,0:T(8,128)(2,1)S(1)}, bf16[64,1664]{1,0:T(8,128)(2,1)S(1)}, u32[]{:S(2)}, u32[]{:S(2)}) collective-permute-start(bf16[64,1664]{1,0:T(8,128)(2,1)S(1)} %add_convert_fusion.7.refs_4_), channel_id=1, source_target_pairs={{0,1},{1,0},{2,3},{3,2},{4,5},{5,4},{6,7},{7,6},{8,9},{9,8},{10,11... | collective-permute-start | bytes 638984 | tf_op jit(solution)/shard_map/ppermute | solution.py:25
  124.0 15.6 %collective-permute-start.19 = (bf16[64,1664]{1,0:T(8,128)(2,1)S(1)}, bf16[64,1664]{1,0:T(8,128)(2,1)S(1)}, u32[]{:S(2)}, u32[]{:S(2)}) collective-permute-start(bf16[64,1664]{1,0:T(8,128)(2,1)S(1)} %add_convert_fusion.8), channel_id=1, source_target_pairs={{0,8},{4,12},{8,0},{12,4},{1,9},{5,13},{9,1},{13,5},{2,10},{6,14},... | collective-permute-start | bytes 638984 | tf_op jit(solution)/shard_map/ppermute | solution.py:25
  124.9 3.3 %copy-start.26 = (bf16[64,1664]{1,0:T(8,128)(2,1)}, bf16[64,1664]{1,0:T(8,128)(2,1)S(1)}, u32[]{:S(2)}) copy-start(bf16[64,1664]{1,0:T(8,128)(2,1)S(1)} %collective-permute-done.23.refs_5_) | copy-start | bytes 638980
  124.9 3.2 %collective-permute-start.25 = (bf16[64,1664]{1,0:T(8,128)(2,1)S(1)}, bf16[64,1664]{1,0:T(8,128)(2,1)S(1)}, u32[]{:S(2)}, u32[]{:S(2)}) collective-permute-start(bf16[64,1664]{1,0:T(8,128)(2,1)S(1)} %collective-permute-done.23.refs_5_), channel_id=1, source_target_pairs={{0,1},{1,0},{2,3},{3,2},{4,5},{5,4},{6,7},{7,6},{8,9},{9,8},{10,11... | collective-permute-start | bytes 638984 | tf_op jit(solution)/shard_map/ppermute | solution.py:25
  126.0 2.2 %copy-start.27 = (bf16[64,1664]{1,0:T(8,128)(2,1)}, bf16[64,1664]{1,0:T(8,128)(2,1)S(1)}, u32[]{:S(2)}) copy-start(bf16[64,1664]{1,0:T(8,128)(2,1)S(1)} %collective-permute-done.21.refs_2_) | copy-start | bytes 638980
  126.0 18.0 %collective-permute-start.18 = (bf16[64,1664]{1,0:T(8,128)(2,1)S(1)}, bf16[64,1664]{1,0:T(8,128)(2,1)S(1)}, u32[]{:S(2)}, u32[]{:S(2)}) collective-permute-start(bf16[64,1664]{1,0:T(8,128)(2,1)S(1)} %add_convert_fusion.6), channel_id=1, source_target_pairs={{0,8},{4,12},{8,0},{12,4},{1,9},{5,13},{9,1},{13,5},{2,10},{6,14},... | collective-permute-start | bytes 638984 | tf_op jit(solution)/shard_map/ppermute | solution.py:25
  128.1 0.8 copy-start.29
  139.6 11.7 %copy-start.17 = (bf16[64,1664]{1,0:T(8,128)(2,1)}, bf16[64,1664]{1,0:T(8,128)(2,1)S(1)}, u32[]{:S(2)}) copy-start(bf16[64,1664]{1,0:T(8,128)(2,1)S(1)} %add_convert_fusion.5.refs_0_) | copy-start | bytes 638980
  139.7 7.1 %collective-permute-start.29 = (bf16[64,1664]{1,0:T(8,128)(2,1)S(1)}, bf16[64,1664]{1,0:T(8,128)(2,1)S(1)}, u32[]{:S(2)}, u32[]{:S(2)}) collective-permute-start(bf16[64,1664]{1,0:T(8,128)(2,1)S(1)} %add_convert_fusion.5.refs_0_), channel_id=1, source_target_pairs={{0,2},{1,3},{2,0},{3,1},{4,6},{5,7},{6,4},{7,5},{8,10},{9,11},{10,... | collective-permute-start | bytes 638984 | tf_op jit(solution)/shard_map/ppermute | solution.py:25
  144.1 15.7 %copy-start.4 = (bf16[64,1664]{1,0:T(8,128)(2,1)}, bf16[64,1664]{1,0:T(8,128)(2,1)S(1)}, u32[]{:S(2)}) copy-start(bf16[64,1664]{1,0:T(8,128)(2,1)S(1)} %add_convert_fusion.4.refs_0_) | copy-start | bytes 638980
  144.1 7.2 %collective-permute-start.26 = (bf16[64,1664]{1,0:T(8,128)(2,1)S(1)}, bf16[64,1664]{1,0:T(8,128)(2,1)S(1)}, u32[]{:S(2)}, u32[]{:S(2)}) collective-permute-start(bf16[64,1664]{1,0:T(8,128)(2,1)S(1)} %add_convert_fusion.4.refs_0_), channel_id=1, source_target_pairs={{0,2},{1,3},{2,0},{3,1},{4,6},{5,7},{6,4},{7,5},{8,10},{9,11},{10,... | collective-permute-start | bytes 638984 | tf_op jit(solution)/shard_map/ppermute | solution.py:25
  144.2 7.2 %collective-permute-start.30 = (bf16[64,1664]{1,0:T(8,128)(2,1)S(1)}, bf16[64,1664]{1,0:T(8,128)(2,1)S(1)}, u32[]{:S(2)}, u32[]{:S(2)}) collective-permute-start(bf16[64,1664]{1,0:T(8,128)(2,1)S(1)} %add_convert_fusion.5.refs_0_), channel_id=1, source_target_pairs={{0,1},{1,0},{2,3},{3,2},{4,5},{5,4},{6,7},{7,6},{8,9},{9,8},{10,11... | collective-permute-start | bytes 638984 | tf_op jit(solution)/shard_map/ppermute | solution.py:25
  146.8 4.6 %copy-start.31 = (bf16[64,1664]{1,0:T(8,128)(2,1)}, bf16[64,1664]{1,0:T(8,128)(2,1)S(1)}, u32[]{:S(2)}) copy-start(bf16[64,1664]{1,0:T(8,128)(2,1)S(1)} %collective-permute-done.29.refs_1_) | copy-start | bytes 638980
  146.8 4.6 %collective-permute-start.31 = (bf16[64,1664]{1,0:T(8,128)(2,1)S(1)}, bf16[64,1664]{1,0:T(8,128)(2,1)S(1)}, u32[]{:S(2)}, u32[]{:S(2)}) collective-permute-start(bf16[64,1664]{1,0:T(8,128)(2,1)S(1)} %collective-permute-done.29.refs_1_), channel_id=1, source_target_pairs={{0,1},{1,0},{2,3},{3,2},{4,5},{5,4},{6,7},{7,6},{8,9},{9,8},{10,11... | collective-permute-start | bytes 638984 | tf_op jit(solution)/shard_map/ppermute | solution.py:25
  146.8 13.1 %collective-permute-start.27 = (bf16[64,1664]{1,0:T(8,128)(2,1)S(1)}, bf16[64,1664]{1,0:T(8,128)(2,1)S(1)}, u32[]{:S(2)}, u32[]{:S(2)}) collective-permute-start(bf16[64,1664]{1,0:T(8,128)(2,1)S(1)} %add_convert_fusion.4.refs_0_), channel_id=1, source_target_pairs={{0,1},{1,0},{2,3},{3,2},{4,5},{5,4},{6,7},{7,6},{8,9},{9,8},{10,11... | collective-permute-start | bytes 638984 | tf_op jit(solution)/shard_map/ppermute | solution.py:25
  151.4 8.5 %copy-start.14 = (bf16[64,1664]{1,0:T(8,128)(2,1)}, bf16[64,1664]{1,0:T(8,128)(2,1)S(1)}, u32[]{:S(2)}) copy-start(bf16[64,1664]{1,0:T(8,128)(2,1)S(1)} %collective-permute-done.26.refs_1_) | copy-start | bytes 638980
  151.4 8.5 %collective-permute-start.28 = (bf16[64,1664]{1,0:T(8,128)(2,1)S(1)}, bf16[64,1664]{1,0:T(8,128)(2,1)S(1)}, u32[]{:S(2)}, u32[]{:S(2)}) collective-permute-start(bf16[64,1664]{1,0:T(8,128)(2,1)S(1)} %collective-permute-done.26.refs_1_), channel_id=1, source_target_pairs={{0,1},{1,0},{2,3},{3,2},{4,5},{5,4},{6,7},{7,6},{8,9},{9,8},{10,11... | collective-permute-start | bytes 638984 | tf_op jit(solution)/shard_map/ppermute | solution.py:25
  166.6 7.7 %collective-permute-start.32 = (bf16[64,1024]{1,0:T(8,128)(2,1)S(1)}, bf16[64,1024]{1,0:T(8,128)(2,1)S(1)}, u32[]{:S(2)}, u32[]{:S(2)}) collective-permute-start(bf16[64,1024]{1,0:T(8,128)(2,1)S(1)} %get-tuple-element.254), channel_id=1, source_target_pairs={{0,4},{4,8},{8,12},{12,0},{1,5},{5,9},{9,13},{13,1},{2,6},{6,10},{... | collective-permute-start | bytes 393224 | tf_op jit(solution)/shard_map/ppermute | solution.py:30
  172.1 8.2 %collective-permute-start.34 = (bf16[64,1024]{1,0:T(8,128)(2,1)S(1)}, bf16[64,1024]{1,0:T(8,128)(2,1)S(1)}, u32[]{:S(2)}, u32[]{:S(2)}) collective-permute-start(bf16[64,1024]{1,0:T(8,128)(2,1)S(1)} %get-tuple-element.258), channel_id=1, source_target_pairs={{0,4},{4,8},{8,12},{12,0},{1,5},{5,9},{9,13},{13,1},{2,6},{6,10},{... | collective-permute-start | bytes 393224 | tf_op jit(solution)/shard_map/ppermute | solution.py:30
  174.3 8.2 %collective-permute-start.33 = (bf16[64,1024]{1,0:T(8,128)(2,1)S(1)}, bf16[64,1024]{1,0:T(8,128)(2,1)S(1)}, u32[]{:S(2)}, u32[]{:S(2)}) collective-permute-start(bf16[64,1024]{1,0:T(8,128)(2,1)S(1)} %add_convert_fusion.17), channel_id=1, source_target_pairs={{0,4},{4,8},{8,12},{12,0},{1,5},{5,9},{9,13},{13,1},{2,6},{6,10},{... | collective-permute-start | bytes 393224 | tf_op jit(solution)/shard_map/ppermute | solution.py:30
  180.3 7.4 %collective-permute-start.36 = (bf16[64,1024]{1,0:T(8,128)(2,1)S(1)}, bf16[64,1024]{1,0:T(8,128)(2,1)S(1)}, u32[]{:S(2)}, u32[]{:S(2)}) collective-permute-start(bf16[64,1024]{1,0:T(8,128)(2,1)S(1)} %add_convert_fusion.16), channel_id=1, source_target_pairs={{0,4},{4,8},{8,12},{12,0},{1,5},{5,9},{9,13},{13,1},{2,6},{6,10},{... | collective-permute-start | bytes 393224 | tf_op jit(solution)/shard_map/ppermute | solution.py:30
  182.6 7.8 %collective-permute-start.35 = (bf16[64,1024]{1,0:T(8,128)(2,1)S(1)}, bf16[64,1024]{1,0:T(8,128)(2,1)S(1)}, u32[]{:S(2)}, u32[]{:S(2)}) collective-permute-start(bf16[64,1024]{1,0:T(8,128)(2,1)S(1)} %add_convert_fusion.15), channel_id=1, source_target_pairs={{0,4},{4,8},{8,12},{12,0},{1,5},{5,9},{9,13},{13,1},{2,6},{6,10},{... | collective-permute-start | bytes 393224 | tf_op jit(solution)/shard_map/ppermute | solution.py:30
  187.8 6.8 %collective-permute-start.37 = (bf16[64,1024]{1,0:T(8,128)(2,1)S(1)}, bf16[64,1024]{1,0:T(8,128)(2,1)S(1)}, u32[]{:S(2)}, u32[]{:S(2)}) collective-permute-start(bf16[64,1024]{1,0:T(8,128)(2,1)S(1)} %add_convert_fusion.14), channel_id=1, source_target_pairs={{0,4},{4,8},{8,12},{12,0},{1,5},{5,9},{9,13},{13,1},{2,6},{6,10},{... | collective-permute-start | bytes 393224 | tf_op jit(solution)/shard_map/ppermute | solution.py:30
  (9 other events, 6.3 us)

commit v3 on v2

--- a/solution.py
+++ b/solution.py
@@ -12,9 +12,10 @@
 FACTOR = 13
 LOW = 128
 SMALL = 16
-TILE = 512
-AHEAD = 3
-VMEM_LIMIT = 56 * 2**20
+FOLD = 8
+DEPTH = 1024
+AHEAD = 2
+VMEM_LIMIT = 32 * 2**20
 
 
 def bits_of(size):
@@ -107,33 +108,30 @@
     )(*[down_code] * chunks, down_scale)
 
 
-def tiles_of(width):
-    return [(low, min(TILE, width - low)) for low in range(0, width, TILE)]
-
-
 def gate_up_kernel(parts, peers, pieces, chunk, *refs):
     token_refs = refs[:parts]
     code_refs = refs[parts : parts + 2]
     scale_refs = refs[parts + 2 : parts + 4]
-    keep_ref, send_ref, rows_ref, codes_ref, terms_ref, arrived, done, left = refs[parts + 4 :]
+    keep_ref, send_ref, rows_ref, codes_ref, total_ref, terms_ref, arrived, done, left = refs[parts + 4 :]
     part = token_refs[0].shape[0]
     half, _, share, width = keep_ref.shape
-    tiles = [(side, low, size) for side in range(2) for low, size in tiles_of(width)]
+    features = rows_ref.shape[1]
+    depth = min(features, DEPTH)
+    tiles = [(side, low) for side in range(2) for low in range(0, features, depth)]
 
     def fetch(index):
-        side, low, size = tiles[index]
+        side, low = tiles[index]
         return pltpu.make_async_copy(
-            code_refs[side].at[:, pl.ds(chunk * width + low, size)],
-            codes_ref.at[side, :, pl.ds(low, size)],
+            code_refs[side].at[pl.ds(low, depth), pl.ds(chunk * width, width)],
+            codes_ref.at[side, pl.ds(low, depth), :],
             done.at[index],
         )
 
-    def leave(index, which):
-        side, low, size = tiles[index]
+    def leave(side, which):
         return pltpu.make_async_copy(
-            terms_ref.at[pl.ds(which * half, half), side, :, pl.ds(low, size)],
-            (keep_ref, send_ref)[which].at[:, side, :, pl.ds(low, size)],
-            left.at[index, which],
+            terms_ref.at[pl.ds(which * half, half), side],
+            (keep_ref, send_ref)[which].at[:, side],
+            left.at[side, which],
         )
 
     place = lax.axis_index("tensor")
@@ -158,30 +156,32 @@
                 )
 
             placed.append(put(hop))
-            if parts > peers and hop == peers // 2:
-                pl.when(place < peers // 2)(put(hop).start)
-                pl.when(place >= peers // 2)(put(parts - 1).start)
-            else:
-                put(hop).start()
+            placed[-1].start()
     for index in range(1, min(AHEAD, len(tiles))):
         fetch(index).start()
     for copy in placed:
         copy.wait()
 
-    for index, (side, low, size) in enumerate(tiles):
+    for index, (side, low) in enumerate(tiles):
         if index + AHEAD < len(tiles):
             fetch(index + AHEAD).start()
         fetch(index).wait()
-        cols = slice(low, low + size)
-        weight = scaled(codes_ref[side, :, cols], scale_refs[side][:, cols].astype(jnp.float32))
-        terms = jnp.dot(rows_ref[...], weight, preferred_element_type=jnp.float32).astype(jnp.bfloat16)
+        scales = scale_refs[side][...].astype(jnp.float32)
+        group = features // scales.shape[0]
+        weight = scaled(codes_ref[side, low : low + depth], scales[low // group : (low + depth) // group])
+        terms = jnp.dot(rows_ref[:, low : low + depth], weight, preferred_element_type=jnp.float32)
+        if low:
+            terms = total_ref[...] + terms
+        if low + depth < features:
+            total_ref[...] = terms
+            continue
         for piece in range(pieces):
-            terms_ref[piece, side, :, cols] = terms[piece * share : (piece + 1) * share]
+            terms_ref[piece, side] = terms[piece * share : (piece + 1) * share].astype(jnp.bfloat16)
         for which in range(2):
-            leave(index, which).start()
-    for index in range(len(tiles)):
+            leave(side, which).start()
+    for side in range(2):
         for which in range(2):
-            leave(index, which).wait()
+            leave(side, which).wait()
 
 
 def gate_up(token_parts, gate_code, up_code, gate_scale, up_scale, chunk, width):
@@ -191,7 +191,6 @@
     row_count = part * peers
     share = row_count // pieces
     groups = gate_scale.shape[0]
-    count = 2 * len(tiles_of(width))
     out = jax.ShapeDtypeStruct((pieces // 2, 2, share, width), jnp.bfloat16)
     anywhere = pl.BlockSpec(memory_space=pl.ANY)
     return pl.pallas_call(
@@ -203,10 +202,11 @@
         scratch_shapes=[
             pltpu.VMEM((row_count, features), jnp.bfloat16),
             pltpu.VMEM((2, features, width), jnp.bfloat16),
+            pltpu.VMEM((row_count, width), jnp.float32),
             pltpu.VMEM((pieces, 2, share, width), jnp.bfloat16),
             pltpu.SemaphoreType.DMA((row_count // min(part, share),)),
-            pltpu.SemaphoreType.DMA((count,)),
-            pltpu.SemaphoreType.DMA((count, 2)),
+            pltpu.SemaphoreType.DMA((2 * features // min(features, DEPTH),)),
+            pltpu.SemaphoreType.DMA((2, 2)),
         ],
         compiler_params=params(),
         cost_estimate=pl.CostEstimate(
@@ -248,11 +248,11 @@
     )(*terms, signs, rotation)
 
 
-def down_kernel(chunks, pieces, peers, sums, weights, *refs):
+def down_kernel(chunks, pieces, peers, sums, weights, outs, *refs):
     part_refs = refs[: chunks * pieces]
     weight_refs = refs[chunks * pieces : chunks * (pieces + weights)]
     sum_refs = refs[chunks * (pieces + weights) : chunks * (pieces + weights) + sums]
-    out_ref, rows_ref = refs[chunks * (pieces + weights) + sums :]
+    out_refs, (rows_ref,) = refs[-1 - outs : -1], refs[-1:]
     share = part_refs[0].shape[0]
     row_count = share * pieces
 
@@ -277,31 +277,31 @@
             term = jnp.dot(rows_ref[chunk, :, low:high], weight_ref[0], preferred_element_type=jnp.float32)
             total = term if total is None else total + term
             low = high
-    total = total.reshape(out_ref.shape)
     for sum_ref in sum_refs:
         total = total + sum_ref[...]
-    out_ref[...] = total.astype(out_ref.dtype)
-
-
-def down(parts, weights, sums, chunk, column, columns, tile, kind):
+    size = row_count // outs
+    for index, out_ref in enumerate(out_refs):
+        out_ref[...] = total[index * size : (index + 1) * size].astype(out_ref.dtype)
+
+
+def down(parts, weights, sums, chunk, column, columns, tile, kind, outs):
     peers = lax.axis_size("tensor")
     chunks, pieces = len(parts), len(parts[0])
     share, width = parts[0][0].shape
     row_count = share * pieces
-    part = row_count // peers
     start = column * columns // tile
 
     def weight_spec(weight, index):
         return pl.BlockSpec((1, weight.shape[1], tile), lambda k: (index, 0, start + k))
 
     return pl.pallas_call(
-        functools.partial(down_kernel, chunks, pieces, peers, len(sums), len(weights)),
+        functools.partial(down_kernel, chunks, pieces, peers, len(sums), len(weights), outs),
         grid=(columns // tile,),
         in_specs=[pl.BlockSpec((share, width), lambda k: (0, 0))] * (chunks * pieces)
         + [weight_spec(weight, chunk + index) for index in range(chunks) for weight in weights]
-        + [pl.BlockSpec((peers, part, tile), lambda k: (0, 0, start + k))] * len(sums),
-        out_specs=pl.BlockSpec((peers, part, tile), lambda k: (0, 0, k)),
-        out_shape=jax.ShapeDtypeStruct((peers, part, columns), kind),
+        + [pl.BlockSpec((row_count, tile), lambda k: (0, start + k))] * len(sums),
+        out_specs=[pl.BlockSpec((row_count // outs, tile), lambda k: (0, k))] * outs,
+        out_shape=[jax.ShapeDtypeStruct((row_count // outs, columns), kind)] * outs,
         scratch_shapes=[pltpu.VMEM((chunks, row_count, width), jnp.bfloat16)],
         compiler_params=params(),
         cost_estimate=pl.CostEstimate(
@@ -395,16 +395,25 @@
         else:
             parts[chunk] = doubled(hidden, "dp")
 
-    def product(first, count, sums, column, columns, kind):
+    def product(first, count, sums, column, columns, kind, outs):
         given = [parts[chunk] for chunk in range(first, first + count)]
         tile = min(columns, 512)
-        return order(lambda ps: down(ps, weights, sums, first, column, columns, tile, kind), given)
+        return order(lambda ps: down(ps, weights, sums, first, column, columns, tile, kind, outs), given)
 
     def finish(first, count, sums, halves=2):
         columns = features // halves
-        terms, totals = [], []
+        totals = []
+        if peers == 4:
+            for column in range(halves):
+                behind, far, before, own = product(first, count, sums, column, columns, jnp.bfloat16, peers)
+                totals.append(
+                    [own, shift(far, "tensor", 2), shift(behind, "tensor", -1), shift(before, "tensor")]
+                )
+            totals = [order(lambda ts: add(*ts), total) for total in totals]
+            return jnp.concatenate(totals, axis=1)
+        terms = []
         for column in range(halves):
-            terms.append(product(first, count, sums, column, columns, jnp.bfloat16))
+            terms.append(product(first, count, sums, column, columns, jnp.bfloat16, peers))
             totals.append(shift(terms[-1][0], "tensor"))
         for hop in range(1, peers):
             for column in range(halves):
@@ -413,19 +422,9 @@
                     totals[column] = shift(totals[column], "tensor")
         return jnp.concatenate(totals, axis=1)
 
-    if peers == 4:
-        before = shift(tokens, "tensor")
-        behind = shift(tokens, "tensor", -1)
-        fold(blocks // 3)
-        before, behind, weights[0] = lax.optimization_barrier((before, behind, weights[0]))
-        far_low = lax.ppermute(behind, "tensor", [(1, 0), (2, 1)])
-        far_high = lax.ppermute(before, "tensor", [(1, 2), (2, 3)])
-        token_parts = [tokens, before, far_low, behind, far_high]
-        fold(blocks // 3)
-    else:
-        token_parts = [tokens]
-        for _ in range(peers - 1):
-            token_parts.append(shift(token_parts[-1], "tensor"))
+    token_parts = [tokens] + [shift(tokens, "tensor", hop) for hop in range(1, peers)]
+    token_parts = list(lax.optimization_barrier(tuple(token_parts)))
+    fold(min(blocks, FOLD))
     rest = blocks - sum(weight.shape[1] for weight in weights) * down_scale.shape[0] // down_code.shape[0]
 
     def land_terms(chunk):
@@ -458,10 +457,10 @@
         land_terms(3)
         pass_terms(3)
         fold(rest // 2)
+        land_terms(2)
+        finish_terms(2)
         land_turn(1)
         turn(1, 0)
-        land_terms(2)
-        finish_terms(2)
         land_turn(0)
         turn(0, 1)
         fold(rest - rest // 2)
@@ -471,18 +470,17 @@
         turn(2, 0)
         land_turn(1)
         turn(1, 1)
+        land_parts(0)
+        sums = product(0, 1, [], 0, features, jnp.float32, 1)
         land_turn(3)
         turn(3, 0)
-        land_parts(0)
-        land_parts(1)
-        sums = [product(0, 2, [], 0, features, jnp.float32)]
         land_turn(2)
         turn(2, 1)
+        land_parts(1)
+        sums = product(1, 1, sums, 0, features, jnp.float32, 1)
         land_turn(3)
         turn(3, 1)
-        land_parts(2)
-        sums = [product(2, 1, sums, 0, features, jnp.float32)]
-        return finish(3, 1, sums)
+        return finish(2, 2, sums)
     fold(rest)
     for chunk in range(chunks):
         start_terms(chunk)

time: 196 us -> 164 us (0.84)
  Pallas kernels: 107 us -> 73.5 us
  starting transfers between devices: 30.4 us -> 36.2 us
  waiting for transfers between devices: 42.2 us -> 39.4 us
    pallas_call x4, Pallas kernels: 40.9 us -> 29.7 us  [gate_up(): pl.pallas_call(functools.partial(gate_up_kernel, len(token_parts), peers,...]
    pallas_call x4 -> x3, Pallas kernels: 30.3 us -> 20.1 us  [folded(): pl.pallas_call(functools.partial(fold_kernel, chunks, blocks, first), gri...]
    ppermute x8 -> x9, waiting for transfers between devices: 22.6 us -> 14.4 us  [shift(): lax.ppermute(shard, axis, [(i, (i + step) % size) for i in range(size)])]
    pallas_call x4, Pallas kernels: 25.2 us -> 17.6 us  [down(): pl.pallas_call(functools.partial(down_kernel, chunks, pieces, peers, len(...]
    ppermute x8 -> x9, starting transfers between devices: 7.7 us -> 13.4 us  [shift(): lax.ppermute(shard, axis, [(i, (i + step) % size) for i in range(size)])]
    ppermute x28, waiting for transfers between devices: 19.6 us -> 25 us  [swap(): lax.ppermute(shard, axis, [(i, i ^ 1 << bit) for i in range(lax.axis_size...]
    pallas_call x4, Pallas kernels: 10.9 us -> 6.06 us  [hidden_of(): pl.pallas_call(functools.partial(hidden_kernel, len(terms)), grid=(1,), i...]
    squeeze x2 -> x0, local copies, waits for them, and re-layouts: 2.26 us -> none  [finish(): terms[column][hop]]
  transfers between devices with their start and end apart: 38 -> 37, of which waited for: 14 -> 12; matrix products, arithmetic and copies ran while one was open for 3% -> 2% of each run, Pallas kernels for 48% -> 38%
where the time goes in v3:
time: 164 us; the launch traced here: 163 us
  Pallas kernels  73.5 us (45%)
  waiting for transfers between devices  39.4 us (24%)
  starting transfers between devices  36.2 us (22%)
  local copies, waits for them, and re-layouts  9.1 us (6%)
  other arithmetic  4.47 us (3%)
    pallas_call x4, Pallas kernels, gate_up(): pl.pallas_call(functools.partial(gate_up_kernel, len(token_parts), peers,...  29.7 us
    ppermute x28, waiting for transfers between devices, swap(): lax.ppermute(shard, axis, [(i, i ^ 1 << bit) for i in range(lax.axis_size...  25 us
    ppermute x28, starting transfers between devices, swap(): lax.ppermute(shard, axis, [(i, i ^ 1 << bit) for i in range(lax.axis_size...  22.7 us
    pallas_call x3, Pallas kernels, folded(): pl.pallas_call(functools.partial(fold_kernel, chunks, blocks, first), gri...  20.1 us
    pallas_call x4, Pallas kernels, down(): pl.pallas_call(functools.partial(down_kernel, chunks, pieces, peers, len(...  17.6 us
    ppermute x9, waiting for transfers between devices, shift(): lax.ppermute(shard, axis, [(i, (i + step) % size) for i in range(size)])  14.4 us
    ppermute x9, starting transfers between devices, shift(): lax.ppermute(shard, axis, [(i, (i + step) % size) for i in range(size)])  13.4 us
    unnamed x28, local copies, waits for them, and re-layouts  9.08 us
  transfers between devices with their start and end apart: 37, of which 12 were waited for; matrix products, arithmetic and copies ran while one was open for 2% of the time, Pallas kernels for 38%

profile of v3, /device:TPU:0, one launch (start us, length us, event | category | flops | bytes accessed | tf_op | source)
XLA Modules:
  0.0 163.0 jit_solution(15740059360469212766)
XLA Ops:
  0.0 4.1 %collective-permute-start.1 = (bf16[64,2048]{1,0:T(8,128)(2,1)}, bf16[64,2048]{1,0:T(8,128)(2,1)S(1)}, u32[]{:S(2)}, u32[]{:S(2)}) collective-permute-start(bf16[64,2048]{1,0:T(8,128)(2,1)} %refs_0_.5), channel_id=1, source_target_pairs={{0,8},{4,12},{8,0},{12,4},{1,9},{5,13},{9,1},{13,5},{2,10},{6,14},... | collective-permute-start | bytes 786440 | tf_op jit(solution)/shard_map/ppermute | solution.py:31
  4.1 1.6 collective-permute-start
  5.7 2.2 %collective-permute-start.2 = (bf16[64,2048]{1,0:T(8,128)(2,1)}, bf16[64,2048]{1,0:T(8,128)(2,1)S(1)}, u32[]{:S(2)}, u32[]{:S(2)}) collective-permute-start(bf16[64,2048]{1,0:T(8,128)(2,1)} %refs_0_.5), channel_id=1, source_target_pairs={{0,12},{4,0},{8,4},{12,8},{1,13},{5,1},{9,5},{13,9},{2,14},{6,2},{... | collective-permute-start | bytes 786440 | tf_op jit(solution)/shard_map/ppermute | solution.py:31
  7.9 0.9 copy-done.4
  8.9 11.4 %fold_down_0.1.refs_4_.refs_8_.refs_11_ = bf16[4,1024,2048]{2,1,0:T(8,128)(2,1)S(1)} custom-call(bf16[6656,2048]{1,0:T(8,128)(2,1)} %refs_3_.3, bf16[6656,2048]{1,0:T(8,128)(2,1)} %refs_3_.3, bf16[6656,2048]{1,0:T(8,128)(2,1)} %refs_3_.3, bf16[6656,2048]{1,0:T(8,128)(2,1)} %refs_3_.3, bf16[52,2048]{1,0:T(8,128)(2,1)S(1)} %copy-done.4), custom_call_target="tpu_custom_call" | custom-call | bytes 33554432 | tf_op jit(solution)/shard_map/fold_down_0/pallas_call | solution.py:95
  20.3 5.8 %copy-done = bf16[4,1024,2048]{2,1,0:T(8,128)(2,1)} copy-done((bf16[4,1024,2048]{2,1,0:T(8,128)(2,1)}, bf16[4,1024,2048]{2,1,0:T(8,128)(2,1)S(1)}, u32[]{:S(2)}) %copy-start) | copy-done | bytes 16777240
  26.1 7.2 %gate_up_0.1 = (bf16[2,2,64,1664]{3,2,1,0:T(8,128)(2,1)S(1)}, bf16[2,2,64,1664]{3,2,1,0:T(8,128)(2,1)S(1)}) custom-call(bf16[64,2048]{1,0:T(8,128)(2,1)S(1)} %copy-done.1, bf16[64,2048]{1,0:T(8,128)(2,1)S(1)} %collective-permute-done.refs_1_, bf16[64,2048]{1,0:T(8,128)(2,1)S(1)} %collective-permute-done.1.refs_2_, ...), custom_call_target="tpu_custom_call" | custom-call | flops 3489660928 | bytes 13631488 | tf_op jit(solution)/shard_map/gate_up_0/pallas_call | solution.py:196
  33.4 7.4 %gate_up_1.1 = (bf16[2,2,64,1664]{3,2,1,0:T(8,128)(2,1)S(1)}, bf16[2,2,64,1664]{3,2,1,0:T(8,128)(2,1)S(1)}) custom-call(bf16[64,2048]{1,0:T(8,128)(2,1)S(1)} %copy-done.1, bf16[64,2048]{1,0:T(8,128)(2,1)S(1)} %collective-permute-done.refs_1_, bf16[64,2048]{1,0:T(8,128)(2,1)S(1)} %collective-permute-done.1.refs_2_, ...), custom_call_target="tpu_custom_call" | custom-call | flops 3489660928 | bytes 13631488 | tf_op jit(solution)/shard_map/gate_up_1/pallas_call | solution.py:196
  40.8 0.3 collective-permute-start.7
  41.1 1.0 add_convert_fusion.3
  42.1 1.5 collective-permute-start.6
  43.6 8.0 %gate_up_2.1 = (bf16[2,2,64,1664]{3,2,1,0:T(8,128)(2,1)S(1)}, bf16[2,2,64,1664]{3,2,1,0:T(8,128)(2,1)}) custom-call(bf16[64,2048]{1,0:T(8,128)(2,1)S(1)} %copy-done.1, bf16[64,2048]{1,0:T(8,128)(2,1)S(1)} %collective-permute-done.refs_1_, bf16[64,2048]{1,0:T(8,128)(2,1)S(1)} %collective-permute-done.1.refs_2_, ...), custom_call_target="tpu_custom_call" | custom-call | flops 3489660928 | bytes 13631488 | tf_op jit(solution)/shard_map/gate_up_2/pallas_call | solution.py:196
  51.6 0.1 collective-permute-start.4
  51.7 0.9 add_convert_fusion.1
  52.6 1.4 collective-permute-start.9
  54.0 0.4 collective-permute-done.6.refs_2_
  54.4 1.2 copy-done.9
  55.5 1.2 copy-done.11
  56.7 1.8 %hidden_0.1 = bf16[64,1664]{1,0:T(8,128)(2,1)S(1)} custom-call(bf16[2,2,64,1664]{3,2,1,0:T(8,128)(2,1)S(1)} %copy-done.9, bf16[2,2,64,1664]{3,2,1,0:T(8,128)(2,1)S(1)} %copy-done.11, bf16[1,2,64,1664]{3,2,1,0:T(8,128)(2,1)} %collective-permute-done.6.refs_2_, f32[4,1,1664]{2,1,0:T(1,128)S(1)} %reshape.3.refs_3_, bf16[208,208]{1,0:T(8,128)(2,1)S(1)} %copy-done.12), custom_call_target="tpu_custom_call" | custom-call | flops 44302336 | bytes 1490944 | tf_op jit(solution)/shard_map/hidden_0/pallas_call | solution.py:236
  58.5 2.3 %collective-permute-start.10 = (bf16[64,1664]{1,0:T(8,128)(2,1)S(1)}, bf16[64,1664]{1,0:T(8,128)(2,1)S(1)}, u32[]{:S(2)}, u32[]{:S(2)}) collective-permute-start(bf16[64,1664]{1,0:T(8,128)(2,1)S(1)} %hidden_0.1), channel_id=1, source_target_pairs={{0,4},{4,0},{8,12},{12,8},{1,5},{5,1},{9,13},{13,9},{2,6},{6,2},{1... | collective-permute-start | bytes 638984 | tf_op jit(solution)/shard_map/ppermute | solution.py:26
  60.8 7.2 %gate_up_3.1 = (bf16[2,2,64,1664]{3,2,1,0:T(8,128)(2,1)S(1)}, bf16[2,2,64,1664]{3,2,1,0:T(8,128)(2,1)S(1)}) custom-call(bf16[64,2048]{1,0:T(8,128)(2,1)S(1)} %copy-done.1, bf16[64,2048]{1,0:T(8,128)(2,1)S(1)} %collective-permute-done.refs_1_, bf16[64,2048]{1,0:T(8,128)(2,1)S(1)} %collective-permute-done.1.refs_2_, ...), custom_call_target="tpu_custom_call" | custom-call | flops 3489660928 | bytes 13631488 | tf_op jit(solution)/shard_map/gate_up_3/pallas_call | solution.py:196
  68.1 1.1 add_convert_fusion.2
  69.2 1.6 collective-permute-start.5
  70.8 2.0 %collective-permute-start.12 = (bf16[64,1664]{1,0:T(8,128)(2,1)S(1)}, bf16[64,1664]{1,0:T(8,128)(2,1)S(1)}, u32[]{:S(2)}, u32[]{:S(2)}) collective-permute-start(bf16[64,1664]{1,0:T(8,128)(2,1)S(1)} %add_convert_fusion.11), channel_id=1, source_target_pairs={{0,8},{4,12},{8,0},{12,4},{1,9},{5,13},{9,1},{13,5},{2,10},{6,14},... | collective-permute-start | bytes 638984 | tf_op jit(solution)/shard_map/ppermute | solution.py:26
  72.8 1.8 %hidden_1.1 = bf16[64,1664]{1,0:T(8,128)(2,1)S(1)} custom-call(bf16[2,2,64,1664]{3,2,1,0:T(8,128)(2,1)S(1)} %get-tuple-element.171.refs_0_, bf16[2,2,64,1664]{3,2,1,0:T(8,128)(2,1)S(1)} %copy-done.7, bf16[1,2,64,1664]{3,2,1,0:T(8,128)(2,1)} %collective-permute-done.9.refs_2_, f32[4,1,1664]{2,1,0:T(1,128)S(1)} %reshape.3.refs_3_, bf16[208,208]{1,0:T(8,128)(2,1)S(1)} %copy-done.12), custom_call_target="tpu_custom_call" | custom-call | flops 44302336 | bytes 1490944 | tf_op jit(solution)/shard_map/hidden_1/pallas_call | solution.py:236
  74.6 2.0 %collective-permute-start.13 = (bf16[64,1664]{1,0:T(8,128)(2,1)S(1)}, bf16[64,1664]{1,0:T(8,128)(2,1)S(1)}, u32[]{:S(2)}, u32[]{:S(2)}) collective-permute-start(bf16[64,1664]{1,0:T(8,128)(2,1)S(1)} %hidden_1.1), channel_id=1, source_target_pairs={{0,4},{4,0},{8,12},{12,8},{1,5},{5,1},{9,13},{13,9},{2,6},{6,2},{1... | collective-permute-start | bytes 638984 | tf_op jit(solution)/shard_map/ppermute | solution.py:26
  76.6 0.1 add_convert_fusion
  76.7 0.6 collective-permute-start.14
  77.3 3.6 %fold_down_8.1.refs_5_.refs_9_.refs_12_ = bf16[4,256,2048]{2,1,0:T(8,128)(2,1)S(1)} custom-call(bf16[6656,2048]{1,0:T(8,128)(2,1)} %refs_3_.3, bf16[6656,2048]{1,0:T(8,128)(2,1)} %refs_3_.3, bf16[6656,2048]{1,0:T(8,128)(2,1)} %refs_3_.3, bf16[6656,2048]{1,0:T(8,128)(2,1)} %refs_3_.3, bf16[52,2048]{1,0:T(8,128)(2,1)S(1)} %copy-done.5), custom_call_target="tpu_custom_call" | custom-call | bytes 8388608 | tf_op jit(solution)/shard_map/fold_down_8/pallas_call | solution.py:95
  80.9 1.0 collective-permute-done.5.refs_2_
  81.9 1.8 %hidden_2.1 = bf16[64,1664]{1,0:T(8,128)(2,1)S(1)} custom-call(bf16[2,2,64,1664]{3,2,1,0:T(8,128)(2,1)S(1)} %get-tuple-element.179.refs_0_, bf16[2,2,64,1664]{3,2,1,0:T(8,128)(2,1)} %collective-permute-done.4.refs_1_, bf16[1,2,64,1664]{3,2,1,0:T(8,128)(2,1)S(1)} %collective-permute-done.5.refs_2_, f32[4,1,1664]{2,1,0:T(1,128)S(1)} %reshape.3.refs_3_, ...), custom_call_target="tpu_custom_call" | custom-call | flops 44302336 | bytes 1490944 | tf_op jit(solution)/shard_map/hidden_2/pallas_call | solution.py:236
  83.6 0.2 collective-permute-start.11
  83.8 2.0 %collective-permute-done.13 = bf16[64,1664]{1,0:T(8,128)(2,1)S(1)} collective-permute-done((bf16[64,1664]{1,0:T(8,128)(2,1)S(1)}, bf16[64,1664]{1,0:T(8,128)(2,1)S(1)}, u32[]{:S(2)}, u32[]{:S(2)}) %collective-permute-start.13) | collective-permute-done | bytes 213024 | tf_op jit(solution)/shard_map/ppermute | solution.py:26
  86.0 0.5 collective-permute-start.17
  86.5 2.8 %collective-permute-start.20 = (bf16[64,1664]{1,0:T(8,128)(2,1)S(1)}, bf16[64,1664]{1,0:T(8,128)(2,1)S(1)}, u32[]{:S(2)}, u32[]{:S(2)}) collective-permute-start(bf16[64,1664]{1,0:T(8,128)(2,1)S(1)} %add_convert_fusion.10), channel_id=1, source_target_pairs={{0,8},{4,12},{8,0},{12,4},{1,9},{5,13},{9,1},{13,5},{2,10},{6,14},... | collective-permute-start | bytes 638984 | tf_op jit(solution)/shard_map/ppermute | solution.py:26
  89.3 5.1 %fold_down_10.1.refs_6_.refs_10_.refs_13_ = bf16[4,384,2048]{2,1,0:T(8,128)(2,1)S(1)} custom-call(bf16[6656,2048]{1,0:T(8,128)(2,1)} %refs_3_.3, bf16[6656,2048]{1,0:T(8,128)(2,1)} %refs_3_.3, bf16[6656,2048]{1,0:T(8,128)(2,1)} %refs_3_.3, bf16[6656,2048]{1,0:T(8,128)(2,1)} %refs_3_.3, bf16[52,2048]{1,0:T(8,128)(2,1)S(1)} %copy-done.5), custom_call_target="tpu_custom_call" | custom-call | bytes 12582912 | tf_op jit(solution)/shard_map/fold_down_10/pallas_call | solution.py:95
  94.3 0.8 collective-permute-done.17.refs_1_
  95.1 0.8 hidden_3.1
  95.9 0.2 collective-permute-start.16
  96.1 3.7 %collective-permute-done.20 = bf16[64,1664]{1,0:T(8,128)(2,1)S(1)} collective-permute-done((bf16[64,1664]{1,0:T(8,128)(2,1)S(1)}, bf16[64,1664]{1,0:T(8,128)(2,1)S(1)}, u32[]{:S(2)}, u32[]{:S(2)}) %collective-permute-start.20) | collective-permute-done | bytes 213024 | tf_op jit(solution)/shard_map/ppermute | solution.py:26
  100.0 1.2 collective-permute-start.25
  101.2 0.6 collective-permute-start.15
  101.8 4.7 %down_0_0.1.refs_7_ = f32[256,2048]{1,0:T(8,128)S(1)} custom-call(bf16[64,1664]{1,0:T(8,128)(2,1)S(1)} %add_convert_fusion.9.refs_0_, bf16[64,1664]{1,0:T(8,128)(2,1)S(1)} %collective-permute-done.17.refs_1_, bf16[64,1664]{1,0:T(8,128)(2,1)S(1)} %collective-permute-done.18.refs_2_, bf16[64,1664]{1,0:T(8,128)(2,1)S(1)} %collective-permute-done.19.refs_3_, ...), custom_call_target="tpu_custom_call" | custom-call | flops 1744830464 | bytes 6815744 | tf_op jit(solution)/shard_map/down_0_0/pallas_call | solution.py:297
  106.6 2.4 %collective-permute-start.24 = (bf16[64,1664]{1,0:T(8,128)(2,1)S(1)}, bf16[64,1664]{1,0:T(8,128)(2,1)S(1)}, u32[]{:S(2)}, u32[]{:S(2)}) collective-permute-start(bf16[64,1664]{1,0:T(8,128)(2,1)S(1)} %add_convert_fusion.6), channel_id=1, source_target_pairs={{0,8},{4,12},{8,0},{12,4},{1,9},{5,13},{9,1},{13,5},{2,10},{6,14},... | collective-permute-start | bytes 638984 | tf_op jit(solution)/shard_map/ppermute | solution.py:26
  109.0 9.9 %collective-permute-done.15 = bf16[64,1664]{1,0:T(8,128)(2,1)S(1)} collective-permute-done((bf16[64,1664]{1,0:T(8,128)(2,1)S(1)}, bf16[64,1664]{1,0:T(8,128)(2,1)S(1)}, u32[]{:S(2)}, u32[]{:S(2)}) %collective-permute-start.15) | collective-permute-done | bytes 213024 | tf_op jit(solution)/shard_map/ppermute | solution.py:26
  119.0 1.2 collective-permute-start.21
  120.3 0.1 collective-permute-done.27.refs_3_
  120.4 4.8 %down_1_0.1.refs_14_ = f32[256,2048]{1,0:T(8,128)S(1)} custom-call(bf16[64,1664]{1,0:T(8,128)(2,1)S(1)} %add_convert_fusion.7.refs_0_, bf16[64,1664]{1,0:T(8,128)(2,1)S(1)} %collective-permute-done.25.refs_1_, bf16[64,1664]{1,0:T(8,128)(2,1)S(1)} %collective-permute-done.26.refs_2_, bf16[64,1664]{1,0:T(8,128)(2,1)S(1)} %collective-permute-done.27.refs_3_, ...), custom_call_target="tpu_custom_call" | custom-call | flops 1744830464 | bytes 6815744 | tf_op jit(solution)/shard_map/down_1_0/pallas_call | solution.py:297
  125.3 1.2 collective-permute-start.28
  126.5 0.5 collective-permute-start.29
  127.0 5.6 %collective-permute-done.28.refs_5_ = bf16[64,1664]{1,0:T(8,128)(2,1)S(1)} collective-permute-done((bf16[64,1664]{1,0:T(8,128)(2,1)S(1)}, bf16[64,1664]{1,0:T(8,128)(2,1)S(1)}, u32[]{:S(2)}, u32[]{:S(2)}) %collective-permute-start.28) | collective-permute-done | bytes 213024 | tf_op jit(solution)/shard_map/ppermute | solution.py:26
  132.7 1.4 collective-permute-done.30.refs_7_
  134.1 4.0 %down_2_0.1 = (bf16[64,1024]{1,0:T(8,128)(2,1)S(1)}, bf16[64,1024]{1,0:T(8,128)(2,1)S(1)}, bf16[64,1024]{1,0:T(8,128)(2,1)S(1)}, bf16[64,1024]{1,0:T(8,128)(2,1)S(1)}) custom-call(bf16[64,1664]{1,0:T(8,128)(2,1)S(1)} %add_convert_fusion.5.refs_0_, bf16[64,1664]{1,0:T(8,128)(2,1)S(1)} %collective-permute-done.21.refs_1_, ...), custom_call_target="tpu_custom_call" | custom-call | flops 1744830464 | bytes 6815744 | tf_op jit(solution)/shard_map/down_2_0/pallas_call | solution.py:297
  138.1 1.0 collective-permute-start.32
  139.2 1.0 collective-permute-start.33
  140.2 4.0 %down_2_1.1 = (bf16[64,1024]{1,0:T(8,128)(2,1)S(1)}, bf16[64,1024]{1,0:T(8,128)(2,1)S(1)}, bf16[64,1024]{1,0:T(8,128)(2,1)S(1)}, bf16[64,1024]{1,0:T(8,128)(2,1)S(1)}) custom-call(bf16[64,1664]{1,0:T(8,128)(2,1)S(1)} %add_convert_fusion.5.refs_0_, bf16[64,1664]{1,0:T(8,128)(2,1)S(1)} %collective-permute-done.21.refs_1_, ...), custom_call_target="tpu_custom_call" | custom-call | flops 1744830464 | bytes 6815744 | tf_op jit(solution)/shard_map/down_2_1/pallas_call | solution.py:297
  144.3 3.0 %collective-permute-start.34 = (bf16[64,1024]{1,0:T(8,128)(2,1)S(1)}, bf16[64,1024]{1,0:T(8,128)(2,1)S(1)}, u32[]{:S(2)}, u32[]{:S(2)}) collective-permute-start(bf16[64,1024]{1,0:T(8,128)(2,1)S(1)} %get-tuple-element.247), channel_id=1, source_target_pairs={{0,8},{4,12},{8,0},{12,4},{1,9},{5,13},{9,1},{13,5},{2,10},{6,14},... | collective-permute-start | bytes 393224 | tf_op jit(solution)/shard_map/ppermute | solution.py:31
  147.3 0.4 collective-permute-start.36
  147.7 9.5 %collective-permute-done.31 = bf16[64,1024]{1,0:T(8,128)(2,1)S(1)} collective-permute-done((bf16[64,1024]{1,0:T(8,128)(2,1)S(1)}, bf16[64,1024]{1,0:T(8,128)(2,1)S(1)}, u32[]{:S(2)}, u32[]{:S(2)}) %collective-permute-start.31) | collective-permute-done | bytes 131104 | tf_op jit(solution)/shard_map/ppermute | solution.py:31
  157.2 0.1 add_convert_fusion.13
  157.3 2.7 %collective-permute-done.34 = bf16[64,1024]{1,0:T(8,128)(2,1)S(1)} collective-permute-done((bf16[64,1024]{1,0:T(8,128)(2,1)S(1)}, bf16[64,1024]{1,0:T(8,128)(2,1)S(1)}, u32[]{:S(2)}, u32[]{:S(2)}) %collective-permute-start.34) | collective-permute-done | bytes 131104 | tf_op jit(solution)/shard_map/ppermute | solution.py:31
  160.0 2.2 %collective-permute-done.35 = bf16[64,1024]{1,0:T(8,128)(2,1)S(1)} collective-permute-done((bf16[64,1024]{1,0:T(8,128)(2,1)S(1)}, bf16[64,1024]{1,0:T(8,128)(2,1)S(1)}, u32[]{:S(2)}, u32[]{:S(2)}) %collective-permute-start.35) | collective-permute-done | bytes 131104 | tf_op jit(solution)/shard_map/ppermute | solution.py:31
  162.2 0.1 add_convert_fusion.12
  162.3 0.7 pad_maximum_fusion
  (70 shorter events, 0.9 us)
Async XLA Ops:
  0.0 26.1 %copy-start.1 = (bf16[64,2048]{1,0:T(8,128)(2,1)S(1)}, bf16[64,2048]{1,0:T(8,128)(2,1)}, u32[]{:S(2)}) copy-start(bf16[64,2048]{1,0:T(8,128)(2,1)} %refs_0_.5) | copy-start | bytes 786436
  0.0 26.1 %copy-start.3 = (bf16[16,6656]{1,0:T(8,128)(2,1)S(1)}, bf16[16,6656]{1,0:T(8,128)(2,1)}, u32[]{:S(2)}) copy-start(bf16[16,6656]{1,0:T(8,128)(2,1)} %refs_7_.7) | copy-start | bytes 638980
  0.0 26.1 %copy-start.2 = (bf16[16,6656]{1,0:T(8,128)(2,1)S(1)}, bf16[16,6656]{1,0:T(8,128)(2,1)}, u32[]{:S(2)}) copy-start(bf16[16,6656]{1,0:T(8,128)(2,1)} %refs_6_.7) | copy-start | bytes 638980
  0.0 26.1 %collective-permute-start.1 = (bf16[64,2048]{1,0:T(8,128)(2,1)}, bf16[64,2048]{1,0:T(8,128)(2,1)S(1)}, u32[]{:S(2)}, u32[]{:S(2)}) collective-permute-start(bf16[64,2048]{1,0:T(8,128)(2,1)} %refs_0_.5), channel_id=1, source_target_pairs={{0,8},{4,12},{8,0},{12,4},{1,9},{5,13},{9,1},{13,5},{2,10},{6,14},... | collective-permute-start | bytes 786440 | tf_op jit(solution)/shard_map/ppermute | solution.py:31
  4.1 22.0 %collective-permute-start = (bf16[64,2048]{1,0:T(8,128)(2,1)}, bf16[64,2048]{1,0:T(8,128)(2,1)S(1)}, u32[]{:S(2)}, u32[]{:S(2)}) collective-permute-start(bf16[64,2048]{1,0:T(8,128)(2,1)} %refs_0_.5), channel_id=1, source_target_pairs={{0,4},{4,8},{8,12},{12,0},{1,5},{5,9},{9,13},{13,1},{2,6},{6,10},{... | collective-permute-start | bytes 786440 | tf_op jit(solution)/shard_map/ppermute | solution.py:31
  5.7 20.4 %collective-permute-start.2 = (bf16[64,2048]{1,0:T(8,128)(2,1)}, bf16[64,2048]{1,0:T(8,128)(2,1)S(1)}, u32[]{:S(2)}, u32[]{:S(2)}) collective-permute-start(bf16[64,2048]{1,0:T(8,128)(2,1)} %refs_0_.5), channel_id=1, source_target_pairs={{0,12},{4,0},{8,4},{12,8},{1,13},{5,1},{9,5},{13,9},{2,14},{6,2},{... | collective-permute-start | bytes 786440 | tf_op jit(solution)/shard_map/ppermute | solution.py:31
  7.9 0.9 copy-start.4
  20.3 5.8 %copy-start = (bf16[4,1024,2048]{2,1,0:T(8,128)(2,1)}, bf16[4,1024,2048]{2,1,0:T(8,128)(2,1)S(1)}, u32[]{:S(2)}) copy-start(bf16[4,1024,2048]{2,1,0:T(8,128)(2,1)S(1)} %fold_down_0.1.refs_4_.refs_8_.refs_11_) | copy-start | bytes 50331652
  33.3 7.8 %copy-start.8 = (bf16[2,2,64,1664]{3,2,1,0:T(8,128)(2,1)}, bf16[2,2,64,1664]{3,2,1,0:T(8,128)(2,1)S(1)}, u32[]{:S(2)}) copy-start(bf16[2,2,64,1664]{3,2,1,0:T(8,128)(2,1)S(1)} %get-tuple-element.159.refs_0_) | copy-start | bytes 2555908
  33.3 7.8 %collective-permute-start.3 = (bf16[2,2,64,1664]{3,2,1,0:T(8,128)(2,1)S(1)}, bf16[2,2,64,1664]{3,2,1,0:T(8,128)(2,1)S(1)}, u32[]{:S(2)}, u32[]{:S(2)}) collective-permute-start(bf16[2,2,64,1664]{3,2,1,0:T(8,128)(2,1)S(1)} %get-tuple-element.138), channel_id=1, source_target_pairs={{0,1},{1,0},{2,3},{3,2},{4,5},{5,4},{6,7},{7,6},{8,9},{9,8},{10,11... | collective-permute-start | bytes 2555912 | tf_op jit(solution)/shard_map/ppermute | solution.py:26
  40.8 2.8 %collective-permute-start.7 = (bf16[2,2,64,1664]{3,2,1,0:T(8,128)(2,1)S(1)}, bf16[2,2,64,1664]{3,2,1,0:T(8,128)(2,1)S(1)}, u32[]{:S(2)}, u32[]{:S(2)}) collective-permute-start(bf16[2,2,64,1664]{3,2,1,0:T(8,128)(2,1)S(1)} %get-tuple-element.156), channel_id=1, source_target_pairs={{0,1},{1,0},{2,3},{3,2},{4,5},{5,4},{6,7},{7,6},{8,9},{9,8},{10,11... | collective-permute-start | bytes 2555912 | tf_op jit(solution)/shard_map/ppermute | solution.py:26
  41.1 10.5 %copy-start.10 = (bf16[2,2,64,1664]{3,2,1,0:T(8,128)(2,1)}, bf16[2,2,64,1664]{3,2,1,0:T(8,128)(2,1)S(1)}, u32[]{:S(2)}) copy-start(bf16[2,2,64,1664]{3,2,1,0:T(8,128)(2,1)S(1)} %collective-permute-done.3.refs_1_) | copy-start | bytes 2555908
  42.1 11.9 %copy-start.13 = (s32[6656]{0:T(1024)S(1)}, s32[6656]{0:T(1024)}, u32[]{:S(2)}) copy-start(s32[6656]{0:T(1024)} %param.16) | copy-start | bytes 79876
  42.1 12.3 %copy-start.12 = (bf16[208,208]{1,0:T(8,128)(2,1)S(1)}, bf16[208,208]{1,0:T(8,128)(2,1)}, u32[]{:S(2)}) copy-start(bf16[208,208]{1,0:T(8,128)(2,1)} %constant.18.clone.refs_4_) | copy-start | bytes 259588
  42.1 12.3 %collective-permute-start.6 = (bf16[1,2,64,1664]{3,2,1,0:T(8,128)(2,1)}, bf16[1,2,64,1664]{3,2,1,0:T(8,128)(2,1)}, u32[]{:S(2)}, u32[]{:S(2)}) collective-permute-start(bf16[1,2,64,1664]{3,2,1,0:T(8,128)(2,1)} %add_convert_fusion.3), channel_id=1, source_target_pairs={{0,2},{1,3},{2,0},{3,1},{4,6},{5,7},{6,4},{7,5},{8,10},{9,11},{10,... | collective-permute-start | bytes 1277960 | tf_op jit(solution)/shard_map/ppermute | solution.py:26
  43.6 8.1 %copy-start.6 = (bf16[2,2,64,1664]{3,2,1,0:T(8,128)(2,1)}, bf16[2,2,64,1664]{3,2,1,0:T(8,128)(2,1)S(1)}, u32[]{:S(2)}) copy-start(bf16[2,2,64,1664]{3,2,1,0:T(8,128)(2,1)S(1)} %collective-permute-done.7.refs_1_) | copy-start | bytes 2555908
  51.6 16.4 %collective-permute-start.4 = (bf16[2,2,64,1664]{3,2,1,0:T(8,128)(2,1)}, bf16[2,2,64,1664]{3,2,1,0:T(8,128)(2,1)}, u32[]{:S(2)}, u32[]{:S(2)}) collective-permute-start(bf16[2,2,64,1664]{3,2,1,0:T(8,128)(2,1)} %get-tuple-element.152), channel_id=1, source_target_pairs={{0,1},{1,0},{2,3},{3,2},{4,5},{5,4},{6,7},{7,6},{8,9},{9,8},{10,11... | collective-permute-start | bytes 2555912 | tf_op jit(solution)/shard_map/ppermute | solution.py:26
  52.6 15.5 %collective-permute-start.9 = (bf16[1,2,64,1664]{3,2,1,0:T(8,128)(2,1)}, bf16[1,2,64,1664]{3,2,1,0:T(8,128)(2,1)}, u32[]{:S(2)}, u32[]{:S(2)}) collective-permute-start(bf16[1,2,64,1664]{3,2,1,0:T(8,128)(2,1)} %add_convert_fusion.1), channel_id=1, source_target_pairs={{0,2},{1,3},{2,0},{3,1},{4,6},{5,7},{6,4},{7,5},{8,10},{9,11},{10,... | collective-permute-start | bytes 1277960 | tf_op jit(solution)/shard_map/ppermute | solution.py:26
  54.4 1.2 copy-start.9
  55.5 1.2 copy-start.11
  58.5 14.3 %copy-start.7 = (bf16[2,2,64,1664]{3,2,1,0:T(8,128)(2,1)S(1)}, bf16[2,2,64,1664]{3,2,1,0:T(8,128)(2,1)}, u32[]{:S(2)}) copy-start(bf16[2,2,64,1664]{3,2,1,0:T(8,128)(2,1)} %copy-done.6) | copy-start | bytes 2555908
  58.5 18.8 %copy-start.5 = (bf16[52,2048]{1,0:T(8,128)(2,1)S(1)}, bf16[52,2048]{1,0:T(8,128)(2,1)}, u32[]{:S(2)}) copy-start(bf16[52,2048]{1,0:T(8,128)(2,1)} %refs_4_.17) | copy-start | bytes 638980
  58.5 9.5 %collective-permute-start.10 = (bf16[64,1664]{1,0:T(8,128)(2,1)S(1)}, bf16[64,1664]{1,0:T(8,128)(2,1)S(1)}, u32[]{:S(2)}, u32[]{:S(2)}) collective-permute-start(bf16[64,1664]{1,0:T(8,128)(2,1)S(1)} %hidden_0.1), channel_id=1, source_target_pairs={{0,4},{4,0},{8,12},{12,8},{1,5},{5,1},{9,13},{13,9},{2,6},{6,2},{1... | collective-permute-start | bytes 638984 | tf_op jit(solution)/shard_map/ppermute | solution.py:26
  68.0 8.6 %collective-permute-start.8 = (bf16[2,2,64,1664]{3,2,1,0:T(8,128)(2,1)S(1)}, bf16[2,2,64,1664]{3,2,1,0:T(8,128)(2,1)S(1)}, u32[]{:S(2)}, u32[]{:S(2)}) collective-permute-start(bf16[2,2,64,1664]{3,2,1,0:T(8,128)(2,1)S(1)} %get-tuple-element.167), channel_id=1, source_target_pairs={{0,1},{1,0},{2,3},{3,2},{4,5},{5,4},{6,7},{7,6},{8,9},{9,8},{10,11... | collective-permute-start | bytes 2555912 | tf_op jit(solution)/shard_map/ppermute | solution.py:26
  69.2 12.7 %collective-permute-start.5 = (bf16[1,2,64,1664]{3,2,1,0:T(8,128)(2,1)S(1)}, bf16[1,2,64,1664]{3,2,1,0:T(8,128)(2,1)S(1)}, u32[]{:S(2)}, u32[]{:S(2)}) collective-permute-start(bf16[1,2,64,1664]{3,2,1,0:T(8,128)(2,1)S(1)} %add_convert_fusion.2), channel_id=1, source_target_pairs={{0,2},{1,3},{2,0},{3,1},{4,6},{5,7},{6,4},{7,5},{8,10},{9,11},{10,... | collective-permute-start | bytes 1277960 | tf_op jit(solution)/shard_map/ppermute | solution.py:26
  70.8 15.1 %collective-permute-start.12 = (bf16[64,1664]{1,0:T(8,128)(2,1)S(1)}, bf16[64,1664]{1,0:T(8,128)(2,1)S(1)}, u32[]{:S(2)}, u32[]{:S(2)}) collective-permute-start(bf16[64,1664]{1,0:T(8,128)(2,1)S(1)} %add_convert_fusion.11), channel_id=1, source_target_pairs={{0,8},{4,12},{8,0},{12,4},{1,9},{5,13},{9,1},{13,5},{2,10},{6,14},... | collective-permute-start | bytes 638984 | tf_op jit(solution)/shard_map/ppermute | solution.py:26
  74.6 11.2 %collective-permute-start.13 = (bf16[64,1664]{1,0:T(8,128)(2,1)S(1)}, bf16[64,1664]{1,0:T(8,128)(2,1)S(1)}, u32[]{:S(2)}, u32[]{:S(2)}) collective-permute-start(bf16[64,1664]{1,0:T(8,128)(2,1)S(1)} %hidden_1.1), channel_id=1, source_target_pairs={{0,4},{4,0},{8,12},{12,8},{1,5},{5,1},{9,13},{13,9},{2,6},{6,2},{1... | collective-permute-start | bytes 638984 | tf_op jit(solution)/shard_map/ppermute | solution.py:26
  76.7 18.5 %collective-permute-start.14 = (bf16[1,2,64,1664]{3,2,1,0:T(8,128)(2,1)S(1)}, bf16[1,2,64,1664]{3,2,1,0:T(8,128)(2,1)S(1)}, u32[]{:S(2)}, u32[]{:S(2)}) collective-permute-start(bf16[1,2,64,1664]{3,2,1,0:T(8,128)(2,1)S(1)} %add_convert_fusion), channel_id=1, source_target_pairs={{0,2},{1,3},{2,0},{3,1},{4,6},{5,7},{6,4},{7,5},{8,10},{9,11},{10,... | collective-permute-start | bytes 1277960 | tf_op jit(solution)/shard_map/ppermute | solution.py:26
  83.6 10.7 %collective-permute-start.11 = (bf16[64,1664]{1,0:T(8,128)(2,1)S(1)}, bf16[64,1664]{1,0:T(8,128)(2,1)S(1)}, u32[]{:S(2)}, u32[]{:S(2)}) collective-permute-start(bf16[64,1664]{1,0:T(8,128)(2,1)S(1)} %hidden_2.1), channel_id=1, source_target_pairs={{0,4},{4,0},{8,12},{12,8},{1,5},{5,1},{9,13},{13,9},{2,6},{6,2},{1... | collective-permute-start | bytes 638984 | tf_op jit(solution)/shard_map/ppermute | solution.py:26
  86.0 9.2 %collective-permute-start.17 = (bf16[64,1664]{1,0:T(8,128)(2,1)S(1)}, bf16[64,1664]{1,0:T(8,128)(2,1)S(1)}, u32[]{:S(2)}, u32[]{:S(2)}) collective-permute-start(bf16[64,1664]{1,0:T(8,128)(2,1)S(1)} %add_convert_fusion.9.refs_0_), channel_id=1, source_target_pairs={{0,2},{1,3},{2,0},{3,1},{4,6},{5,7},{6,4},{7,5},{8,10},{9,11},{10,... | collective-permute-start | bytes 638984 | tf_op jit(solution)/shard_map/ppermute | solution.py:26
  86.5 14.7 %collective-permute-start.18 = (bf16[64,1664]{1,0:T(8,128)(2,1)S(1)}, bf16[64,1664]{1,0:T(8,128)(2,1)S(1)}, u32[]{:S(2)}, u32[]{:S(2)}) collective-permute-start(bf16[64,1664]{1,0:T(8,128)(2,1)S(1)} %add_convert_fusion.9.refs_0_), channel_id=1, source_target_pairs={{0,1},{1,0},{2,3},{3,2},{4,5},{5,4},{6,7},{7,6},{8,9},{9,8},{10,11... | collective-permute-start | bytes 638984 | tf_op jit(solution)/shard_map/ppermute | solution.py:26
  86.5 13.3 %collective-permute-start.20 = (bf16[64,1664]{1,0:T(8,128)(2,1)S(1)}, bf16[64,1664]{1,0:T(8,128)(2,1)S(1)}, u32[]{:S(2)}, u32[]{:S(2)}) collective-permute-start(bf16[64,1664]{1,0:T(8,128)(2,1)S(1)} %add_convert_fusion.10), channel_id=1, source_target_pairs={{0,8},{4,12},{8,0},{12,4},{1,9},{5,13},{9,1},{13,5},{2,10},{6,14},... | collective-permute-start | bytes 638984 | tf_op jit(solution)/shard_map/ppermute | solution.py:26
  95.1 6.6 %collective-permute-start.19 = (bf16[64,1664]{1,0:T(8,128)(2,1)S(1)}, bf16[64,1664]{1,0:T(8,128)(2,1)S(1)}, u32[]{:S(2)}, u32[]{:S(2)}) collective-permute-start(bf16[64,1664]{1,0:T(8,128)(2,1)S(1)} %collective-permute-done.17.refs_1_), channel_id=1, source_target_pairs={{0,1},{1,0},{2,3},{3,2},{4,5},{5,4},{6,7},{7,6},{8,9},{9,8},{10,11... | collective-permute-start | bytes 638984 | tf_op jit(solution)/shard_map/ppermute | solution.py:26
  95.9 10.6 %collective-permute-start.16 = (bf16[64,1664]{1,0:T(8,128)(2,1)S(1)}, bf16[64,1664]{1,0:T(8,128)(2,1)S(1)}, u32[]{:S(2)}, u32[]{:S(2)}) collective-permute-start(bf16[64,1664]{1,0:T(8,128)(2,1)S(1)} %hidden_3.1), channel_id=1, source_target_pairs={{0,4},{4,0},{8,12},{12,8},{1,5},{5,1},{9,13},{13,9},{2,6},{6,2},{1... | collective-permute-start | bytes 638984 | tf_op jit(solution)/shard_map/ppermute | solution.py:26
  99.9 20.4 %collective-permute-start.26 = (bf16[64,1664]{1,0:T(8,128)(2,1)S(1)}, bf16[64,1664]{1,0:T(8,128)(2,1)S(1)}, u32[]{:S(2)}, u32[]{:S(2)}) collective-permute-start(bf16[64,1664]{1,0:T(8,128)(2,1)S(1)} %add_convert_fusion.7.refs_0_), channel_id=1, source_target_pairs={{0,1},{1,0},{2,3},{3,2},{4,5},{5,4},{6,7},{7,6},{8,9},{9,8},{10,11... | collective-permute-start | bytes 638984 | tf_op jit(solution)/shard_map/ppermute | solution.py:26
  100.0 19.0 %collective-permute-start.25 = (bf16[64,1664]{1,0:T(8,128)(2,1)S(1)}, bf16[64,1664]{1,0:T(8,128)(2,1)S(1)}, u32[]{:S(2)}, u32[]{:S(2)}) collective-permute-start(bf16[64,1664]{1,0:T(8,128)(2,1)S(1)} %add_convert_fusion.7.refs_0_), channel_id=1, source_target_pairs={{0,2},{1,3},{2,0},{3,1},{4,6},{5,7},{6,4},{7,5},{8,10},{9,11},{10,... | collective-permute-start | bytes 638984 | tf_op jit(solution)/shard_map/ppermute | solution.py:26
  101.2 17.7 %collective-permute-start.15 = (bf16[64,1664]{1,0:T(8,128)(2,1)S(1)}, bf16[64,1664]{1,0:T(8,128)(2,1)S(1)}, u32[]{:S(2)}, u32[]{:S(2)}) collective-permute-start(bf16[64,1664]{1,0:T(8,128)(2,1)S(1)} %add_convert_fusion.8), channel_id=1, source_target_pairs={{0,8},{4,12},{8,0},{12,4},{1,9},{5,13},{9,1},{13,5},{2,10},{6,14},... | collective-permute-start | bytes 638984 | tf_op jit(solution)/shard_map/ppermute | solution.py:26
  106.6 18.6 %collective-permute-start.24 = (bf16[64,1664]{1,0:T(8,128)(2,1)S(1)}, bf16[64,1664]{1,0:T(8,128)(2,1)S(1)}, u32[]{:S(2)}, u32[]{:S(2)}) collective-permute-start(bf16[64,1664]{1,0:T(8,128)(2,1)S(1)} %add_convert_fusion.6), channel_id=1, source_target_pairs={{0,8},{4,12},{8,0},{12,4},{1,9},{5,13},{9,1},{13,5},{2,10},{6,14},... | collective-permute-start | bytes 638984 | tf_op jit(solution)/shard_map/ppermute | solution.py:26
  118.9 1.5 collective-permute-start.27
  119.0 8.0 %collective-permute-start.21 = (bf16[64,1664]{1,0:T(8,128)(2,1)S(1)}, bf16[64,1664]{1,0:T(8,128)(2,1)S(1)}, u32[]{:S(2)}, u32[]{:S(2)}) collective-permute-start(bf16[64,1664]{1,0:T(8,128)(2,1)S(1)} %add_convert_fusion.5.refs_0_), channel_id=1, source_target_pairs={{0,2},{1,3},{2,0},{3,1},{4,6},{5,7},{6,4},{7,5},{8,10},{9,11},{10,... | collective-permute-start | bytes 638984 | tf_op jit(solution)/shard_map/ppermute | solution.py:26
  125.3 7.4 %collective-permute-start.28 = (bf16[64,1664]{1,0:T(8,128)(2,1)S(1)}, bf16[64,1664]{1,0:T(8,128)(2,1)S(1)}, u32[]{:S(2)}, u32[]{:S(2)}) collective-permute-start(bf16[64,1664]{1,0:T(8,128)(2,1)S(1)} %add_convert_fusion.4.refs_4_), channel_id=1, source_target_pairs={{0,2},{1,3},{2,0},{3,1},{4,6},{5,7},{6,4},{7,5},{8,10},{9,11},{10,... | collective-permute-start | bytes 638984 | tf_op jit(solution)/shard_map/ppermute | solution.py:26
  126.5 6.1 %collective-permute-start.22 = (bf16[64,1664]{1,0:T(8,128)(2,1)S(1)}, bf16[64,1664]{1,0:T(8,128)(2,1)S(1)}, u32[]{:S(2)}, u32[]{:S(2)}) collective-permute-start(bf16[64,1664]{1,0:T(8,128)(2,1)S(1)} %add_convert_fusion.5.refs_0_), channel_id=1, source_target_pairs={{0,1},{1,0},{2,3},{3,2},{4,5},{5,4},{6,7},{7,6},{8,9},{9,8},{10,11... | collective-permute-start | bytes 638984 | tf_op jit(solution)/shard_map/ppermute | solution.py:26
  126.5 6.1 %collective-permute-start.29 = (bf16[64,1664]{1,0:T(8,128)(2,1)S(1)}, bf16[64,1664]{1,0:T(8,128)(2,1)S(1)}, u32[]{:S(2)}, u32[]{:S(2)}) collective-permute-start(bf16[64,1664]{1,0:T(8,128)(2,1)S(1)} %add_convert_fusion.4.refs_4_), channel_id=1, source_target_pairs={{0,1},{1,0},{2,3},{3,2},{4,5},{5,4},{6,7},{7,6},{8,9},{9,8},{10,11... | collective-permute-start | bytes 638984 | tf_op jit(solution)/shard_map/ppermute | solution.py:26
  127.0 5.6 %collective-permute-start.23 = (bf16[64,1664]{1,0:T(8,128)(2,1)S(1)}, bf16[64,1664]{1,0:T(8,128)(2,1)S(1)}, u32[]{:S(2)}, u32[]{:S(2)}) collective-permute-start(bf16[64,1664]{1,0:T(8,128)(2,1)S(1)} %collective-permute-done.21.refs_1_), channel_id=1, source_target_pairs={{0,1},{1,0},{2,3},{3,2},{4,5},{5,4},{6,7},{7,6},{8,9},{9,8},{10,11... | collective-permute-start | bytes 638984 | tf_op jit(solution)/shard_map/ppermute | solution.py:26
  132.6 1.5 collective-permute-start.30
  138.1 19.0 %collective-permute-start.32 = (bf16[64,1024]{1,0:T(8,128)(2,1)S(1)}, bf16[64,1024]{1,0:T(8,128)(2,1)S(1)}, u32[]{:S(2)}, u32[]{:S(2)}) collective-permute-start(bf16[64,1024]{1,0:T(8,128)(2,1)S(1)} %get-tuple-element.231), channel_id=1, source_target_pairs={{0,12},{4,0},{8,4},{12,8},{1,13},{5,1},{9,5},{13,9},{2,14},{6,2},{... | collective-permute-start | bytes 393224 | tf_op jit(solution)/shard_map/ppermute | solution.py:31
  139.2 18.0 %collective-permute-start.31 = (bf16[64,1024]{1,0:T(8,128)(2,1)S(1)}, bf16[64,1024]{1,0:T(8,128)(2,1)S(1)}, u32[]{:S(2)}, u32[]{:S(2)}) collective-permute-start(bf16[64,1024]{1,0:T(8,128)(2,1)S(1)} %get-tuple-element.230), channel_id=1, source_target_pairs={{0,8},{4,12},{8,0},{12,4},{1,9},{5,13},{9,1},{13,5},{2,10},{6,14},... | collective-permute-start | bytes 393224 | tf_op jit(solution)/shard_map/ppermute | solution.py:31
  139.2 18.0 %collective-permute-start.33 = (bf16[64,1024]{1,0:T(8,128)(2,1)S(1)}, bf16[64,1024]{1,0:T(8,128)(2,1)S(1)}, u32[]{:S(2)}, u32[]{:S(2)}) collective-permute-start(bf16[64,1024]{1,0:T(8,128)(2,1)S(1)} %get-tuple-element.232), channel_id=1, source_target_pairs={{0,4},{4,8},{8,12},{12,0},{1,5},{5,9},{9,13},{13,1},{2,6},{6,10},{... | collective-permute-start | bytes 393224 | tf_op jit(solution)/shard_map/ppermute | solution.py:31
  144.3 15.7 %collective-permute-start.34 = (bf16[64,1024]{1,0:T(8,128)(2,1)S(1)}, bf16[64,1024]{1,0:T(8,128)(2,1)S(1)}, u32[]{:S(2)}, u32[]{:S(2)}) collective-permute-start(bf16[64,1024]{1,0:T(8,128)(2,1)S(1)} %get-tuple-element.247), channel_id=1, source_target_pairs={{0,8},{4,12},{8,0},{12,4},{1,9},{5,13},{9,1},{13,5},{2,10},{6,14},... | collective-permute-start | bytes 393224 | tf_op jit(solution)/shard_map/ppermute | solution.py:31
  147.3 12.7 %collective-permute-start.36 = (bf16[64,1024]{1,0:T(8,128)(2,1)S(1)}, bf16[64,1024]{1,0:T(8,128)(2,1)S(1)}, u32[]{:S(2)}, u32[]{:S(2)}) collective-permute-start(bf16[64,1024]{1,0:T(8,128)(2,1)S(1)} %get-tuple-element.248), channel_id=1, source_target_pairs={{0,4},{4,8},{8,12},{12,0},{1,5},{5,9},{9,13},{13,1},{2,6},{6,10},{... | collective-permute-start | bytes 393224 | tf_op jit(solution)/shard_map/ppermute | solution.py:31
  157.2 5.0 %collective-permute-start.35 = (bf16[64,1024]{1,0:T(8,128)(2,1)S(1)}, bf16[64,1024]{1,0:T(8,128)(2,1)S(1)}, u32[]{:S(2)}, u32[]{:S(2)}) collective-permute-start(bf16[64,1024]{1,0:T(8,128)(2,1)S(1)} %get-tuple-element.241), channel_id=1, source_target_pairs={{0,12},{4,0},{8,4},{12,8},{1,13},{5,1},{9,5},{13,9},{2,14},{6,2},{... | collective-permute-start | bytes 393224 | tf_op jit(solution)/shard_map/ppermute | solution.py:31

commit v4 on v3

--- a/solution.py
+++ b/solution.py
@@ -448,30 +448,29 @@
         pass_terms(1)
         finish_terms(0)
         start_terms(3)
-        land_turn(0)
         land_terms(1)
         land_terms(2)
         pass_terms(2)
+        finish_terms(1)
+        land_turn(0)
         turn(0, 0)
-        finish_terms(1)
         land_terms(3)
         pass_terms(3)
-        fold(rest // 2)
+        fold(rest)
+        land_turn(1)
+        turn(1, 0)
         land_terms(2)
         finish_terms(2)
-        land_turn(1)
-        turn(1, 0)
         land_turn(0)
         turn(0, 1)
-        fold(rest - rest // 2)
-        land_turn(2)
         land_terms(3)
         finish_terms(3)
+        land_turn(2)
         turn(2, 0)
+        land_parts(0)
+        sums = product(0, 1, [], 0, features, jnp.float32, 1)
         land_turn(1)
         turn(1, 1)
-        land_parts(0)
-        sums = product(0, 1, [], 0, features, jnp.float32, 1)
         land_turn(3)
         turn(3, 0)
         land_turn(2)

time: 164 us -> 157 us (0.957)
  waiting for transfers between devices: 39.4 us -> 35.1 us
  Pallas kernels: 73.5 us -> 71.4 us
    ppermute x9, waiting for transfers between devices: 14.4 us -> 12 us  [shift(): lax.ppermute(shard, axis, [(i, (i + step) % size) for i in range(size)])]
    ppermute x28, waiting for transfers between devices: 25 us -> 23.2 us  [swap(): lax.ppermute(shard, axis, [(i, i ^ 1 << bit) for i in range(lax.axis_size...]
    pallas_call x3 -> x2, Pallas kernels: 20.1 us -> 19 us  [folded(): pl.pallas_call(functools.partial(fold_kernel, chunks, blocks, first), gri...]
    unnamed x28 -> x32, local copies, waits for them, and re-layouts: 9.08 us -> 9.07 us
  transfers between devices with their start and end apart: 37 -> 37, of which waited for: 12 -> 11; matrix products, arithmetic and copies ran while one was open for 2% -> 2% of each run, Pallas kernels for 38% -> 39%
where the time goes in v4:
time: 157 us; the launch traced here: 156 us
  Pallas kernels  71.4 us (45%)
  starting transfers between devices  36.7 us (23%)
  waiting for transfers between devices  35.1 us (22%)
  local copies, waits for them, and re-layouts  9.1 us (6%)
  other arithmetic  3.44 us (2%)
    pallas_call x4, Pallas kernels, gate_up(): pl.pallas_call(functools.partial(gate_up_kernel, len(token_parts), peers,...  29.8 us
    ppermute x28, waiting for transfers between devices, swap(): lax.ppermute(shard, axis, [(i, i ^ 1 << bit) for i in range(lax.axis_size...  23.2 us
    ppermute x28, starting transfers between devices, swap(): lax.ppermute(shard, axis, [(i, i ^ 1 << bit) for i in range(lax.axis_size...  22.6 us
    pallas_call x2, Pallas kernels, folded(): pl.pallas_call(functools.partial(fold_kernel, chunks, blocks, first), gri...  19 us
    pallas_call x4, Pallas kernels, down(): pl.pallas_call(functools.partial(down_kernel, chunks, pieces, peers, len(...  17.6 us
    ppermute x9, starting transfers between devices, shift(): lax.ppermute(shard, axis, [(i, (i + step) % size) for i in range(size)])  14.1 us
    ppermute x9, waiting for transfers between devices, shift(): lax.ppermute(shard, axis, [(i, (i + step) % size) for i in range(size)])  12 us
    unnamed x32, local copies, waits for them, and re-layouts  9.07 us
  transfers between devices with their start and end apart: 37, of which 11 were waited for; matrix products, arithmetic and copies ran while one was open for 2% of the time, Pallas kernels for 39%

profile of v4, /device:TPU:0, one launch (start us, length us, event | category | flops | bytes accessed | tf_op | source)
XLA Modules:
  0.0 156.3 jit_solution(15880769661558476983)
XLA Ops:
  0.0 3.1 %collective-permute-start = (bf16[64,2048]{1,0:T(8,128)(2,1)}, bf16[64,2048]{1,0:T(8,128)(2,1)S(1)}, u32[]{:S(2)}, u32[]{:S(2)}) collective-permute-start(bf16[64,2048]{1,0:T(8,128)(2,1)} %refs_0_.5), channel_id=1, source_target_pairs={{0,4},{4,8},{8,12},{12,0},{1,5},{5,9},{9,13},{13,1},{2,6},{6,10},{... | collective-permute-start | bytes 786440 | tf_op jit(solution)/shard_map/ppermute | solution.py:31
  3.1 2.6 %collective-permute-start.1 = (bf16[64,2048]{1,0:T(8,128)(2,1)}, bf16[64,2048]{1,0:T(8,128)(2,1)S(1)}, u32[]{:S(2)}, u32[]{:S(2)}) collective-permute-start(bf16[64,2048]{1,0:T(8,128)(2,1)} %refs_0_.5), channel_id=1, source_target_pairs={{0,8},{4,12},{8,0},{12,4},{1,9},{5,13},{9,1},{13,5},{2,10},{6,14},... | collective-permute-start | bytes 786440 | tf_op jit(solution)/shard_map/ppermute | solution.py:31
  5.7 1.3 collective-permute-start.2
  7.0 0.9 copy-done.13
  8.0 11.4 %fold_down_0.1.refs_4_.refs_8_.refs_10_ = bf16[4,1024,2048]{2,1,0:T(8,128)(2,1)S(1)} custom-call(bf16[6656,2048]{1,0:T(8,128)(2,1)} %refs_3_.2, bf16[6656,2048]{1,0:T(8,128)(2,1)} %refs_3_.2, bf16[6656,2048]{1,0:T(8,128)(2,1)} %refs_3_.2, bf16[6656,2048]{1,0:T(8,128)(2,1)} %refs_3_.2, bf16[52,2048]{1,0:T(8,128)(2,1)S(1)} %copy-done.13), custom_call_target="tpu_custom_call" | custom-call | bytes 33554432 | tf_op jit(solution)/shard_map/fold_down_0/pallas_call | solution.py:95
  19.4 5.8 %copy-done = bf16[4,1024,2048]{2,1,0:T(8,128)(2,1)} copy-done((bf16[4,1024,2048]{2,1,0:T(8,128)(2,1)}, bf16[4,1024,2048]{2,1,0:T(8,128)(2,1)S(1)}, u32[]{:S(2)}) %copy-start) | copy-done | bytes 16777240
  25.2 7.2 %gate_up_0.1 = (bf16[2,2,64,1664]{3,2,1,0:T(8,128)(2,1)S(1)}, bf16[2,2,64,1664]{3,2,1,0:T(8,128)(2,1)S(1)}) custom-call(bf16[64,2048]{1,0:T(8,128)(2,1)S(1)} %copy-done.1, bf16[64,2048]{1,0:T(8,128)(2,1)S(1)} %collective-permute-done.refs_1_, bf16[64,2048]{1,0:T(8,128)(2,1)S(1)} %collective-permute-done.1.refs_2_, ...), custom_call_target="tpu_custom_call" | custom-call | flops 3489660928 | bytes 13631488 | tf_op jit(solution)/shard_map/gate_up_0/pallas_call | solution.py:196
  32.4 0.1 collective-permute-start.3
  32.5 7.4 %gate_up_1.1 = (bf16[2,2,64,1664]{3,2,1,0:T(8,128)(2,1)S(1)}, bf16[2,2,64,1664]{3,2,1,0:T(8,128)(2,1)S(1)}) custom-call(bf16[64,2048]{1,0:T(8,128)(2,1)S(1)} %copy-done.1, bf16[64,2048]{1,0:T(8,128)(2,1)S(1)} %collective-permute-done.refs_1_, bf16[64,2048]{1,0:T(8,128)(2,1)S(1)} %collective-permute-done.1.refs_2_, ...), custom_call_target="tpu_custom_call" | custom-call | flops 3489660928 | bytes 13631488 | tf_op jit(solution)/shard_map/gate_up_1/pallas_call | solution.py:196
  39.9 0.3 collective-permute-start.6
  40.2 1.0 add_convert_fusion.3
  41.2 1.5 collective-permute-start.8
  42.7 8.0 %gate_up_2.1 = (bf16[2,2,64,1664]{3,2,1,0:T(8,128)(2,1)S(1)}, bf16[2,2,64,1664]{3,2,1,0:T(8,128)(2,1)}) custom-call(bf16[64,2048]{1,0:T(8,128)(2,1)S(1)} %copy-done.1, bf16[64,2048]{1,0:T(8,128)(2,1)S(1)} %collective-permute-done.refs_1_, bf16[64,2048]{1,0:T(8,128)(2,1)S(1)} %collective-permute-done.1.refs_2_, ...), custom_call_target="tpu_custom_call" | custom-call | flops 3489660928 | bytes 13631488 | tf_op jit(solution)/shard_map/gate_up_2/pallas_call | solution.py:196
  50.7 0.1 collective-permute-start.4
  50.8 0.9 add_convert_fusion.1
  51.7 1.4 collective-permute-start.7
  53.1 0.4 collective-permute-done.8.refs_2_
  53.5 1.2 copy-done.9
  54.6 1.2 copy-done.11
  55.8 1.8 %hidden_0.1 = bf16[64,1664]{1,0:T(8,128)(2,1)S(1)} custom-call(bf16[2,2,64,1664]{3,2,1,0:T(8,128)(2,1)S(1)} %copy-done.9, bf16[2,2,64,1664]{3,2,1,0:T(8,128)(2,1)S(1)} %copy-done.11, bf16[1,2,64,1664]{3,2,1,0:T(8,128)(2,1)} %collective-permute-done.8.refs_2_, f32[4,1,1664]{2,1,0:T(1,128)S(1)} %reshape.3.refs_3_, bf16[208,208]{1,0:T(8,128)(2,1)S(1)} %copy-done.12), custom_call_target="tpu_custom_call" | custom-call | flops 44302336 | bytes 1490944 | tf_op jit(solution)/shard_map/hidden_0/pallas_call | solution.py:236
  57.6 4.0 %collective-permute-start.11 = (bf16[64,1664]{1,0:T(8,128)(2,1)S(1)}, bf16[64,1664]{1,0:T(8,128)(2,1)S(1)}, u32[]{:S(2)}, u32[]{:S(2)}) collective-permute-start(bf16[64,1664]{1,0:T(8,128)(2,1)S(1)} %hidden_0.1), channel_id=1, source_target_pairs={{0,4},{4,0},{8,12},{12,8},{1,5},{5,1},{9,13},{13,9},{2,6},{6,2},{1... | collective-permute-start | bytes 638984 | tf_op jit(solution)/shard_map/ppermute | solution.py:26
  61.6 7.2 %gate_up_3.1 = (bf16[2,2,64,1664]{3,2,1,0:T(8,128)(2,1)S(1)}, bf16[2,2,64,1664]{3,2,1,0:T(8,128)(2,1)S(1)}) custom-call(bf16[64,2048]{1,0:T(8,128)(2,1)S(1)} %copy-done.1, bf16[64,2048]{1,0:T(8,128)(2,1)S(1)} %collective-permute-done.refs_1_, bf16[64,2048]{1,0:T(8,128)(2,1)S(1)} %collective-permute-done.1.refs_2_, ...), custom_call_target="tpu_custom_call" | custom-call | flops 3489660928 | bytes 13631488 | tf_op jit(solution)/shard_map/gate_up_3/pallas_call | solution.py:196
  68.8 0.1 collective-permute-start.10
  68.9 0.1 add_convert_fusion.2
  69.0 1.6 collective-permute-start.5
  70.5 1.8 %hidden_1.1 = bf16[64,1664]{1,0:T(8,128)(2,1)S(1)} custom-call(bf16[2,2,64,1664]{3,2,1,0:T(8,128)(2,1)S(1)} %copy-done.5, bf16[2,2,64,1664]{3,2,1,0:T(8,128)(2,1)S(1)} %copy-done.7, bf16[1,2,64,1664]{3,2,1,0:T(8,128)(2,1)} %collective-permute-done.7.refs_2_, f32[4,1,1664]{2,1,0:T(1,128)S(1)} %reshape.3.refs_3_, bf16[208,208]{1,0:T(8,128)(2,1)S(1)} %copy-done.12), custom_call_target="tpu_custom_call" | custom-call | flops 44302336 | bytes 1490944 | tf_op jit(solution)/shard_map/hidden_1/pallas_call | solution.py:236
  72.3 0.2 collective-permute-start.9
  72.6 1.6 %collective-permute-start.14 = (bf16[64,1664]{1,0:T(8,128)(2,1)S(1)}, bf16[64,1664]{1,0:T(8,128)(2,1)S(1)}, u32[]{:S(2)}, u32[]{:S(2)}) collective-permute-start(bf16[64,1664]{1,0:T(8,128)(2,1)S(1)} %add_convert_fusion.11), channel_id=1, source_target_pairs={{0,8},{4,12},{8,0},{12,4},{1,9},{5,13},{9,1},{13,5},{2,10},{6,14},... | collective-permute-start | bytes 638984 | tf_op jit(solution)/shard_map/ppermute | solution.py:26
  74.2 0.1 add_convert_fusion
  74.4 0.6 collective-permute-start.13
  75.0 7.6 %fold_down_8.1.refs_5_.refs_9_.refs_11_ = bf16[4,640,2048]{2,1,0:T(8,128)(2,1)S(1)} custom-call(bf16[6656,2048]{1,0:T(8,128)(2,1)} %refs_3_.2, bf16[6656,2048]{1,0:T(8,128)(2,1)} %refs_3_.2, bf16[6656,2048]{1,0:T(8,128)(2,1)} %refs_3_.2, bf16[6656,2048]{1,0:T(8,128)(2,1)} %refs_3_.2, bf16[52,2048]{1,0:T(8,128)(2,1)S(1)} %copy-done.14), custom_call_target="tpu_custom_call" | custom-call | bytes 20971520 | tf_op jit(solution)/shard_map/fold_down_8/pallas_call | solution.py:95
  82.6 1.7 %collective-permute-done.9 = bf16[64,1664]{1,0:T(8,128)(2,1)S(1)} collective-permute-done((bf16[64,1664]{1,0:T(8,128)(2,1)S(1)}, bf16[64,1664]{1,0:T(8,128)(2,1)S(1)}, u32[]{:S(2)}, u32[]{:S(2)}) %collective-permute-start.9) | collective-permute-done | bytes 213024 | tf_op jit(solution)/shard_map/ppermute | solution.py:26
  84.4 0.8 hidden_2.1
  85.2 0.6 collective-permute-start.18
  85.8 1.1 collective-permute-start.12
  87.0 2.4 %collective-permute-start.17 = (bf16[64,1664]{1,0:T(8,128)(2,1)S(1)}, bf16[64,1664]{1,0:T(8,128)(2,1)S(1)}, u32[]{:S(2)}, u32[]{:S(2)}) collective-permute-start(bf16[64,1664]{1,0:T(8,128)(2,1)S(1)} %add_convert_fusion.10), channel_id=1, source_target_pairs={{0,8},{4,12},{8,0},{12,4},{1,9},{5,13},{9,1},{13,5},{2,10},{6,14},... | collective-permute-start | bytes 638984 | tf_op jit(solution)/shard_map/ppermute | solution.py:26
  89.4 5.5 %collective-permute-done.18.refs_1_ = bf16[64,1664]{1,0:T(8,128)(2,1)S(1)} collective-permute-done((bf16[64,1664]{1,0:T(8,128)(2,1)S(1)}, bf16[64,1664]{1,0:T(8,128)(2,1)S(1)}, u32[]{:S(2)}, u32[]{:S(2)}) %collective-permute-start.18) | collective-permute-done | bytes 213024 | tf_op jit(solution)/shard_map/ppermute | solution.py:26
  94.9 0.8 hidden_3.1
  95.7 0.2 collective-permute-start.16
  96.0 1.6 %collective-permute-start.15 = (bf16[64,1664]{1,0:T(8,128)(2,1)S(1)}, bf16[64,1664]{1,0:T(8,128)(2,1)S(1)}, u32[]{:S(2)}, u32[]{:S(2)}) collective-permute-start(bf16[64,1664]{1,0:T(8,128)(2,1)S(1)} %add_convert_fusion.8), channel_id=1, source_target_pairs={{0,8},{4,12},{8,0},{12,4},{1,9},{5,13},{9,1},{13,5},{2,10},{6,14},... | collective-permute-start | bytes 638984 | tf_op jit(solution)/shard_map/ppermute | solution.py:26
  97.7 4.7 %down_0_0.1.refs_6_ = f32[256,2048]{1,0:T(8,128)S(1)} custom-call(bf16[64,1664]{1,0:T(8,128)(2,1)S(1)} %add_convert_fusion.9.refs_0_, bf16[64,1664]{1,0:T(8,128)(2,1)S(1)} %collective-permute-done.18.refs_1_, bf16[64,1664]{1,0:T(8,128)(2,1)S(1)} %collective-permute-done.19.refs_2_, bf16[64,1664]{1,0:T(8,128)(2,1)S(1)} %collective-permute-done.20.refs_3_, ...), custom_call_target="tpu_custom_call" | custom-call | flops 1744830464 | bytes 6815744 | tf_op jit(solution)/shard_map/down_0_0/pallas_call | solution.py:297
  102.5 1.6 collective-permute-start.25
  104.1 3.9 %collective-permute-done.16 = bf16[64,1664]{1,0:T(8,128)(2,1)S(1)} collective-permute-done((bf16[64,1664]{1,0:T(8,128)(2,1)S(1)}, bf16[64,1664]{1,0:T(8,128)(2,1)S(1)}, u32[]{:S(2)}, u32[]{:S(2)}) %collective-permute-start.16) | collective-permute-done | bytes 213024 | tf_op jit(solution)/shard_map/ppermute | solution.py:26
  108.1 0.1 collective-permute-start.24
  108.2 1.6 %collective-permute-done.25.refs_1_ = bf16[64,1664]{1,0:T(8,128)(2,1)S(1)} collective-permute-done((bf16[64,1664]{1,0:T(8,128)(2,1)S(1)}, bf16[64,1664]{1,0:T(8,128)(2,1)S(1)}, u32[]{:S(2)}, u32[]{:S(2)}) %collective-permute-start.25) | collective-permute-done | bytes 213024 | tf_op jit(solution)/shard_map/ppermute | solution.py:26
  109.9 1.6 collective-permute-start.21
  111.4 4.8 %down_1_0.1.refs_12_ = f32[256,2048]{1,0:T(8,128)S(1)} custom-call(bf16[64,1664]{1,0:T(8,128)(2,1)S(1)} %add_convert_fusion.7.refs_0_, bf16[64,1664]{1,0:T(8,128)(2,1)S(1)} %collective-permute-done.25.refs_1_, bf16[64,1664]{1,0:T(8,128)(2,1)S(1)} %collective-permute-done.26.refs_2_, bf16[64,1664]{1,0:T(8,128)(2,1)S(1)} %collective-permute-done.27.refs_3_, ...), custom_call_target="tpu_custom_call" | custom-call | flops 1744830464 | bytes 6815744 | tf_op jit(solution)/shard_map/down_1_0/pallas_call | solution.py:297
  116.2 3.3 %collective-permute-done.24 = bf16[64,1664]{1,0:T(8,128)(2,1)S(1)} collective-permute-done((bf16[64,1664]{1,0:T(8,128)(2,1)S(1)}, bf16[64,1664]{1,0:T(8,128)(2,1)S(1)}, u32[]{:S(2)}, u32[]{:S(2)}) %collective-permute-start.24) | collective-permute-done | bytes 213024 | tf_op jit(solution)/shard_map/ppermute | solution.py:26
  119.5 1.6 collective-permute-start.28
  121.1 0.5 collective-permute-start.29
  121.6 5.2 %collective-permute-done.28.refs_5_ = bf16[64,1664]{1,0:T(8,128)(2,1)S(1)} collective-permute-done((bf16[64,1664]{1,0:T(8,128)(2,1)S(1)}, bf16[64,1664]{1,0:T(8,128)(2,1)S(1)}, u32[]{:S(2)}, u32[]{:S(2)}) %collective-permute-start.28) | collective-permute-done | bytes 213024 | tf_op jit(solution)/shard_map/ppermute | solution.py:26
  126.8 1.4 collective-permute-done.30.refs_7_
  128.3 4.0 %down_2_0.1 = (bf16[64,1024]{1,0:T(8,128)(2,1)S(1)}, bf16[64,1024]{1,0:T(8,128)(2,1)S(1)}, bf16[64,1024]{1,0:T(8,128)(2,1)S(1)}, bf16[64,1024]{1,0:T(8,128)(2,1)S(1)}) custom-call(bf16[64,1664]{1,0:T(8,128)(2,1)S(1)} %add_convert_fusion.5.refs_0_, bf16[64,1664]{1,0:T(8,128)(2,1)S(1)} %collective-permute-done.21.refs_1_, ...), custom_call_target="tpu_custom_call" | custom-call | flops 1744830464 | bytes 6815744 | tf_op jit(solution)/shard_map/down_2_0/pallas_call | solution.py:297
  132.3 1.2 collective-permute-start.32
  133.5 0.9 collective-permute-start.33
  134.4 4.0 %down_2_1.1 = (bf16[64,1024]{1,0:T(8,128)(2,1)S(1)}, bf16[64,1024]{1,0:T(8,128)(2,1)S(1)}, bf16[64,1024]{1,0:T(8,128)(2,1)S(1)}, bf16[64,1024]{1,0:T(8,128)(2,1)S(1)}) custom-call(bf16[64,1664]{1,0:T(8,128)(2,1)S(1)} %add_convert_fusion.5.refs_0_, bf16[64,1664]{1,0:T(8,128)(2,1)S(1)} %collective-permute-done.21.refs_1_, ...), custom_call_target="tpu_custom_call" | custom-call | flops 1744830464 | bytes 6815744 | tf_op jit(solution)/shard_map/down_2_1/pallas_call | solution.py:297
  138.4 3.0 %collective-permute-start.34 = (bf16[64,1024]{1,0:T(8,128)(2,1)S(1)}, bf16[64,1024]{1,0:T(8,128)(2,1)S(1)}, u32[]{:S(2)}, u32[]{:S(2)}) collective-permute-start(bf16[64,1024]{1,0:T(8,128)(2,1)S(1)} %get-tuple-element.249), channel_id=1, source_target_pairs={{0,8},{4,12},{8,0},{12,4},{1,9},{5,13},{9,1},{13,5},{2,10},{6,14},... | collective-permute-start | bytes 393224 | tf_op jit(solution)/shard_map/ppermute | solution.py:31
  141.4 2.0 %collective-permute-start.35 = (bf16[64,1024]{1,0:T(8,128)(2,1)S(1)}, bf16[64,1024]{1,0:T(8,128)(2,1)S(1)}, u32[]{:S(2)}, u32[]{:S(2)}) collective-permute-start(bf16[64,1024]{1,0:T(8,128)(2,1)S(1)} %get-tuple-element.243), channel_id=1, source_target_pairs={{0,12},{4,0},{8,4},{12,8},{1,13},{5,1},{9,5},{13,9},{2,14},{6,2},{... | collective-permute-start | bytes 393224 | tf_op jit(solution)/shard_map/ppermute | solution.py:31
  143.4 5.2 %collective-permute-done.31 = bf16[64,1024]{1,0:T(8,128)(2,1)S(1)} collective-permute-done((bf16[64,1024]{1,0:T(8,128)(2,1)S(1)}, bf16[64,1024]{1,0:T(8,128)(2,1)S(1)}, u32[]{:S(2)}, u32[]{:S(2)}) %collective-permute-start.31) | collective-permute-done | bytes 131104 | tf_op jit(solution)/shard_map/ppermute | solution.py:31
  148.6 0.1 add_convert_fusion.13
  148.7 2.7 %collective-permute-done.34 = bf16[64,1024]{1,0:T(8,128)(2,1)S(1)} collective-permute-done((bf16[64,1024]{1,0:T(8,128)(2,1)S(1)}, bf16[64,1024]{1,0:T(8,128)(2,1)S(1)}, u32[]{:S(2)}, u32[]{:S(2)}) %collective-permute-start.34) | collective-permute-done | bytes 131104 | tf_op jit(solution)/shard_map/ppermute | solution.py:31
  151.4 4.1 %collective-permute-done.36 = bf16[64,1024]{1,0:T(8,128)(2,1)S(1)} collective-permute-done((bf16[64,1024]{1,0:T(8,128)(2,1)S(1)}, bf16[64,1024]{1,0:T(8,128)(2,1)S(1)}, u32[]{:S(2)}, u32[]{:S(2)}) %collective-permute-start.36) | collective-permute-done | bytes 131104 | tf_op jit(solution)/shard_map/ppermute | solution.py:31
  155.5 0.1 add_convert_fusion.12
  155.5 0.7 pad_maximum_fusion
  (73 shorter events, 0.8 us)
Async XLA Ops:
  0.0 25.2 %copy-start.1 = (bf16[64,2048]{1,0:T(8,128)(2,1)S(1)}, bf16[64,2048]{1,0:T(8,128)(2,1)}, u32[]{:S(2)}) copy-start(bf16[64,2048]{1,0:T(8,128)(2,1)} %refs_0_.5) | copy-start | bytes 786436
  0.0 25.2 %copy-start.2 = (bf16[16,6656]{1,0:T(8,128)(2,1)S(1)}, bf16[16,6656]{1,0:T(8,128)(2,1)}, u32[]{:S(2)}) copy-start(bf16[16,6656]{1,0:T(8,128)(2,1)} %refs_6_.7) | copy-start | bytes 638980
  0.0 25.2 %copy-start.3 = (bf16[16,6656]{1,0:T(8,128)(2,1)S(1)}, bf16[16,6656]{1,0:T(8,128)(2,1)}, u32[]{:S(2)}) copy-start(bf16[16,6656]{1,0:T(8,128)(2,1)} %refs_7_.7) | copy-start | bytes 638980
  0.0 25.2 %collective-permute-start = (bf16[64,2048]{1,0:T(8,128)(2,1)}, bf16[64,2048]{1,0:T(8,128)(2,1)S(1)}, u32[]{:S(2)}, u32[]{:S(2)}) collective-permute-start(bf16[64,2048]{1,0:T(8,128)(2,1)} %refs_0_.5), channel_id=1, source_target_pairs={{0,4},{4,8},{8,12},{12,0},{1,5},{5,9},{9,13},{13,1},{2,6},{6,10},{... | collective-permute-start | bytes 786440 | tf_op jit(solution)/shard_map/ppermute | solution.py:31
  3.1 22.1 %collective-permute-start.1 = (bf16[64,2048]{1,0:T(8,128)(2,1)}, bf16[64,2048]{1,0:T(8,128)(2,1)S(1)}, u32[]{:S(2)}, u32[]{:S(2)}) collective-permute-start(bf16[64,2048]{1,0:T(8,128)(2,1)} %refs_0_.5), channel_id=1, source_target_pairs={{0,8},{4,12},{8,0},{12,4},{1,9},{5,13},{9,1},{13,5},{2,10},{6,14},... | collective-permute-start | bytes 786440 | tf_op jit(solution)/shard_map/ppermute | solution.py:31
  5.7 19.5 %collective-permute-start.2 = (bf16[64,2048]{1,0:T(8,128)(2,1)}, bf16[64,2048]{1,0:T(8,128)(2,1)S(1)}, u32[]{:S(2)}, u32[]{:S(2)}) collective-permute-start(bf16[64,2048]{1,0:T(8,128)(2,1)} %refs_0_.5), channel_id=1, source_target_pairs={{0,12},{4,0},{8,4},{12,8},{1,13},{5,1},{9,5},{13,9},{2,14},{6,2},{... | collective-permute-start | bytes 786440 | tf_op jit(solution)/shard_map/ppermute | solution.py:31
  7.0 0.9 copy-start.13
  19.4 5.8 %copy-start = (bf16[4,1024,2048]{2,1,0:T(8,128)(2,1)}, bf16[4,1024,2048]{2,1,0:T(8,128)(2,1)S(1)}, u32[]{:S(2)}) copy-start(bf16[4,1024,2048]{2,1,0:T(8,128)(2,1)S(1)} %fold_down_0.1.refs_4_.refs_8_.refs_10_) | copy-start | bytes 50331652
  32.4 7.8 %copy-start.8 = (bf16[2,2,64,1664]{3,2,1,0:T(8,128)(2,1)}, bf16[2,2,64,1664]{3,2,1,0:T(8,128)(2,1)S(1)}, u32[]{:S(2)}) copy-start(bf16[2,2,64,1664]{3,2,1,0:T(8,128)(2,1)S(1)} %get-tuple-element.160.refs_0_) | copy-start | bytes 2555908
  32.4 7.8 %collective-permute-start.3 = (bf16[2,2,64,1664]{3,2,1,0:T(8,128)(2,1)S(1)}, bf16[2,2,64,1664]{3,2,1,0:T(8,128)(2,1)S(1)}, u32[]{:S(2)}, u32[]{:S(2)}) collective-permute-start(bf16[2,2,64,1664]{3,2,1,0:T(8,128)(2,1)S(1)} %get-tuple-element.139), channel_id=1, source_target_pairs={{0,1},{1,0},{2,3},{3,2},{4,5},{5,4},{6,7},{7,6},{8,9},{9,8},{10,11... | collective-permute-start | bytes 2555912 | tf_op jit(solution)/shard_map/ppermute | solution.py:26
  39.9 10.9 %copy-start.4 = (bf16[2,2,64,1664]{3,2,1,0:T(8,128)(2,1)}, bf16[2,2,64,1664]{3,2,1,0:T(8,128)(2,1)S(1)}, u32[]{:S(2)}) copy-start(bf16[2,2,64,1664]{3,2,1,0:T(8,128)(2,1)S(1)} %get-tuple-element.169.refs_0_) | copy-start | bytes 2555908
  39.9 2.8 %collective-permute-start.6 = (bf16[2,2,64,1664]{3,2,1,0:T(8,128)(2,1)S(1)}, bf16[2,2,64,1664]{3,2,1,0:T(8,128)(2,1)S(1)}, u32[]{:S(2)}, u32[]{:S(2)}) collective-permute-start(bf16[2,2,64,1664]{3,2,1,0:T(8,128)(2,1)S(1)} %get-tuple-element.156), channel_id=1, source_target_pairs={{0,1},{1,0},{2,3},{3,2},{4,5},{5,4},{6,7},{7,6},{8,9},{9,8},{10,11... | collective-permute-start | bytes 2555912 | tf_op jit(solution)/shard_map/ppermute | solution.py:26
  40.2 10.5 %copy-start.10 = (bf16[2,2,64,1664]{3,2,1,0:T(8,128)(2,1)}, bf16[2,2,64,1664]{3,2,1,0:T(8,128)(2,1)S(1)}, u32[]{:S(2)}) copy-start(bf16[2,2,64,1664]{3,2,1,0:T(8,128)(2,1)S(1)} %collective-permute-done.3.refs_1_) | copy-start | bytes 2555908
  41.2 11.9 %copy-start.15 = (s32[6656]{0:T(1024)S(1)}, s32[6656]{0:T(1024)}, u32[]{:S(2)}) copy-start(s32[6656]{0:T(1024)} %param.16) | copy-start | bytes 79876
  41.2 12.3 %copy-start.12 = (bf16[208,208]{1,0:T(8,128)(2,1)S(1)}, bf16[208,208]{1,0:T(8,128)(2,1)}, u32[]{:S(2)}) copy-start(bf16[208,208]{1,0:T(8,128)(2,1)} %constant.18.clone.refs_4_) | copy-start | bytes 259588
  41.2 12.3 %collective-permute-start.8 = (bf16[1,2,64,1664]{3,2,1,0:T(8,128)(2,1)}, bf16[1,2,64,1664]{3,2,1,0:T(8,128)(2,1)}, u32[]{:S(2)}, u32[]{:S(2)}) collective-permute-start(bf16[1,2,64,1664]{3,2,1,0:T(8,128)(2,1)} %add_convert_fusion.3), channel_id=1, source_target_pairs={{0,2},{1,3},{2,0},{3,1},{4,6},{5,7},{6,4},{7,5},{8,10},{9,11},{10,... | collective-permute-start | bytes 1277960 | tf_op jit(solution)/shard_map/ppermute | solution.py:26
  42.7 8.1 %copy-start.6 = (bf16[2,2,64,1664]{3,2,1,0:T(8,128)(2,1)}, bf16[2,2,64,1664]{3,2,1,0:T(8,128)(2,1)S(1)}, u32[]{:S(2)}) copy-start(bf16[2,2,64,1664]{3,2,1,0:T(8,128)(2,1)S(1)} %collective-permute-done.6.refs_1_) | copy-start | bytes 2555908
  50.7 18.1 %collective-permute-start.4 = (bf16[2,2,64,1664]{3,2,1,0:T(8,128)(2,1)}, bf16[2,2,64,1664]{3,2,1,0:T(8,128)(2,1)S(1)}, u32[]{:S(2)}, u32[]{:S(2)}) collective-permute-start(bf16[2,2,64,1664]{3,2,1,0:T(8,128)(2,1)} %get-tuple-element.153), channel_id=1, source_target_pairs={{0,1},{1,0},{2,3},{3,2},{4,5},{5,4},{6,7},{7,6},{8,9},{9,8},{10,11... | collective-permute-start | bytes 2555912 | tf_op jit(solution)/shard_map/ppermute | solution.py:26
  51.7 17.1 %collective-permute-start.7 = (bf16[1,2,64,1664]{3,2,1,0:T(8,128)(2,1)}, bf16[1,2,64,1664]{3,2,1,0:T(8,128)(2,1)}, u32[]{:S(2)}, u32[]{:S(2)}) collective-permute-start(bf16[1,2,64,1664]{3,2,1,0:T(8,128)(2,1)} %add_convert_fusion.1), channel_id=1, source_target_pairs={{0,2},{1,3},{2,0},{3,1},{4,6},{5,7},{6,4},{7,5},{8,10},{9,11},{10,... | collective-permute-start | bytes 1277960 | tf_op jit(solution)/shard_map/ppermute | solution.py:26
  53.5 1.2 copy-start.9
  54.6 1.2 copy-start.11
  57.6 13.0 %copy-start.5 = (bf16[2,2,64,1664]{3,2,1,0:T(8,128)(2,1)S(1)}, bf16[2,2,64,1664]{3,2,1,0:T(8,128)(2,1)}, u32[]{:S(2)}) copy-start(bf16[2,2,64,1664]{3,2,1,0:T(8,128)(2,1)} %copy-done.4) | copy-start | bytes 2555908
  57.6 12.9 %copy-start.7 = (bf16[2,2,64,1664]{3,2,1,0:T(8,128)(2,1)S(1)}, bf16[2,2,64,1664]{3,2,1,0:T(8,128)(2,1)}, u32[]{:S(2)}) copy-start(bf16[2,2,64,1664]{3,2,1,0:T(8,128)(2,1)} %copy-done.6) | copy-start | bytes 2555908
  57.6 17.4 %copy-start.14 = (bf16[52,2048]{1,0:T(8,128)(2,1)S(1)}, bf16[52,2048]{1,0:T(8,128)(2,1)}, u32[]{:S(2)}) copy-start(bf16[52,2048]{1,0:T(8,128)(2,1)} %refs_4_.15) | copy-start | bytes 638980
  57.6 14.9 %collective-permute-start.11 = (bf16[64,1664]{1,0:T(8,128)(2,1)S(1)}, bf16[64,1664]{1,0:T(8,128)(2,1)S(1)}, u32[]{:S(2)}, u32[]{:S(2)}) collective-permute-start(bf16[64,1664]{1,0:T(8,128)(2,1)S(1)} %hidden_0.1), channel_id=1, source_target_pairs={{0,4},{4,0},{8,12},{12,8},{1,5},{5,1},{9,13},{13,9},{2,6},{6,2},{1... | collective-permute-start | bytes 638984 | tf_op jit(solution)/shard_map/ppermute | solution.py:26
  68.8 5.5 %collective-permute-start.10 = (bf16[2,2,64,1664]{3,2,1,0:T(8,128)(2,1)S(1)}, bf16[2,2,64,1664]{3,2,1,0:T(8,128)(2,1)S(1)}, u32[]{:S(2)}, u32[]{:S(2)}) collective-permute-start(bf16[2,2,64,1664]{3,2,1,0:T(8,128)(2,1)S(1)} %get-tuple-element.172), channel_id=1, source_target_pairs={{0,1},{1,0},{2,3},{3,2},{4,5},{5,4},{6,7},{7,6},{8,9},{9,8},{10,11... | collective-permute-start | bytes 2555912 | tf_op jit(solution)/shard_map/ppermute | solution.py:26
  69.0 15.4 %collective-permute-start.5 = (bf16[1,2,64,1664]{3,2,1,0:T(8,128)(2,1)S(1)}, bf16[1,2,64,1664]{3,2,1,0:T(8,128)(2,1)S(1)}, u32[]{:S(2)}, u32[]{:S(2)}) collective-permute-start(bf16[1,2,64,1664]{3,2,1,0:T(8,128)(2,1)S(1)} %add_convert_fusion.2), channel_id=1, source_target_pairs={{0,2},{1,3},{2,0},{3,1},{4,6},{5,7},{6,4},{7,5},{8,10},{9,11},{10,... | collective-permute-start | bytes 1277960 | tf_op jit(solution)/shard_map/ppermute | solution.py:26
  72.3 12.0 %collective-permute-start.9 = (bf16[64,1664]{1,0:T(8,128)(2,1)S(1)}, bf16[64,1664]{1,0:T(8,128)(2,1)S(1)}, u32[]{:S(2)}, u32[]{:S(2)}) collective-permute-start(bf16[64,1664]{1,0:T(8,128)(2,1)S(1)} %hidden_1.1), channel_id=1, source_target_pairs={{0,4},{4,0},{8,12},{12,8},{1,5},{5,1},{9,13},{13,9},{2,6},{6,2},{1... | collective-permute-start | bytes 638984 | tf_op jit(solution)/shard_map/ppermute | solution.py:26
  72.6 12.6 %collective-permute-start.14 = (bf16[64,1664]{1,0:T(8,128)(2,1)S(1)}, bf16[64,1664]{1,0:T(8,128)(2,1)S(1)}, u32[]{:S(2)}, u32[]{:S(2)}) collective-permute-start(bf16[64,1664]{1,0:T(8,128)(2,1)S(1)} %add_convert_fusion.11), channel_id=1, source_target_pairs={{0,8},{4,12},{8,0},{12,4},{1,9},{5,13},{9,1},{13,5},{2,10},{6,14},... | collective-permute-start | bytes 638984 | tf_op jit(solution)/shard_map/ppermute | solution.py:26
  74.4 20.6 %collective-permute-start.13 = (bf16[1,2,64,1664]{3,2,1,0:T(8,128)(2,1)S(1)}, bf16[1,2,64,1664]{3,2,1,0:T(8,128)(2,1)S(1)}, u32[]{:S(2)}, u32[]{:S(2)}) collective-permute-start(bf16[1,2,64,1664]{3,2,1,0:T(8,128)(2,1)S(1)} %add_convert_fusion), channel_id=1, source_target_pairs={{0,2},{1,3},{2,0},{3,1},{4,6},{5,7},{6,4},{7,5},{8,10},{9,11},{10,... | collective-permute-start | bytes 1277960 | tf_op jit(solution)/shard_map/ppermute | solution.py:26
  85.2 9.7 %collective-permute-start.18 = (bf16[64,1664]{1,0:T(8,128)(2,1)S(1)}, bf16[64,1664]{1,0:T(8,128)(2,1)S(1)}, u32[]{:S(2)}, u32[]{:S(2)}) collective-permute-start(bf16[64,1664]{1,0:T(8,128)(2,1)S(1)} %add_convert_fusion.9.refs_0_), channel_id=1, source_target_pairs={{0,2},{1,3},{2,0},{3,1},{4,6},{5,7},{6,4},{7,5},{8,10},{9,11},{10,... | collective-permute-start | bytes 638984 | tf_op jit(solution)/shard_map/ppermute | solution.py:26
  85.8 10.1 %collective-permute-start.12 = (bf16[64,1664]{1,0:T(8,128)(2,1)S(1)}, bf16[64,1664]{1,0:T(8,128)(2,1)S(1)}, u32[]{:S(2)}, u32[]{:S(2)}) collective-permute-start(bf16[64,1664]{1,0:T(8,128)(2,1)S(1)} %hidden_2.1), channel_id=1, source_target_pairs={{0,4},{4,0},{8,12},{12,8},{1,5},{5,1},{9,13},{13,9},{2,6},{6,2},{1... | collective-permute-start | bytes 638984 | tf_op jit(solution)/shard_map/ppermute | solution.py:26
  87.0 15.4 %collective-permute-start.17 = (bf16[64,1664]{1,0:T(8,128)(2,1)S(1)}, bf16[64,1664]{1,0:T(8,128)(2,1)S(1)}, u32[]{:S(2)}, u32[]{:S(2)}) collective-permute-start(bf16[64,1664]{1,0:T(8,128)(2,1)S(1)} %add_convert_fusion.10), channel_id=1, source_target_pairs={{0,8},{4,12},{8,0},{12,4},{1,9},{5,13},{9,1},{13,5},{2,10},{6,14},... | collective-permute-start | bytes 638984 | tf_op jit(solution)/shard_map/ppermute | solution.py:26
  89.4 8.3 %collective-permute-start.19 = (bf16[64,1664]{1,0:T(8,128)(2,1)S(1)}, bf16[64,1664]{1,0:T(8,128)(2,1)S(1)}, u32[]{:S(2)}, u32[]{:S(2)}) collective-permute-start(bf16[64,1664]{1,0:T(8,128)(2,1)S(1)} %add_convert_fusion.9.refs_0_), channel_id=1, source_target_pairs={{0,1},{1,0},{2,3},{3,2},{4,5},{5,4},{6,7},{7,6},{8,9},{9,8},{10,11... | collective-permute-start | bytes 638984 | tf_op jit(solution)/shard_map/ppermute | solution.py:26
  94.9 2.8 %collective-permute-start.20 = (bf16[64,1664]{1,0:T(8,128)(2,1)S(1)}, bf16[64,1664]{1,0:T(8,128)(2,1)S(1)}, u32[]{:S(2)}, u32[]{:S(2)}) collective-permute-start(bf16[64,1664]{1,0:T(8,128)(2,1)S(1)} %collective-permute-done.18.refs_1_), channel_id=1, source_target_pairs={{0,1},{1,0},{2,3},{3,2},{4,5},{5,4},{6,7},{7,6},{8,9},{9,8},{10,11... | collective-permute-start | bytes 638984 | tf_op jit(solution)/shard_map/ppermute | solution.py:26
  95.7 12.3 %collective-permute-start.16 = (bf16[64,1664]{1,0:T(8,128)(2,1)S(1)}, bf16[64,1664]{1,0:T(8,128)(2,1)S(1)}, u32[]{:S(2)}, u32[]{:S(2)}) collective-permute-start(bf16[64,1664]{1,0:T(8,128)(2,1)S(1)} %hidden_3.1), channel_id=1, source_target_pairs={{0,4},{4,0},{8,12},{12,8},{1,5},{5,1},{9,13},{13,9},{2,6},{6,2},{1... | collective-permute-start | bytes 638984 | tf_op jit(solution)/shard_map/ppermute | solution.py:26
  96.0 12.1 %collective-permute-start.15 = (bf16[64,1664]{1,0:T(8,128)(2,1)S(1)}, bf16[64,1664]{1,0:T(8,128)(2,1)S(1)}, u32[]{:S(2)}, u32[]{:S(2)}) collective-permute-start(bf16[64,1664]{1,0:T(8,128)(2,1)S(1)} %add_convert_fusion.8), channel_id=1, source_target_pairs={{0,8},{4,12},{8,0},{12,4},{1,9},{5,13},{9,1},{13,5},{2,10},{6,14},... | collective-permute-start | bytes 638984 | tf_op jit(solution)/shard_map/ppermute | solution.py:26
  102.5 7.3 %collective-permute-start.25 = (bf16[64,1664]{1,0:T(8,128)(2,1)S(1)}, bf16[64,1664]{1,0:T(8,128)(2,1)S(1)}, u32[]{:S(2)}, u32[]{:S(2)}) collective-permute-start(bf16[64,1664]{1,0:T(8,128)(2,1)S(1)} %add_convert_fusion.7.refs_0_), channel_id=1, source_target_pairs={{0,2},{1,3},{2,0},{3,1},{4,6},{5,7},{6,4},{7,5},{8,10},{9,11},{10,... | collective-permute-start | bytes 638984 | tf_op jit(solution)/shard_map/ppermute | solution.py:26
  104.1 7.4 %collective-permute-start.26 = (bf16[64,1664]{1,0:T(8,128)(2,1)S(1)}, bf16[64,1664]{1,0:T(8,128)(2,1)S(1)}, u32[]{:S(2)}, u32[]{:S(2)}) collective-permute-start(bf16[64,1664]{1,0:T(8,128)(2,1)S(1)} %add_convert_fusion.7.refs_0_), channel_id=1, source_target_pairs={{0,1},{1,0},{2,3},{3,2},{4,5},{5,4},{6,7},{7,6},{8,9},{9,8},{10,11... | collective-permute-start | bytes 638984 | tf_op jit(solution)/shard_map/ppermute | solution.py:26
  108.1 11.4 %collective-permute-start.24 = (bf16[64,1664]{1,0:T(8,128)(2,1)S(1)}, bf16[64,1664]{1,0:T(8,128)(2,1)S(1)}, u32[]{:S(2)}, u32[]{:S(2)}) collective-permute-start(bf16[64,1664]{1,0:T(8,128)(2,1)S(1)} %add_convert_fusion.6), channel_id=1, source_target_pairs={{0,8},{4,12},{8,0},{12,4},{1,9},{5,13},{9,1},{13,5},{2,10},{6,14},... | collective-permute-start | bytes 638984 | tf_op jit(solution)/shard_map/ppermute | solution.py:26
  109.8 1.6 %collective-permute-start.27 = (bf16[64,1664]{1,0:T(8,128)(2,1)S(1)}, bf16[64,1664]{1,0:T(8,128)(2,1)S(1)}, u32[]{:S(2)}, u32[]{:S(2)}) collective-permute-start(bf16[64,1664]{1,0:T(8,128)(2,1)S(1)} %collective-permute-done.25.refs_1_), channel_id=1, source_target_pairs={{0,1},{1,0},{2,3},{3,2},{4,5},{5,4},{6,7},{7,6},{8,9},{9,8},{10,11... | collective-permute-start | bytes 638984 | tf_op jit(solution)/shard_map/ppermute | solution.py:26
  109.9 11.7 %collective-permute-start.21 = (bf16[64,1664]{1,0:T(8,128)(2,1)S(1)}, bf16[64,1664]{1,0:T(8,128)(2,1)S(1)}, u32[]{:S(2)}, u32[]{:S(2)}) collective-permute-start(bf16[64,1664]{1,0:T(8,128)(2,1)S(1)} %add_convert_fusion.5.refs_0_), channel_id=1, source_target_pairs={{0,2},{1,3},{2,0},{3,1},{4,6},{5,7},{6,4},{7,5},{8,10},{9,11},{10,... | collective-permute-start | bytes 638984 | tf_op jit(solution)/shard_map/ppermute | solution.py:26
  119.5 7.2 %collective-permute-start.28 = (bf16[64,1664]{1,0:T(8,128)(2,1)S(1)}, bf16[64,1664]{1,0:T(8,128)(2,1)S(1)}, u32[]{:S(2)}, u32[]{:S(2)}) collective-permute-start(bf16[64,1664]{1,0:T(8,128)(2,1)S(1)} %add_convert_fusion.4.refs_4_), channel_id=1, source_target_pairs={{0,2},{1,3},{2,0},{3,1},{4,6},{5,7},{6,4},{7,5},{8,10},{9,11},{10,... | collective-permute-start | bytes 638984 | tf_op jit(solution)/shard_map/ppermute | solution.py:26
  121.1 5.7 %collective-permute-start.22 = (bf16[64,1664]{1,0:T(8,128)(2,1)S(1)}, bf16[64,1664]{1,0:T(8,128)(2,1)S(1)}, u32[]{:S(2)}, u32[]{:S(2)}) collective-permute-start(bf16[64,1664]{1,0:T(8,128)(2,1)S(1)} %add_convert_fusion.5.refs_0_), channel_id=1, source_target_pairs={{0,1},{1,0},{2,3},{3,2},{4,5},{5,4},{6,7},{7,6},{8,9},{9,8},{10,11... | collective-permute-start | bytes 638984 | tf_op jit(solution)/shard_map/ppermute | solution.py:26
  121.1 5.7 %collective-permute-start.29 = (bf16[64,1664]{1,0:T(8,128)(2,1)S(1)}, bf16[64,1664]{1,0:T(8,128)(2,1)S(1)}, u32[]{:S(2)}, u32[]{:S(2)}) collective-permute-start(bf16[64,1664]{1,0:T(8,128)(2,1)S(1)} %add_convert_fusion.4.refs_4_), channel_id=1, source_target_pairs={{0,1},{1,0},{2,3},{3,2},{4,5},{5,4},{6,7},{7,6},{8,9},{9,8},{10,11... | collective-permute-start | bytes 638984 | tf_op jit(solution)/shard_map/ppermute | solution.py:26
  121.6 5.2 %collective-permute-start.23 = (bf16[64,1664]{1,0:T(8,128)(2,1)S(1)}, bf16[64,1664]{1,0:T(8,128)(2,1)S(1)}, u32[]{:S(2)}, u32[]{:S(2)}) collective-permute-start(bf16[64,1664]{1,0:T(8,128)(2,1)S(1)} %collective-permute-done.21.refs_1_), channel_id=1, source_target_pairs={{0,1},{1,0},{2,3},{3,2},{4,5},{5,4},{6,7},{7,6},{8,9},{9,8},{10,11... | collective-permute-start | bytes 638984 | tf_op jit(solution)/shard_map/ppermute | solution.py:26
  126.8 1.5 collective-permute-start.30
  132.3 16.3 %collective-permute-start.32 = (bf16[64,1024]{1,0:T(8,128)(2,1)S(1)}, bf16[64,1024]{1,0:T(8,128)(2,1)S(1)}, u32[]{:S(2)}, u32[]{:S(2)}) collective-permute-start(bf16[64,1024]{1,0:T(8,128)(2,1)S(1)} %get-tuple-element.233), channel_id=1, source_target_pairs={{0,12},{4,0},{8,4},{12,8},{1,13},{5,1},{9,5},{13,9},{2,14},{6,2},{... | collective-permute-start | bytes 393224 | tf_op jit(solution)/shard_map/ppermute | solution.py:31
  133.5 15.1 %collective-permute-start.31 = (bf16[64,1024]{1,0:T(8,128)(2,1)S(1)}, bf16[64,1024]{1,0:T(8,128)(2,1)S(1)}, u32[]{:S(2)}, u32[]{:S(2)}) collective-permute-start(bf16[64,1024]{1,0:T(8,128)(2,1)S(1)} %get-tuple-element.232), channel_id=1, source_target_pairs={{0,8},{4,12},{8,0},{12,4},{1,9},{5,13},{9,1},{13,5},{2,10},{6,14},... | collective-permute-start | bytes 393224 | tf_op jit(solution)/shard_map/ppermute | solution.py:31
  133.5 15.1 %collective-permute-start.33 = (bf16[64,1024]{1,0:T(8,128)(2,1)S(1)}, bf16[64,1024]{1,0:T(8,128)(2,1)S(1)}, u32[]{:S(2)}, u32[]{:S(2)}) collective-permute-start(bf16[64,1024]{1,0:T(8,128)(2,1)S(1)} %get-tuple-element.234), channel_id=1, source_target_pairs={{0,4},{4,8},{8,12},{12,0},{1,5},{5,9},{9,13},{13,1},{2,6},{6,10},{... | collective-permute-start | bytes 393224 | tf_op jit(solution)/shard_map/ppermute | solution.py:31
  138.4 13.0 %collective-permute-start.34 = (bf16[64,1024]{1,0:T(8,128)(2,1)S(1)}, bf16[64,1024]{1,0:T(8,128)(2,1)S(1)}, u32[]{:S(2)}, u32[]{:S(2)}) collective-permute-start(bf16[64,1024]{1,0:T(8,128)(2,1)S(1)} %get-tuple-element.249), channel_id=1, source_target_pairs={{0,8},{4,12},{8,0},{12,4},{1,9},{5,13},{9,1},{13,5},{2,10},{6,14},... | collective-permute-start | bytes 393224 | tf_op jit(solution)/shard_map/ppermute | solution.py:31
  141.4 10.0 %collective-permute-start.35 = (bf16[64,1024]{1,0:T(8,128)(2,1)S(1)}, bf16[64,1024]{1,0:T(8,128)(2,1)S(1)}, u32[]{:S(2)}, u32[]{:S(2)}) collective-permute-start(bf16[64,1024]{1,0:T(8,128)(2,1)S(1)} %get-tuple-element.243), channel_id=1, source_target_pairs={{0,12},{4,0},{8,4},{12,8},{1,13},{5,1},{9,5},{13,9},{2,14},{6,2},{... | collective-permute-start | bytes 393224 | tf_op jit(solution)/shard_map/ppermute | solution.py:31
  148.6 6.9 %collective-permute-start.36 = (bf16[64,1024]{1,0:T(8,128)(2,1)S(1)}, bf16[64,1024]{1,0:T(8,128)(2,1)S(1)}, u32[]{:S(2)}, u32[]{:S(2)}) collective-permute-start(bf16[64,1024]{1,0:T(8,128)(2,1)S(1)} %get-tuple-element.250), channel_id=1, source_target_pairs={{0,4},{4,8},{8,12},{12,0},{1,5},{5,9},{9,13},{13,1},{2,6},{6,10},{... | collective-permute-start | bytes 393224 | tf_op jit(solution)/shard_map/ppermute | solution.py:31
